TPU v7x, 128 devices: a whole 4x4x4 slice. The times are simulated.
128 devices in a mesh: lev: 4 (over z), box: 32 (over x, y, core).
Axes of the slice: x: 4, y: 4, z: 4, core: 2. Of those that a mesh axis runs over, the one named last changes fastest.
Arguments:
- box_states: float32 [512, 8, 32, 1024], P(('lev', 'box')), may hold values from -6 to 6
- cell_code: int32 [512, 32, 1024], P(('lev', 'box')), may hold values from 0 to 15
- diffusivity: float32 [8], replicated, may hold values from 0.02 to 0.1
- reaction: float32 [8, 8], replicated, may hold values from -2 to 2
- coarse_child: int32 [128], P('box'), may hold values from -1 to 59, as said below
- coarse_octant: int32 [128], P('box'), may hold values from 0 to 3, as said below
- fine_parent: int32 [512], P(('lev', 'box')), may hold values from -1 to 127, as said below
- fine_octant: int32 [512], P(('lev', 'box')), may hold values from 0 to 3, as said below
- fine_count: int32 [128], P(('lev', 'box')), may hold values from 0 to 4, as said below
Outputs:
- new_states: float32 [512, 8, 32, 1024], P(('lev', 'box'))
Inputs may be any that keep to these rules, and one draw needn't show every extreme that they name: `coarse_child`: -1 where the coarse box has no fine box; else ((r - 1) (5) + e + 2) * 4 + s: the fine box is slot s of the device with lev index r >= 1 whose box index is the parent device's box index plus e, |e| <= 2. Each coarse box has at most one fine box. `coarse_octant`: for a refined coarse box, the refined halves; equal to fine_octant of its fine box. `fine_parent`: the parent of each used fine slot, -1 for unused slots and on lev index 0; used slots are those below fine_count, and coarse_child points back to them. `fine_octant`: the halves covered by a used fine slot, 0 for unused slots. `fine_count`: 0 on lev index 0; at most 4, reached on some device in every draw.
All inputs are finite; a program needn't handle non-finite values.
Results may differ from a plain program's by a relative error of at most 0.0003.
Values sent between devices are 32-bit elements; how exact they have to be, the bound alone decides.
No kernel may reach another device: no remote copies, remote signals or barrier semaphores. Data moves between devices by JAX's collectives and lax.ppermute only.
A program may use at most 192 MiB of HBM per device.

v0:
```python
import functools

import jax
import jax.numpy as jnp
import numpy as np
from jax import lax
from jax.experimental import pallas as pl
from jax.experimental.pallas import tpu as pltpu
from jax.sharding import PartitionSpec as P

ADVECT = 0.4
COARSE_STEP = 0.5
FLOOR = 0.5
LEVELS = 15.0
SLOTS = 4
REACH = 2
OFFSETS = 2 * REACH + 1
F32 = jnp.float32
BF16 = jnp.bfloat16


def selection_tables():
    lane = np.arange(1024)
    y, z = lane // 32, lane % 32
    place = np.arange(256)
    a, b = place // 16, place % 16
    i = np.arange(16)
    sel_x = np.zeros((4, 1024, 256), np.float32)
    sel_yz = np.zeros((4, 1024, 128), np.float32)
    for octant in range(4):
        y_half, z_half = octant % 2, octant // 2
        sel_x[octant, (16 * y_half + a) * 32 + 16 * z_half + b, place] = 1
        for g in range(4):
            sel_yz[octant, (16 - y_half) * 32 + 16 * z_half + i, 32 * g + i] = 1
            sel_yz[octant, (16 * y_half + i) * 32 + 16 - z_half, 32 * g + 16 + i] = 1
    up_x = np.zeros((256, 1024), np.float32)
    up_x[(y // 2) * 16 + z // 2, lane] = 1
    twice = np.zeros((256, 128), np.float32)
    rows = np.arange(256)
    twice[rows, rows // 32 * 16 + rows % 32 // 2] = 1
    window_z = np.zeros((2, 1024, 128), np.float32)
    for z_half in range(2):
        for step in range(3):
            rows = np.arange(32)
            window_z[z_half, rows * 32 + 15 - z_half + step, step * 32 + rows] = 1
    center = np.zeros((4, 256, 128), np.float32)
    for octant in range(4):
        for g in range(4):
            center[octant, 32 + 16 * (octant // 2) + i, 32 * g + i] = 1
            center[octant, 160 + 16 * (octant % 2) + i, 32 * g + 16 + i] = 1
    layers = np.zeros((4, 128, 1024), np.float32)
    line = np.arange(32)
    for octant in range(4):
        y_face, y_next = (0, 1) if octant % 2 else (31, 30)
        z_face, z_next = (0, 1) if octant // 2 else (31, 30)
        layers[octant, line, y_face * 32 + line] = 1
        layers[octant, 32 + line, y_next * 32 + line] = 1
        layers[octant, 64 + line, line * 32 + z_face] = 1
        layers[octant, 96 + line, line * 32 + z_next] = 1
    up_layer = np.zeros((128, 128), np.float32)
    for g in range(4):
        up_layer[32 * g + line // 2, line] = 1
        up_layer[32 * g + 16 + line // 2, 64 + line] = 1
    return sel_x, sel_yz, up_x, twice, window_z, center, layers, up_layer


SEL_X, SEL_YZ, UP_X, TWICE, WINDOW_Z, CENTER, LAYERS, UP_LAYER = selection_tables()


def table(values):
    return jnp.asarray(values.astype(jnp.bfloat16))


def halves(a):
    high = a.astype(BF16)
    return high, (a - high.astype(F32)).astype(BF16)


def dot(a, b):
    return jnp.dot(a, b, preferred_element_type=F32)


def pick(a, w):
    high, low = halves(a)
    return dot(high, w) + dot(low, w)


def left_pick(w, a):
    high, low = halves(a)
    return dot(w, high) + dot(w, low)


def iota(shape, dim):
    return lax.broadcasted_iota(jnp.int32, shape, dim)


def pack_rows(rows):
    group = iota((32, 128), 1) // 32
    out = rows[0:32]
    for g in range(1, 4):
        out = jnp.where(group == g, rows[32 * g : 32 * g + 32], out)
    return out


def unpack_rows(packed):
    group = iota((32, 128), 1) // 32
    return jnp.concatenate([jnp.where(group == g, packed, 0.0) for g in range(4)], axis=0)


def species_column(values_ref, factor, width):
    row = iota((8, width), 0)
    out = jnp.zeros((8, width), F32)
    for s in range(8):
        out = jnp.where(row == s, values_ref[s] * factor, out)
    return out


def set_rates(rates, reaction_ref, step):
    column = iota((1, 256), 1)
    for s in range(8):
        line = jnp.zeros((1, 256), F32)
        for t in range(8):
            line = jnp.where(column // 32 == t, reaction_ref[s, t] * step, line)
        high, low = halves(jnp.where(iota((32, 256), 0) == iota((32, 256), 1) % 32, line, 0.0))
        rates[0, 32 * s : 32 * s + 32] = high
        rates[1, 32 * s : 32 * s + 32] = low


def load_cells(cells, amounts):
    for t in range(8):
        cells[:, t + 1, 8:40, :] = amounts[:, :, 128 * t : 128 * t + 128]


def prepare(f, f_low, f_high, coef, scale):
    lane = iota((32, 1024), 1)
    row = iota((32, 1024), 0)
    depth = lane % 32
    scaling = scale / jnp.maximum(f, FLOOR)
    x_low = scaling * jnp.minimum(f, jnp.where(row == 0, f_low, pltpu.roll(f, 1, 0)))
    x_high = scaling * jnp.minimum(f, jnp.where(row == 31, f_high, pltpu.roll(f, 31, 0)))
    y_low = scaling * jnp.where(lane < 32, 0.0, jnp.minimum(f, pltpu.roll(f, 32, 1)))
    y_high = scaling * jnp.where(lane >= 992, 0.0, jnp.minimum(f, pltpu.roll(f, 992, 1)))
    z_low = scaling * jnp.where(depth == 0, 0.0, jnp.minimum(f, pltpu.roll(f, 1, 1)))
    z_high = scaling * jnp.where(depth == 31, 0.0, jnp.minimum(f, pltpu.roll(f, 1023, 1)))
    everything = x_low + x_high + y_low + y_high + z_low + z_high
    kinds = [x_low, x_high, y_low, y_high, z_low, z_high, everything, 1.0 - ADVECT * x_high, ADVECT * x_low]
    for k, kind in enumerate(kinds):
        for t in range(8):
            coef[k, t] = kind[:, 128 * t : 128 * t + 128]


def advance(cells, coef, reacted, rates, spread, store):
    lane = iota((8, 128), 1)

    def react(n, to):
        block = jnp.concatenate([cells[:, 2 * n + 1 + h, 8:40, :].reshape(256, 128) for h in range(2)], axis=1)
        high, low = halves(block)
        out = dot(rates[0], high) + dot(rates[1], high) + dot(rates[0], low)
        for h in range(2):
            to[:, h] = out[:, 128 * h : 128 * h + 128].reshape(8, 32, 128)

    def add(t, term):
        for xt in range(4):
            kinds = [coef[k, t, 8 * xt : 8 * xt + 8, :] for k in range(9)]
            x_low, x_high, y_low, y_high, z_low, z_high, everything, own, upwind = kinds
            at = 8 + 8 * xt
            for s in range(8):
                c = cells[s, t + 1, at : at + 8, :]
                below = cells[s, t + 1, at - 1 : at + 7, :]
                above = cells[s, t + 1, at + 1 : at + 9, :]
                left = pltpu.roll(jnp.where(lane >= 96, cells[s, t, at : at + 8, :], c), 32, 1)
                right = pltpu.roll(jnp.where(lane < 32, cells[s, t + 2, at : at + 8, :], c), 96, 1)
                change = x_low * below + x_high * above + y_low * left + y_high * right
                change = change + z_low * pltpu.roll(c, 1, 1) + z_high * pltpu.roll(c, 127, 1)
                change = change - everything * c
                result = own * c + upwind * below + spread[s] * change
                store(s, t, xt, result + term[s, 8 * xt : 8 * xt + 8, :])

    now, later = reacted
    react(0, now)

    def pair(m, carry):
        react(2 * m + 1, later)
        for h in range(2):
            add(4 * m + h, now.at[:, h])
        react(jnp.minimum(2 * m + 2, 3), now)
        for h in range(2):
            add(4 * m + 2 + h, later.at[:, h])
        return carry

    lax.fori_loop(0, 2, pair, 0)


def clear_rim(cells):
    cells[:, 0] = jnp.zeros((8, 48, 128), F32)
    cells[:, 9] = jnp.zeros((8, 48, 128), F32)
    cells[:, :, 0:8, :] = jnp.zeros((8, 10, 8, 128), F32)
    cells[:, :, 40:48, :] = jnp.zeros((8, 10, 8, 128), F32)


def message_kernel(
    octants, codes, spread_ref, reaction_smem, reaction_ref, boxes, words, sel_x_all, window_z_all, center_all, message,
    halo, rates, box_ref, code_ref, sel_x_ref, window_z_ref, center_ref, sems,
):
    def copies(i):
        octant = octants[i]
        pairs = (
            (boxes.at[i], box_ref.at[i]), (words.at[i], code_ref.at[i]), (window_z_all.at[octant // 2], window_z_ref.at[i]),
            (sel_x_all.at[octant], sel_x_ref.at[i]), (center_all.at[octant], center_ref.at[i]),
        )
        return [pltpu.make_async_copy(source, target, sems.at[i, n]) for n, (source, target) in enumerate(pairs)]

    def one_message(i, listed):
        y_half = octants[i] % 2
        box = box_ref.at[pl.ds(i, 1)]
        f = code_ref[i].astype(F32) / LEVELS
        lane = iota((32, 128), 1)
        place = lane % 32
        turn = 32 * (1 + y_half)
        spread = [spread_ref[s] for s in range(8)]

        def window_y(a, b):
            return jnp.where(iota(a.shape, 1) < turn, pltpu.roll(a, turn, 1), pltpu.roll(b, turn, 1))

        around_y = window_y(
            box[0, :, :, 384:512].reshape(256, 128), box[0, :, :, 512:640].reshape(256, 128)
        )
        around_z = pick(box[0].reshape(256, 1024), window_z_ref[i])
        f_windows = (window_y(f[:, 384:512], f[:, 512:640]), pick(f, window_z_ref[i]))
        both = jnp.concatenate([around_y, around_z], axis=1)
        high, low = halves(both)
        reacted = dot(rates[0], high) + dot(rates[1], high) + dot(rates[0], low)
        old_rows, new_rows = [[], []], [[], []]
        for w, (around, fw) in enumerate(zip((around_y, around_z), f_windows)):
            inner = fw[8:24]
            scaling = COARSE_STEP / jnp.maximum(inner, FLOOR)
            x_low = scaling * jnp.minimum(inner, pltpu.roll(fw, 1, 0)[8:24])
            x_high = scaling * jnp.minimum(inner, pltpu.roll(fw, 31, 0)[8:24])
            low_side = scaling * jnp.minimum(inner, pltpu.roll(inner, 32, 1))
            high_side = scaling * jnp.minimum(inner, pltpu.roll(inner, 96, 1))
            before = scaling * jnp.where(place[8:24] == 0, 0.0, jnp.minimum(inner, pltpu.roll(inner, 1, 1)))
            after = scaling * jnp.where(place[8:24] == 31, 0.0, jnp.minimum(inner, pltpu.roll(inner, 127, 1)))
            everything = x_low + x_high + low_side + high_side + before + after
            own = 1.0 - ADVECT * x_high
            upwind = ADVECT * x_low
            for s in range(8):
                rows = around[32 * s : 32 * s + 32]
                c = rows[8:24]
                below = pltpu.roll(rows, 1, 0)[8:24]
                above = pltpu.roll(rows, 31, 0)[8:24]
                change = x_low * below + x_high * above
                change = change + low_side * pltpu.roll(c, 32, 1) + high_side * pltpu.roll(c, 96, 1)
                change = change + before * pltpu.roll(c, 1, 1) + after * pltpu.roll(c, 127, 1) - everything * c
                term = reacted[32 * s + 8 : 32 * s + 24, 128 * w : 128 * w + 128]
                old_rows[w].append(c)
                new_rows[w].append(own * c + upwind * below + spread[s] * change + term)
        fractions = jnp.concatenate([fw[8:24] for fw in f_windows], axis=1)
        sides = [
            jnp.concatenate([jnp.concatenate(part[0], axis=0), jnp.concatenate(part[1], axis=0)], axis=1)
            for part in (old_rows, new_rows)
        ]
        side_parts = pick(jnp.concatenate(sides + [fractions], axis=0), center_ref[i])

        wide = species_column(spread_ref, 1.0, 1024)
        long = iota((1, 1024), 1)
        planes = [box[0, :, x, :] for x in (7, 24)]
        mixed = jnp.dot(
            reaction_ref[...], jnp.concatenate(planes, axis=1), precision=lax.Precision.HIGHEST,
            preferred_element_type=F32,
        )
        new_planes = []
        for n, x in enumerate((7, 24)):
            fx = f[x : x + 1]
            scaling = COARSE_STEP / jnp.maximum(fx, FLOOR)
            x_low = scaling * jnp.minimum(fx, f[x - 1 : x])
            x_high = scaling * jnp.minimum(fx, f[x + 1 : x + 2])
            shifts = ((32, long < 32), (992, long >= 992), (1, long % 32 == 0), (1023, long % 32 == 31))
            c = planes[n]
            below = box[0, :, x - 1, :]
            change = x_low * below + x_high * box[0, :, x + 1, :]
            everything = x_low + x_high
            for amount, wall in shifts:
                factor = scaling * jnp.where(wall, 0.0, jnp.minimum(fx, pltpu.roll(fx, amount, 1)))
                change = change + factor * pltpu.roll(c, amount, 1)
                everything = everything + factor
            change = change - everything * c
            moved = (1.0 - ADVECT * x_high) * c + ADVECT * x_low * below + wide * change
            new_planes.append(moved + COARSE_STEP * mixed[:, 1024 * n : 1024 * n + 1024])
        sublane = iota((8, 1024), 0)
        faces = jnp.where(sublane == 0, f[7:8], jnp.where(sublane == 1, f[24:25], 0.0))
        blank = jnp.zeros((8, 1024), F32)
        x_parts = pick(jnp.concatenate(planes + [faces] + new_planes + [blank], axis=0), sel_x_ref[i])

        message[i, 0:16, :] = x_parts[0:16, 0:128]
        message[i, 16:24, :] = jnp.where(iota((8, 128), 0) == 7, listed, x_parts[16:24, 0:128])
        message[i, 24:48, :] = x_parts[0:24, 128:256]
        message[i, 48:80, :] = pack_rows(side_parts[0:128])
        message[i, 80:96, :] = side_parts[256:272]
        message[i, 96:112, :] = x_parts[24:40, 0:128]
        message[i, 112:128, :] = x_parts[24:40, 128:256]
        message[i, 128:160, :] = pack_rows(side_parts[128:256])

        def put_plane(p, x):
            plane = box[0, :, x, :]
            for t in range(8):
                base = 32 + (p * 8 + t) * 16
                halo[base : base + 8, :] = plane[:, 128 * t : 128 * t + 128]
                halo[base + 8 : base + 16, :] = jnp.broadcast_to(f[x : x + 1, 128 * t : 128 * t + 128], (8, 128))

        @pl.when(i == 0)
        def _():
            put_plane(0, 0)

        @pl.when(i == SLOTS - 1)
        def _():
            put_plane(1, 31)

    @pl.when(lax.axis_index("lev") == 0)
    def _():
        for i in range(SLOTS):
            for copy in copies(i):
                copy.start()
        set_rates(rates, reaction_smem, COARSE_STEP)
        where = iota((8, 128), 1)
        listed = jnp.zeros((8, 128), F32)
        for j in range(SLOTS):
            listed = jnp.where(where == j, codes[j].astype(F32), listed)
        halo[...] = jnp.zeros((640, 128), F32)
        halo[16:24, :] = listed

        def each(i, carry):
            for copy in copies(i):
                copy.wait()
            one_message(i, listed)
            return carry

        lax.fori_loop(0, SLOTS, each, 0)


def early_kernel(
    base, again, octants, fine_octants, counts, spread_ref, reaction_smem, box, code, before, code_before, after,
    code_after, sel_x, sel_yz, layers, mean_x, couple, *refs,
):
    states, register, edges, ends, average, cells, later, coef, now, then, rates = refs[5 * again :]
    i = pl.program_id(0)
    at = base + i
    coarse = lax.axis_index("lev") == 0
    used = coarse | (at < counts[0])

    @pl.when(jnp.logical_not(used))
    def _():
        states[0] = box[0]

    @pl.when(used)
    def _():
        @pl.when(i == 0)
        def _():
            set_rates(rates, reaction_smem, jnp.where(coarse, COARSE_STEP, 0.5 * COARSE_STEP))
            clear_rim(cells)
            clear_rim(later)

        f = code[0].astype(F32) / LEVELS
        f_before = jnp.where(coarse & (at > 0), code_before[0, 7:8, :].astype(F32) / LEVELS, 0.0)
        f_after = jnp.where(coarse & (at < SLOTS - 1), code_after[0, 0:1, :].astype(F32) / LEVELS, 0.0)
        load_cells(cells, box[0])
        for t in range(8):
            cells[:, t + 1, 7, :] = before[0, :, 7, 128 * t : 128 * t + 128]
            cells[:, t + 1, 40, :] = after[0, :, 0, 128 * t : 128 * t + 128]
        prepare(f, f_before, f_after, coef, COARSE_STEP)

        def store(s, t, xt, value):
            states[0, s, 8 * xt : 8 * xt + 8, pl.ds(pl.multiple_of(128 * t, 128), 128)] = value

        def store_later(s, t, xt, value):
            later[s, t + 1, 8 + 8 * xt : 16 + 8 * xt, :] = value

        @pl.when(coarse)
        def _():
            spread = [spread_ref[s] for s in range(8)]
            advance(cells, coef, (now, then), rates, spread, store)
            octant = octants[at]
            y_half = octant % 2
            z_half = octant // 2
            wide = species_column(spread_ref, 1.0, 1024)
            c7, c8 = box[0, :, 7, :], box[0, :, 8, :]
            c23, c24 = box[0, :, 23, :], box[0, :, 24, :]
            low_flux = -jnp.minimum(f[7:8], f[8:9]) * (ADVECT * c7 - wide * (c8 - c7))
            high_flux = jnp.minimum(f[23:24], f[24:25]) * (ADVECT * c23 - wide * (c24 - c23))
            x_parts = pick(jnp.concatenate([low_flux, high_flux], axis=0), sel_x[0])

            lane = iota((1, 1024), 1)
            y_row = lane // 32 == 16 - y_half
            y_roll = jnp.where(y_half == 0, 32, 992)
            z_roll = jnp.where(z_half == 0, 1, 1023)
            middle = f[8:24]
            inner_f = jnp.where(y_row, pltpu.roll(middle, y_roll, 1), pltpu.roll(middle, z_roll, 1))
            weight = -jnp.minimum(middle, inner_f)
            fluxes = []
            for s in range(8):
                c = box[0, s, 8:24, :]
                inner = jnp.where(y_row, pltpu.roll(c, y_roll, 1), pltpu.roll(c, z_roll, 1))
                fluxes.append(spread[s] * weight * (c - inner))
            side_parts = pick(jnp.concatenate(fluxes, axis=0), sel_yz[0])
            register[0, 0:16, :] = x_parts[:, 0:128]
            register[0, 16:32, :] = x_parts[:, 128:256]
            register[0, 32:64, :] = pack_rows(side_parts)

        @pl.when(jnp.logical_not(coarse))
        def _():
            spread = [spread_ref[s] * 2.0 for s in range(8)]
            advance(cells, coef, (now, then), rates, spread, store_later)
            advance(later, coef, (now, then), rates, spread, store)
            edges[0, 0:256] = pick(box[0].reshape(256, 1024), layers[0])
            middle = jnp.concatenate([later[:, t + 1, 8:40, :].reshape(256, 128) for t in range(8)], axis=1)
            edges[0, 256:512] = pick(middle, layers[0])
            edges[0, 512:544] = pick(f, layers[0])
            ends[0, 0:8] = box[0, :, 0, :]
            ends[0, 8:16] = box[0, :, 31, :]
            for t in range(8):
                ends[0, 16:24, 128 * t : 128 * t + 128] = later[:, t + 1, 8, :]
                ends[0, 24:32, 128 * t : 128 * t + 128] = later[:, t + 1, 39, :]
            average[0] = 0.5 * left_pick(couple[...], pick(states[0].reshape(256, 1024), mean_x[...]))


def interface_kernel(
    parents, octants, counts, spread_ref, reaction_smem, reaction_ref, words, edges_all, ends_all, average_all, up_x_all,
    up_layer_all, twice_all, mean_x_all, mean_layer_all, couple_all, layers_all, layers_t_all, mean_layers_all,
    own, own_low, own_high, other, other_low, other_high, started, states, payload, codes, rates, messages, taken, coarse,
    first, code, edges, ends, average, up_x, up_layer, twice, mean_x, mean_layer, couple, layers, layers_t, mean_layers,
    sems, fixed_sems,
):
    column = lax.axis_index("box")
    lists = [
        pltpu.make_async_copy(source.at[0, 16:24], codes.at[n], fixed_sems.at[n])
        for n, source in enumerate((own_low, own, own_high))
    ]
    fixed = [
        pltpu.make_async_copy(source, target, fixed_sems.at[3 + n])
        for n, (source, target) in enumerate((
            (up_x_all, up_x), (up_layer_all, up_layer), (twice_all, twice), (mean_x_all, mean_x),
            (mean_layer_all, mean_layer), (couple_all, couple),
        ))
    ]

    def copies(n, last):
        octant = octants[n]
        pairs = (
            (words, code, n), (edges_all, edges, n), (ends_all, ends, n), (average_all, average, n),
            (layers_all, layers, octant), (layers_t_all, layers_t, octant), (mean_layers_all, mean_layers, octant),
            (started, first, n),
        )
        return [
            pltpu.make_async_copy(source.at[index], target.at[n], sems.at[n, k])
            for k, (source, target, index) in enumerate(pairs)
            if last is None or last == (k == 7)
        ]

    def message_copy(source, box, n):
        return pltpu.make_async_copy(source.at[box], messages.at[n], sems.at[n, 8])

    def result_copy(n):
        return pltpu.make_async_copy(first.at[n], states.at[n], sems.at[n, 9])

    for copy in lists:
        copy.start()

    def one_slot(i, carry):
        for copy in copies(i, False):
            copy.wait()
        message_copy(own, 0, i).wait()
        chosen = messages.at[i]
        octant = octants[i]
        y_half = octant % 2
        z_half = octant // 2
        spread = [spread_ref[s] * 2.0 for s in range(8)]
        wide = species_column(spread_ref, 2.0, 1024)
        f = code[i].astype(F32) / LEVELS

        x_old = jnp.concatenate([chosen[0:24], chosen[24:48]], axis=1)
        x_new = jnp.concatenate([chosen[96:112], chosen[112:128]], axis=1)
        x_mid = 0.5 * (x_old[0:16] + x_new)
        ghosts = pick(jnp.concatenate([x_old, x_mid, jnp.zeros((8, 256), F32)], axis=0), up_x[...])
        side_old = chosen[48:80]
        side_mid = 0.5 * (side_old + chosen[128:160])

        def side_ghosts(side):
            high, low = halves(unpack_rows(side))
            high = dot(twice[...], high).astype(BF16)
            low = dot(twice[...], low).astype(BF16)
            return dot(high, up_layer[...]) + dot(low, up_layer[...])

        ghost_old = side_ghosts(side_old)
        ghost_mid = side_ghosts(side_mid)
        high, low = halves(jnp.where(iota((16, 128), 1) < 32, chosen[80:96], 0.0))
        high = dot(twice[0:32, 0:16], high).astype(BF16)
        low = dot(twice[0:32, 0:16], low).astype(BF16)
        f_ghost = dot(high, up_layer[...]) + dot(low, up_layer[...])

        lane = iota((32, 128), 1)
        row = iota((32, 128), 0)
        face = lane // 32 % 2 == 0
        place = lane % 32
        fl = edges[i, 512:544]
        scaling = COARSE_STEP / jnp.maximum(fl, FLOOR)
        at_face = jnp.where(face, scaling, 0.0)
        through = jnp.where(face, jnp.minimum(fl, f_ghost), 0.0)
        x_low = at_face * jnp.where(row == 0, 0.0, jnp.minimum(fl, pltpu.roll(fl, 1, 0)))
        x_high = at_face * jnp.where(row == 31, 0.0, jnp.minimum(fl, pltpu.roll(fl, 31, 0)))
        t_low = at_face * jnp.where(place == 0, 0.0, jnp.minimum(fl, pltpu.roll(fl, 1, 1)))
        t_high = at_face * jnp.where(place == 31, 0.0, jnp.minimum(fl, pltpu.roll(fl, 127, 1)))
        behind = at_face * jnp.minimum(fl, pltpu.roll(fl, 96, 1))
        ahead = jnp.where(face, 0.0, scaling * jnp.minimum(fl, pltpu.roll(fl, 32, 1)))
        everything = x_low + x_high + t_low + t_high + behind
        own_part = 1.0 - ADVECT * x_high
        upwind = ADVECT * x_low
        flux_one = []
        for s in range(8):
            part = slice(32 * s, 32 * s + 32)
            q = through * (ghost_old[part] - edges[i, part])
            flux_one.append(q)
            taken[s] = spread[s] * (scaling * q)

        long = iota((1, 1024), 1)
        f_low, f_high = ghosts[16:17], ghosts[17:18]
        m_low = jnp.minimum(f[0:1], f_low)
        m_high = jnp.minimum(f[31:32], f_high)
        scale_low = COARSE_STEP / jnp.maximum(f[0:1], FLOOR)
        scale_high = COARSE_STEP / jnp.maximum(f[31:32], FLOOR)

        def end_fluxes(low, high, c_low, c_high):
            low_flux = -m_low * (ADVECT * low - wide * (c_low - low))
            high_flux = m_high * (ADVECT * c_high - wide * (high - c_high))
            return low_flux, high_flux

        low_one, high_one = end_fluxes(ghosts[0:8], ghosts[8:16], ends[i, 0:8], ends[i, 8:16])
        end_low = -scale_low * low_one
        end_high = -scale_high * high_one

        crossed = pick(jnp.concatenate([taken[:, 0, :], taken[:, 31, :]], axis=0), layers[i])
        ends_there = pick(jnp.concatenate([end_low, end_high], axis=0), layers_t[i])
        corner_y = jnp.where(z_half == 1, 0, 31)
        corner_z = 64 + jnp.where(y_half == 1, 0, 31)
        turn = corner_y - corner_z + 128
        back = corner_z - corner_y
        flux_two = []
        for s in range(8):
            part = slice(32 * s, 32 * s + 32)
            v = taken[s]
            c = edges[i, 256 + 32 * s : 288 + 32 * s] + v
            c = c + jnp.where(lane == corner_y, pltpu.roll(v, turn, 1), 0.0)
            c = c + jnp.where(lane == corner_z, pltpu.roll(v, back, 1), 0.0)
            c = c + jnp.where(row == 0, ends_there[s : s + 1], jnp.where(row == 31, ends_there[8 + s : 9 + s], 0.0))
            flux_two.append(through * (ghost_mid[part] - c))
        low_two, high_two = end_fluxes(
            ghosts[24:32], ghosts[32:40], ends[i, 16:24] + end_low + crossed[0:8],
            ends[i, 24:32] + end_high + crossed[8:16],
        )

        high, low = halves(taken[...].reshape(256, 128))
        mixed = dot(rates[0], high) + dot(rates[1], high) + dot(rates[0], low)
        totals = []
        for s in range(8):
            v = taken[s]
            below = pltpu.roll(v, 1, 0)
            change = x_low * below + x_high * pltpu.roll(v, 31, 0)
            change = change + t_low * pltpu.roll(v, 1, 1) + t_high * pltpu.roll(v, 127, 1)
            change = change + ahead * pltpu.roll(v, 32, 1) - everything * v + scaling * flux_two[s]
            totals.append(own_part * v + upwind * below + spread[s] * change + mixed[32 * s : 32 * s + 32])
        total = jnp.concatenate(totals, axis=0)

        def tangential(c, fx, scale, inner):
            change = jnp.zeros_like(c)
            everything = inner
            for amount, wall in ((32, long < 32), (992, long >= 992), (1, long % 32 == 0), (1023, long % 32 == 31)):
                factor = scale * jnp.where(wall, 0.0, jnp.minimum(fx, pltpu.roll(fx, amount, 1)))
                change = change + factor * pltpu.roll(c, amount, 1)
                everything = everything + factor
            return change - everything * c

        end_mixed = 0.5 * COARSE_STEP * jnp.dot(
            reaction_ref[...], jnp.concatenate([end_low, end_high], axis=1), precision=lax.Precision.HIGHEST,
            preferred_element_type=F32,
        )
        inner_low = jnp.minimum(f[0:1], f[1:2])
        inner_high = jnp.minimum(f[30:31], f[31:32])
        row0 = (1.0 - ADVECT * (scale_low * inner_low)) * end_low - scale_low * low_two + end_mixed[:, 0:1024]
        row0 = row0 + wide * tangential(end_low, f[0:1], scale_low, scale_low * inner_low)
        row1 = (wide + ADVECT) * (COARSE_STEP / jnp.maximum(f[1:2], FLOOR) * inner_low) * end_low
        row30 = wide * (COARSE_STEP / jnp.maximum(f[30:31], FLOOR) * inner_high) * end_high
        row31 = end_high - scale_high * high_two + end_mixed[:, 1024:2048]
        row31 = row31 + wide * tangential(end_high, f[31:32], scale_high, scale_high * inner_high)

        x_parts = pick(
            jnp.concatenate([low_one + low_two, high_one + high_two, row0 + row1, row30 + row31], axis=0), mean_x[...]
        )
        coarse[...] = (average[i] + 0.5 * left_pick(couple[...], pick(total, mean_layers[i]))).reshape(8, 16, 256)
        coarse[:, 0, :] += 0.5 * x_parts[16:24]
        coarse[:, 15, :] += 0.5 * x_parts[24:32]
        for q in range(3):
            payload[q, i] = coarse[...].reshape(128, 256)[40 * q : 40 * q + 40]
        payload[3, i, 0:8] = coarse[...].reshape(128, 256)[120:128]
        payload[3, i, 8:24] = 0.5 * x_parts[0:16]
        fluxes = jnp.concatenate([flux_one[s] + flux_two[s] for s in range(8)], axis=0)
        sides = left_pick(couple[...], pick(fluxes, mean_layer[...])).reshape(8, 16, 128)
        sides = jnp.concatenate([(-0.5 * spread[s]) * sides[s] for s in range(8)], axis=0)
        sides = pack_rows(sides)
        payload[3, i, 24:40, 0:128] = sides[0:16]
        payload[3, i, 24:40, 128:256] = sides[16:32]

        copies(i, True)[0].wait()
        high, low = halves(total)
        for n in range(4):
            part = slice(256 * n, 256 * n + 256)
            added = dot(high, layers[i, :, part]) + dot(low, layers[i, :, part])
            first[i, :, :, part] += added.reshape(8, 32, 256)
        first[i, :, 0, :] += row0
        first[i, :, 1, :] += row1
        first[i, :, 30, :] += row30
        first[i, :, 31, :] += row31
        result_copy(i).start()
        return carry

    @pl.when(counts[0] > 0)
    def _():
        for copy in fixed:
            copy.start()
        for n in range(SLOTS):

            @pl.when(n < counts[0])
            def _():
                for copy in copies(n, None):
                    copy.start()
                home = parents[n] // SLOTS
                away = (home >> 1) - (column >> 1)
                same = ((home - column) & 1) == 0
                for source, is_same, step in (
                    (own_low, True, -1), (own, True, 0), (own_high, True, 1),
                    (other_low, False, -1), (other, False, 0), (other_high, False, 1),
                ):

                    @pl.when((same == is_same) & (away == step))
                    def _():
                        message_copy(source, parents[n] % SLOTS, n).start()

        set_rates(rates, reaction_smem, 0.5 * COARSE_STEP)
        for copy in fixed:
            copy.wait()
        lax.fori_loop(0, counts[0], one_slot, 0)
        for n in range(SLOTS):

            @pl.when(n < counts[0])
            def _():
                result_copy(n).wait()

    for copy in lists:
        copy.wait()


def decode(code):
    safe = jnp.maximum(code, 0)
    return safe // (OFFSETS * SLOTS) + 1, safe // SLOTS % OFFSETS - REACH, safe % SLOTS


def route_kernel(codes, mine, others, to_low, stay, to_high):
    column = lax.axis_index("box")
    for n, (step, target) in enumerate(((-1, to_low), (0, stay), (1, to_high))):
        for j in range(SLOTS):
            row, offset, slot = decode(codes[n, 7, j].astype(jnp.int32))
            child = column + 2 * step + offset
            target[j] = jnp.where(((child - column) & 1) == 0, mine[row, slot], others[row, slot])


def choose_kernel(codes, from_low, stay, from_high, chosen):
    column = lax.axis_index("box")
    for j in range(SLOTS):
        _, offset, _ = decode(codes[j])
        away = ((column + offset) >> 1) - (column >> 1)
        chosen[j] = jnp.where(away < 0, from_low[j], jnp.where(away == 0, stay[j], from_high[j]))


def finish_kernel(
    octants, codes, spread_ref, updated, message, register, code_words, halo, other_low, other, other_high,
    part0, part1, part2, part3, sel_x, sel_yz, states, chosen,
):
    i = pl.program_id(0)
    column = lax.axis_index("box")
    states[...] = updated[...]

    @pl.when(lax.axis_index("lev") == 0)
    def _():
        wide = species_column(spread_ref, 1.0, 128)
        odd = (column & 1) == 1

        def end_plane(x, p, neighbour_p, neighbour):
            f = code_words[0, x : x + 1, :].astype(F32) / LEVELS
            scaling = COARSE_STEP / jnp.maximum(f, FLOOR)
            for t in range(8):
                part = slice(128 * t, 128 * t + 128)
                base = 32 + (p * 8 + t) * 16
                there = 32 + (neighbour_p * 8 + t) * 16
                c = halo[base : base + 8, :]
                g = neighbour(there, there + 8)
                m = jnp.minimum(f[:, part], neighbour(there + 8, there + 9))
                if p == 0:
                    gain = m * (ADVECT * g - wide * (c - g))
                else:
                    gain = -m * (ADVECT * c - wide * (g - c))
                states[0, :, x, part] += scaling[:, part] * gain

        @pl.when(i == 0)
        def _():
            end_plane(0, 0, 1, lambda a, b: jnp.where(odd, other[a:b, :], other_low[a:b, :]))

        @pl.when(i == SLOTS - 1)
        def _():
            end_plane(31, 1, 0, lambda a, b: jnp.where(odd, other_high[a:b, :], other[a:b, :]))

        child = codes[i]

        @pl.when(child >= 0)
        def _():
            for q, part in enumerate((part0, part1, part2, part3)):
                chosen[40 * q : 40 * q + 40, :] = part[0]
            octant = octants[i]
            y_half = octant % 2
            z_half = octant // 2
            lane = iota((1, 1024), 1)
            inside = (lane // 512 == y_half) & (lane % 32 // 16 == z_half)
            own_f = jnp.concatenate([message[0, 0:24, :], message[0, 24:48, :]], axis=1)
            half = iota((16, 256), 0) < 8
            x_f = jnp.where(half, own_f[16:17], own_f[17:18])
            reg_x = jnp.concatenate([register[0, 0:16, :], register[0, 16:32, :]], axis=1)
            fix_x = COARSE_STEP / jnp.maximum(x_f, FLOOR) * (chosen[128:144, :] - reg_x)
            side_f = jnp.concatenate([message[0, 80:96, :]] * 2, axis=0)
            sides = jnp.concatenate([chosen[144:160, 0:128], chosen[144:160, 128:256]], axis=0)
            fix_sides = COARSE_STEP / jnp.maximum(side_f, FLOOR) * (sides - register[0, 32:64, :])
            planes = pick(fix_x, sel_x[0])
            states[0, :, 7, :] += planes[0:8]
            states[0, :, 24, :] += planes[8:16]
            filled = pick(chosen[0:128, :], sel_x[0])
            added = pick(unpack_rows(fix_sides), sel_yz[0])
            for s in range(8):
                part = slice(16 * s, 16 * s + 16)
                here = states[0, s, 8:24, :]
                states[0, s, 8:24, :] = jnp.where(inside, filled[part], here + added[part])


def shifted(block, axis, distance):
    devices = range(lax.axis_size(axis))
    return lax.ppermute(block, axis, [(i - distance, i) for i in devices if i - distance in devices])


def per_device(
    box_states, cell_code, diffusivity, reaction, coarse_child, coarse_octant, fine_parent, fine_octant, fine_count
):
    row = lax.axis_index("lev")
    count = lax.axis_size("box")
    swap = [(i, i ^ 1) for i in range(count)]
    vmem = pltpu.CompilerParams(vmem_limit_bytes=62 * 1024 * 1024)
    small = pltpu.CompilerParams(vmem_limit_bytes=8 * 1024 * 1024)

    def whole(a):
        zeros = (0,) * a.ndim
        return pl.BlockSpec(a.shape, lambda i, *_: zeros)

    def each(shape):
        tail = (0,) * len(shape)
        return pl.BlockSpec((1,) + shape, lambda i, *_: (i,) + tail)

    smem = pl.BlockSpec(memory_space=pltpu.SMEM)
    hbm = pl.BlockSpec(memory_space=pl.ANY)
    in_vmem = pl.BlockSpec(memory_space=pltpu.VMEM)
    previous = lambda i: jnp.maximum(i - 1, 0)
    following = lambda i: jnp.minimum(i + 1, SLOTS - 1)
    shape = jax.ShapeDtypeStruct
    sel_x, sel_yz = table(SEL_X), table(SEL_YZ)
    by_octant = lambda i, octants, *_: (octants[i], 0, 0)

    message, halo = pl.pallas_call(
        message_kernel,
        in_specs=[smem] * 4 + [in_vmem] + [hbm] * 5,
        out_specs=[in_vmem, in_vmem],
        scratch_shapes=[
            pltpu.VMEM((2, 256, 256), BF16),
            pltpu.VMEM((SLOTS, 8, 32, 1024), F32),
            pltpu.VMEM((SLOTS, 32, 1024), jnp.int32),
            pltpu.VMEM((SLOTS, 1024, 256), BF16),
            pltpu.VMEM((SLOTS, 1024, 128), BF16),
            pltpu.VMEM((SLOTS, 256, 128), BF16),
            pltpu.SemaphoreType.DMA((SLOTS, 5)),
        ],
        out_shape=[shape((SLOTS, 160, 128), F32), shape((640, 128), F32)],
        compiler_params=vmem,
        name="shells",
    )(
        coarse_octant, coarse_child, diffusivity, reaction, reaction, box_states, cell_code, sel_x, table(WINDOW_Z),
        table(CENTER),
    )

    mean_x, couple = table(0.25 * UP_X.T), table(TWICE.T)
    layers, layers_t = table(LAYERS), table(LAYERS.transpose(0, 2, 1))

    def early(base, boxes, *carried):
        def at(dims):
            tail = (0,) * len(dims)
            return pl.BlockSpec((1,) + dims, lambda i, *_: (base + i,) + tail)

        def for_octant(dims):
            return pl.BlockSpec((1,) + dims, lambda i, octants, *_: (octants[base + i], 0, 0))

        blocks = [(8, 32, 1024), (64, 128), (544, 128), (32, 1024), (128, 256)]
        return pl.pallas_call(
            functools.partial(early_kernel, base, len(carried) > 0),
            grid_spec=pltpu.PrefetchScalarGridSpec(
                num_scalar_prefetch=3,
                grid=(boxes,),
                in_specs=[
                    smem,
                    smem,
                    at((8, 32, 1024)),
                    at((32, 1024)),
                    pl.BlockSpec((1, 8, 8, 1024), lambda i, *_: (previous(base + i), 0, 3, 0)),
                    pl.BlockSpec((1, 8, 1024), lambda i, *_: (previous(base + i), 3, 0)),
                    pl.BlockSpec((1, 8, 8, 1024), lambda i, *_: (following(base + i), 0, 0, 0)),
                    pl.BlockSpec((1, 8, 1024), lambda i, *_: (following(base + i), 0, 0)),
                    for_octant((1024, 256)),
                    for_octant((1024, 128)),
                    pl.BlockSpec((1, 1024, 128), lambda i, octants, fine, *_: (fine[base + i], 0, 0)),
                    whole(mean_x),
                    whole(couple),
                ]
                + [hbm] * len(carried),
                out_specs=[at(dims) for dims in blocks],
                scratch_shapes=[
                    pltpu.VMEM((8, 10, 48, 128), F32),
                    pltpu.VMEM((8, 10, 48, 128), F32),
                    pltpu.VMEM((9, 8, 32, 128), F32),
                    pltpu.VMEM((8, 2, 32, 128), F32),
                    pltpu.VMEM((8, 2, 32, 128), F32),
                    pltpu.VMEM((2, 256, 256), BF16),
                ],
            ),
            out_shape=[shape((SLOTS,) + dims, F32) for dims in blocks],
            input_output_aliases={16 + n: n for n in range(len(carried))},
            compiler_params=vmem,
            cost_estimate=pl.CostEstimate(flops=10**9, bytes_accessed=30 * 10**6, transcendentals=0),
            name=f"early_{base}",
        )(
            coarse_octant, fine_octant, fine_count, diffusivity, reaction, box_states, cell_code, box_states, cell_code,
            box_states, cell_code, sel_x, sel_yz, layers_t, mean_x, couple, *carried,
        )

    updated, *carried = early(0, 3)
    spread_out = [lax.ppermute(message, "lev", [(0, r)]) for r in (1, 3, 2)]
    *spread_out, updated = lax.optimization_barrier((*spread_out, updated))
    own = jnp.where(row == 0, halo.reshape(SLOTS, 160, 128), spread_out[0] + spread_out[1] + spread_out[2])
    own_low = shifted(own, "box", 2)
    own_high = shifted(own, "box", -2)
    updated, register, *carried = early(3, 1, updated, *carried)
    own_low, own_high, updated = lax.optimization_barrier((own_low, own_high, updated))
    other = lax.ppermute(own, "box", swap)
    other_low = lax.ppermute(own_low, "box", swap)
    other_high = lax.ppermute(own_high, "box", swap)

    up_x, up_layer, twice, mean_layer = table(UP_X), table(UP_LAYER), table(TWICE), table(0.25 * UP_LAYER.T)
    mean_layers = table(LAYERS @ (0.25 * UP_X.T))
    constants = [up_x, up_layer, twice, mean_x, mean_layer, couple]
    states, payload, codes = pl.pallas_call(
        interface_kernel,
        in_specs=[smem] * 5 + [in_vmem] + [hbm] * 20,
        out_specs=[hbm, in_vmem, smem],
        scratch_shapes=[
            pltpu.VMEM((2, 256, 256), BF16),
            pltpu.VMEM((SLOTS, 160, 128), F32),
            pltpu.VMEM((8, 32, 128), F32),
            pltpu.VMEM((8, 16, 256), F32),
            pltpu.VMEM((SLOTS, 8, 32, 1024), F32),
            pltpu.VMEM((SLOTS, 32, 1024), jnp.int32),
            pltpu.VMEM((SLOTS, 544, 128), F32),
            pltpu.VMEM((SLOTS, 32, 1024), F32),
            pltpu.VMEM((SLOTS, 128, 256), F32),
        ]
        + [pltpu.VMEM(a.shape, BF16) for a in constants]
        + [
            pltpu.VMEM((SLOTS, 128, 1024), BF16),
            pltpu.VMEM((SLOTS, 1024, 128), BF16),
            pltpu.VMEM((SLOTS, 128, 256), BF16),
            pltpu.SemaphoreType.DMA((SLOTS, 10)),
            pltpu.SemaphoreType.DMA((9,)),
        ],
        out_shape=[
            shape((SLOTS, 8, 32, 1024), F32), shape((4, SLOTS, 40, 256), F32), shape((3, 8, 128), F32)
        ],
        input_output_aliases={25: 0},
        compiler_params=vmem,
        name="interfaces",
    )(
        fine_parent, fine_octant, fine_count, diffusivity, reaction, reaction, cell_code, *carried, *constants, layers,
        layers_t, mean_layers, own, own_low, own_high, other, other_low, other_high, updated,
    )

    mine = lax.all_to_all(payload, "lev", 0, 0)
    others = lax.ppermute(mine, "box", swap)
    bundle = shape((SLOTS, 40, 256), F32)
    to_low, stay, to_high = pl.pallas_call(
        route_kernel,
        in_specs=[smem] + [in_vmem] * 2,
        out_specs=[in_vmem] * 3,
        out_shape=[bundle] * 3,
        compiler_params=small,
        name="route",
    )(codes, mine, others)
    from_high = shifted(to_low, "box", -2)
    from_low = shifted(to_high, "box", 2)
    quarter = pl.pallas_call(
        choose_kernel,
        in_specs=[smem] + [in_vmem] * 3,
        out_specs=in_vmem,
        out_shape=bundle,
        compiler_params=small,
        name="choose",
    )(coarse_child, from_low, stay, from_high)
    quarters = [quarter] + [lax.ppermute(quarter, "lev", [(q, 0)]) for q in range(1, 4)]

    back_x, back_yz = table(SEL_X.transpose(0, 2, 1)), table(SEL_YZ.transpose(0, 2, 1))
    flat = [a.reshape(640, 128) for a in (other_low, other, other_high)]
    return pl.pallas_call(
        finish_kernel,
        grid_spec=pltpu.PrefetchScalarGridSpec(
            num_scalar_prefetch=2,
            grid=(SLOTS,),
            in_specs=[smem, each((8, 32, 1024)), each((160, 128)), each((64, 128)), each((32, 1024))]
            + [whole(halo)] * 4
            + [each((40, 256))] * 4
            + [pl.BlockSpec((1, 256, 1024), by_octant), pl.BlockSpec((1, 128, 1024), by_octant)],
            out_specs=each((8, 32, 1024)),
            scratch_shapes=[pltpu.VMEM((160, 256), F32)],
        ),
        out_shape=shape((SLOTS, 8, 32, 1024), F32),
        input_output_aliases={3: 0},
        compiler_params=vmem,
        name="finish",
    )(
        coarse_octant, coarse_child, diffusivity, states, message, register, cell_code, halo, *flat,
        *quarters, back_x, back_yz,
    )


def solution(mesh):
    return jax.shard_map(
        per_device,
        mesh=mesh,
        in_specs=(
            P(("lev", "box"), None, None, None),
            P(("lev", "box"), None, None),
            P(),
            P(),
            P("box"),
            P("box"),
            P(("lev", "box")),
            P(("lev", "box")),
            P(("lev", "box")),
        ),
        out_specs=P(("lev", "box"), None, None, None),
        check_vma=False,
    )
```

profile of v0, /device:TPU:3, one launch (start us, length us, event | category | flops | bytes accessed | tf_op | source)
XLA Modules:
  0.0 111.1 jit_solution(8400450896870106841)
XLA Ops:
  0.0 9.8 %shells.1 = (f32[4,160,128]{2,1,0:T(8,128)}, f32[640,128]{1,0:T(8,128)}) custom-call(s32[4]{0:T(128)} %octants.9, s32[4]{0:T(128)} %codes.5, f32[8]{0:T(128)} %spread_ref.9, f32[8,8]{1,0:T(8,128)} %reaction_ref.3, f32[8,8]{1,0:T(8,128)} %reaction_ref.3, f32[4,8,32,1024]{3,2,1,0:T(8,128)} %after.3, s32[4,32,1024]{2,1,0:T(8,128)} %code_words.1, ...), custom_call_target="tpu_custom_call" | custom-call | tf_op jit(solution)/shard_map/shells/pallas_call | solution.py:779
  9.8 1.3 %collective-permute-start = (f32[4,160,128]{2,1,0:T(8,128)}, f32[4,160,128]{2,1,0:T(8,128)S(1)}, u32[]{:S(2)}, u32[]{:S(2)}) collective-permute-start(f32[4,160,128]{2,1,0:T(8,128)} %get-tuple-element.30.message), channel_id=1, source_target_pairs={{0,32},{1,33},{2,34},{3,35},{4,36},{5,37},{6,38},{7,39},{8,40},{9,... | collective-permute-start | bytes 983048 | tf_op jit(solution)/shard_map/ppermute | solution.py:854
  11.1 1.3 %collective-permute-start.1 = (f32[4,160,128]{2,1,0:T(8,128)}, f32[4,160,128]{2,1,0:T(8,128)S(1)}, u32[]{:S(2)}, u32[]{:S(2)}) collective-permute-start(f32[4,160,128]{2,1,0:T(8,128)} %get-tuple-element.30.message), channel_id=1, source_target_pairs={{0,96},{1,97},{2,98},{3,99},{4,100},{5,101},{6,102},{7,103},{8,104... | collective-permute-start | bytes 983048 | tf_op jit(solution)/shard_map/ppermute | solution.py:854
  12.5 1.3 %collective-permute-start.2 = (f32[4,160,128]{2,1,0:T(8,128)}, f32[4,160,128]{2,1,0:T(8,128)S(1)}, u32[]{:S(2)}, u32[]{:S(2)}) collective-permute-start(f32[4,160,128]{2,1,0:T(8,128)} %get-tuple-element.30.message), channel_id=1, source_target_pairs={{0,64},{1,65},{2,66},{3,67},{4,68},{5,69},{6,70},{7,71},{8,72},{9,... | collective-permute-start | bytes 983048 | tf_op jit(solution)/shard_map/ppermute | solution.py:854
  14.4 0.0 copy-start.7
  14.4 12.6 %early_0.1 = (f32[4,8,32,1024]{3,2,1,0:T(8,128)}, f32[4,64,128]{2,1,0:T(8,128)}, f32[4,544,128]{2,1,0:T(8,128)}, f32[4,32,1024]{2,1,0:T(8,128)}, f32[4,128,256]{2,1,0:T(8,128)}) custom-call(s32[4]{0:T(128)} %octants.9, s32[4]{0:T(128)} %octants.8, s32[1]{0:T(128)S(6)} %copy.39.counts, f32[8]{0:T(128)} %spread_ref.9, f32[8,8]{1,0:T(8,128)} %reaction_ref.3, ...), custom_call_target="tpu_custom_call" | custom-call | flops 1000000000 | bytes 30000000 | tf_op jit(solution)/shard_map/early_0/pallas_call | solution.py:812
  27.1 0.0 collective-permute-done
  27.1 0.0 collective-permute-done.1
  27.1 0.0 collective-permute-done.2
  27.1 0.0 copy-done.7
  27.1 0.1 add_select_fusion.own
  27.2 0.0 copy-start.3
  27.2 2.8 %collective-permute-start.3 = (f32[4,160,128]{2,1,0:T(8,128)S(1)}, f32[4,160,128]{2,1,0:T(8,128)S(1)}, u32[]{:S(2)}, u32[]{:S(2)}) collective-permute-start(f32[4,160,128]{2,1,0:T(8,128)S(1)} %add_select_fusion.own), channel_id=1, source_target_pairs={{0,2},{1,3},{2,4},{3,5},{4,6},{5,7},{6,8},{7,9},{8,10},{9,11},{10,... | collective-permute-start | bytes 983048 | tf_op jit(solution)/shard_map/ppermute | solution.py:750
  30.0 4.6 %collective-permute-start.4 = (f32[4,160,128]{2,1,0:T(8,128)S(1)}, f32[4,160,128]{2,1,0:T(8,128)S(1)}, u32[]{:S(2)}, u32[]{:S(2)}) collective-permute-start(f32[4,160,128]{2,1,0:T(8,128)S(1)} %add_select_fusion.own), channel_id=1, source_target_pairs={{2,0},{3,1},{4,2},{5,3},{6,4},{7,5},{8,6},{9,7},{10,8},{11,9},{12,... | collective-permute-start | bytes 983048 | tf_op jit(solution)/shard_map/ppermute | solution.py:750
  34.6 1.3 %collective-permute-start.5 = (f32[4,160,128]{2,1,0:T(8,128)S(1)}, f32[4,160,128]{2,1,0:T(8,128)S(1)}, u32[]{:S(2)}, u32[]{:S(2)}) collective-permute-start(f32[4,160,128]{2,1,0:T(8,128)S(1)} %add_select_fusion.own), channel_id=1, source_target_pairs={{0,1},{1,0},{2,3},{3,2},{4,5},{5,4},{6,7},{7,6},{8,9},{9,8},{10,11... | collective-permute-start | bytes 983048 | tf_op jit(solution)/shard_map/ppermute | solution.py:861
  35.9 7.0 %early_3.1 = (f32[4,8,32,1024]{3,2,1,0:T(8,128)}, f32[4,64,128]{2,1,0:T(8,128)}, f32[4,544,128]{2,1,0:T(8,128)}, f32[4,32,1024]{2,1,0:T(8,128)}, f32[4,128,256]{2,1,0:T(8,128)}) custom-call(s32[4]{0:T(128)} %octants.9, s32[4]{0:T(128)} %octants.8, s32[1]{0:T(128)S(6)} %copy.39.counts, ...), custom_call_target="tpu_custom_call", output_to_operand_aliasing={{0}: (16, {}), {1}: (17, {}), {2}: (18, {}), {3}: (19, {}),... | custom-call | flops 1000000000 | bytes 30000000 | tf_op jit(solution)/shard_map/early_3/pallas_call | solution.py:812
  42.9 0.0 copy-done.3
  42.9 0.0 collective-permute-done.3.own_low
  42.9 0.0 collective-permute-done.4.own_high
  43.0 0.1 collective-permute-start.6
  43.1 0.5 collective-permute-start.7
  43.5 0.0 collective-permute-done.5.other
  43.6 1.1 %collective-permute-done.6.other_low = f32[4,160,128]{2,1,0:T(8,128)S(1)} collective-permute-done((f32[4,160,128]{2,1,0:T(8,128)S(1)}, f32[4,160,128]{2,1,0:T(8,128)S(1)}, u32[]{:S(2)}, u32[]{:S(2)}) %collective-permute-start.6) | collective-permute-done | bytes 327712 | tf_op jit(solution)/shard_map/ppermute | solution.py:862
  44.7 0.5 collective-permute-done.7.other_high
  45.1 0.0 copy-done.9
  45.1 0.2 copy-done.5
  45.4 0.5 copy-done.6
  45.9 3.0 %interfaces.1 = (f32[4,8,32,1024]{3,2,1,0:T(8,128)}, f32[4,4,40,256]{3,2,1,0:T(8,128)}, f32[3,8,128]{2,1,0:T(8,128)}) custom-call(s32[4]{0:T(128)} %parents.1, s32[4]{0:T(128)} %octants.8, s32[1]{0:T(128)S(6)} %copy.39.counts, f32[8]{0:T(128)} %spread_ref.9, f32[8,8]{1,0:T(8,128)} %reaction_ref.3, ...), custom_call_target="tpu_custom_call", output_to_operand_aliasing={{0}: (25, {})} | custom-call | tf_op jit(solution)/shard_map/interfaces/pallas_call | solution.py:868
  48.9 21.5 %all_to_all.5.mine = f32[4,4,40,256]{3,2,1,0:T(8,128)S(1)} all-to-all(f32[4,4,40,256]{3,2,1,0:T(8,128)} %get-tuple-element.51), channel_id=1, replica_groups=mesh['lev'=4,'box'=32] {'lev'}, dimensions={0} | all-to-all | bytes 1310720 | tf_op jit(solution)/shard_map/all_to_all | solution.py:902
  70.4 0.0 collective-permute-start.8
  70.4 2.1 %collective-permute-done.8.others = f32[4,4,40,256]{3,2,1,0:T(8,128)S(1)} collective-permute-done((f32[4,4,40,256]{3,2,1,0:T(8,128)S(1)}, f32[4,4,40,256]{3,2,1,0:T(8,128)S(1)}, u32[]{:S(2)}, u32[]{:S(2)}) %collective-permute-start.8) | collective-permute-done | bytes 655392 | tf_op jit(solution)/shard_map/ppermute | solution.py:903
  72.5 0.7 copy-done.1
  73.2 0.9 route.1
  74.1 3.4 %collective-permute-start.10 = (f32[4,40,256]{2,1,0:T(8,128)S(1)}, f32[4,40,256]{2,1,0:T(8,128)S(1)}, u32[]{:S(2)}, u32[]{:S(2)}) collective-permute-start(f32[4,40,256]{2,1,0:T(8,128)S(1)} %get-tuple-element.54), channel_id=1, source_target_pairs={{2,0},{3,1},{4,2},{5,3},{6,4},{7,5},{8,6},{9,7},{10,8},{11,9},{12,... | collective-permute-start | bytes 491528 | tf_op jit(solution)/shard_map/ppermute | solution.py:750
  77.5 1.9 %collective-permute-start.9 = (f32[4,40,256]{2,1,0:T(8,128)S(1)}, f32[4,40,256]{2,1,0:T(8,128)S(1)}, u32[]{:S(2)}, u32[]{:S(2)}) collective-permute-start(f32[4,40,256]{2,1,0:T(8,128)S(1)} %get-tuple-element.52), channel_id=1, source_target_pairs={{0,2},{1,3},{2,4},{3,5},{4,6},{5,7},{6,8},{7,9},{8,10},{9,11},{10,... | collective-permute-start | bytes 491528 | tf_op jit(solution)/shard_map/ppermute | solution.py:750
  79.5 2.2 %collective-permute-done.10.from_high = f32[4,40,256]{2,1,0:T(8,128)S(1)} collective-permute-done((f32[4,40,256]{2,1,0:T(8,128)S(1)}, f32[4,40,256]{2,1,0:T(8,128)S(1)}, u32[]{:S(2)}, u32[]{:S(2)}) %collective-permute-start.10) | collective-permute-done | bytes 163872 | tf_op jit(solution)/shard_map/ppermute | solution.py:750
  81.7 5.2 %collective-permute-done.9.from_low = f32[4,40,256]{2,1,0:T(8,128)S(1)} collective-permute-done((f32[4,40,256]{2,1,0:T(8,128)S(1)}, f32[4,40,256]{2,1,0:T(8,128)S(1)}, u32[]{:S(2)}, u32[]{:S(2)}) %collective-permute-start.9) | collective-permute-done | bytes 163872 | tf_op jit(solution)/shard_map/ppermute | solution.py:750
  86.9 0.6 choose.1.part0
  87.5 1.3 %collective-permute-start.11 = (f32[4,40,256]{2,1,0:T(8,128)S(1)}, f32[4,40,256]{2,1,0:T(8,128)S(1)}, u32[]{:S(2)}, u32[]{:S(2)}) collective-permute-start(f32[4,40,256]{2,1,0:T(8,128)S(1)} %choose.1.part0), channel_id=1, source_target_pairs={{32,0},{33,1},{34,2},{35,3},{36,4},{37,5},{38,6},{39,7},{40,8},{41... | collective-permute-start | bytes 491528 | tf_op jit(solution)/shard_map/ppermute | solution.py:923
  88.8 1.3 %collective-permute-start.12 = (f32[4,40,256]{2,1,0:T(8,128)S(1)}, f32[4,40,256]{2,1,0:T(8,128)S(1)}, u32[]{:S(2)}, u32[]{:S(2)}) collective-permute-start(f32[4,40,256]{2,1,0:T(8,128)S(1)} %choose.1.part0), channel_id=1, source_target_pairs={{64,0},{65,1},{66,2},{67,3},{68,4},{69,5},{70,6},{71,7},{72,8},{73... | collective-permute-start | bytes 491528 | tf_op jit(solution)/shard_map/ppermute | solution.py:923
  90.1 1.3 %collective-permute-start.13 = (f32[4,40,256]{2,1,0:T(8,128)S(1)}, f32[4,40,256]{2,1,0:T(8,128)S(1)}, u32[]{:S(2)}, u32[]{:S(2)}) collective-permute-start(f32[4,40,256]{2,1,0:T(8,128)S(1)} %choose.1.part0), channel_id=1, source_target_pairs={{96,0},{97,1},{98,2},{99,3},{100,4},{101,5},{102,6},{103,7},{104,8... | collective-permute-start | bytes 491528 | tf_op jit(solution)/shard_map/ppermute | solution.py:923
  91.4 2.2 %collective-permute-done.11.part1 = f32[4,40,256]{2,1,0:T(8,128)S(1)} collective-permute-done((f32[4,40,256]{2,1,0:T(8,128)S(1)}, f32[4,40,256]{2,1,0:T(8,128)S(1)}, u32[]{:S(2)}, u32[]{:S(2)}) %collective-permute-start.11) | collective-permute-done | bytes 163872 | tf_op jit(solution)/shard_map/ppermute | solution.py:923
  93.6 2.9 %collective-permute-done.12.part2 = f32[4,40,256]{2,1,0:T(8,128)S(1)} collective-permute-done((f32[4,40,256]{2,1,0:T(8,128)S(1)}, f32[4,40,256]{2,1,0:T(8,128)S(1)}, u32[]{:S(2)}, u32[]{:S(2)}) %collective-permute-start.12) | collective-permute-done | bytes 163872 | tf_op jit(solution)/shard_map/ppermute | solution.py:923
  96.4 5.4 %collective-permute-done.13.part3 = f32[4,40,256]{2,1,0:T(8,128)S(1)} collective-permute-done((f32[4,40,256]{2,1,0:T(8,128)S(1)}, f32[4,40,256]{2,1,0:T(8,128)S(1)}, u32[]{:S(2)}, u32[]{:S(2)}) %collective-permute-start.13) | collective-permute-done | bytes 163872 | tf_op jit(solution)/shard_map/ppermute | solution.py:923
  101.8 0.0 copy-done
  101.8 0.0 copy-done.11
  101.8 0.6 copy-done.12
  102.5 8.5 %finish.1 = f32[4,8,32,1024]{3,2,1,0:T(8,128)} custom-call(s32[4]{0:T(128)} %octants.9, s32[4]{0:T(128)} %codes.5, f32[8]{0:T(128)} %spread_ref.9, f32[4,8,32,1024]{3,2,1,0:T(8,128)} %get-tuple-element.48.updated, f32[4,160,128]{2,1,0:T(8,128)} %get-tuple-element.30.message, ...), custom_call_target="tpu_custom_call", output_to_operand_aliasing={{}: (3, {})} | custom-call | tf_op jit(solution)/shard_map/finish/pallas_call | solution.py:927
  (15 shorter events, 0.0 us)
Async XLA Ops:
  9.8 17.2 %collective-permute-start = (f32[4,160,128]{2,1,0:T(8,128)}, f32[4,160,128]{2,1,0:T(8,128)S(1)}, u32[]{:S(2)}, u32[]{:S(2)}) collective-permute-start(f32[4,160,128]{2,1,0:T(8,128)} %get-tuple-element.30.message), channel_id=1, source_target_pairs={{0,32},{1,33},{2,34},{3,35},{4,36},{5,37},{6,38},{7,39},{8,40},{9,... | collective-permute-start | bytes 983048 | tf_op jit(solution)/shard_map/ppermute | solution.py:854
  11.1 15.9 %collective-permute-start.1 = (f32[4,160,128]{2,1,0:T(8,128)}, f32[4,160,128]{2,1,0:T(8,128)S(1)}, u32[]{:S(2)}, u32[]{:S(2)}) collective-permute-start(f32[4,160,128]{2,1,0:T(8,128)} %get-tuple-element.30.message), channel_id=1, source_target_pairs={{0,96},{1,97},{2,98},{3,99},{4,100},{5,101},{6,102},{7,103},{8,104... | collective-permute-start | bytes 983048 | tf_op jit(solution)/shard_map/ppermute | solution.py:854
  12.5 14.6 %collective-permute-start.2 = (f32[4,160,128]{2,1,0:T(8,128)}, f32[4,160,128]{2,1,0:T(8,128)S(1)}, u32[]{:S(2)}, u32[]{:S(2)}) collective-permute-start(f32[4,160,128]{2,1,0:T(8,128)} %get-tuple-element.30.message), channel_id=1, source_target_pairs={{0,64},{1,65},{2,66},{3,67},{4,68},{5,69},{6,70},{7,71},{8,72},{9,... | collective-permute-start | bytes 983048 | tf_op jit(solution)/shard_map/ppermute | solution.py:854
  14.4 12.7 %copy-start.7 = (f32[640,128]{1,0:T(8,128)S(1)}, f32[640,128]{1,0:T(8,128)}, u32[]{:S(2)}) copy-start(f32[640,128]{1,0:T(8,128)} %get-tuple-element.40.halo) | copy-start | bytes 983044
  27.2 15.7 %copy-start.3 = (f32[4,160,128]{2,1,0:T(8,128)}, f32[4,160,128]{2,1,0:T(8,128)S(1)}, u32[]{:S(2)}) copy-start(f32[4,160,128]{2,1,0:T(8,128)S(1)} %add_select_fusion.own) | copy-start | bytes 983044
  27.2 15.7 %collective-permute-start.3 = (f32[4,160,128]{2,1,0:T(8,128)S(1)}, f32[4,160,128]{2,1,0:T(8,128)S(1)}, u32[]{:S(2)}, u32[]{:S(2)}) collective-permute-start(f32[4,160,128]{2,1,0:T(8,128)S(1)} %add_select_fusion.own), channel_id=1, source_target_pairs={{0,2},{1,3},{2,4},{3,5},{4,6},{5,7},{6,8},{7,9},{8,10},{9,11},{10,... | collective-permute-start | bytes 983048 | tf_op jit(solution)/shard_map/ppermute | solution.py:750
  30.0 13.0 %collective-permute-start.4 = (f32[4,160,128]{2,1,0:T(8,128)S(1)}, f32[4,160,128]{2,1,0:T(8,128)S(1)}, u32[]{:S(2)}, u32[]{:S(2)}) collective-permute-start(f32[4,160,128]{2,1,0:T(8,128)S(1)} %add_select_fusion.own), channel_id=1, source_target_pairs={{2,0},{3,1},{4,2},{5,3},{6,4},{7,5},{8,6},{9,7},{10,8},{11,9},{12,... | collective-permute-start | bytes 983048 | tf_op jit(solution)/shard_map/ppermute | solution.py:750
  34.6 9.0 %collective-permute-start.5 = (f32[4,160,128]{2,1,0:T(8,128)S(1)}, f32[4,160,128]{2,1,0:T(8,128)S(1)}, u32[]{:S(2)}, u32[]{:S(2)}) collective-permute-start(f32[4,160,128]{2,1,0:T(8,128)S(1)} %add_select_fusion.own), channel_id=1, source_target_pairs={{0,1},{1,0},{2,3},{3,2},{4,5},{5,4},{6,7},{7,6},{8,9},{9,8},{10,11... | collective-permute-start | bytes 983048 | tf_op jit(solution)/shard_map/ppermute | solution.py:861
  42.9 2.2 %copy-start.8 = (f32[4,160,128]{2,1,0:T(8,128)}, f32[4,160,128]{2,1,0:T(8,128)S(1)}, u32[]{:S(2)}) copy-start(f32[4,160,128]{2,1,0:T(8,128)S(1)} %collective-permute-done.3.own_low) | copy-start | bytes 983044
  42.9 2.2 %copy-start.9 = (f32[4,160,128]{2,1,0:T(8,128)}, f32[4,160,128]{2,1,0:T(8,128)S(1)}, u32[]{:S(2)}) copy-start(f32[4,160,128]{2,1,0:T(8,128)S(1)} %collective-permute-done.4.own_high) | copy-start | bytes 983044
  43.0 1.7 %collective-permute-start.6 = (f32[4,160,128]{2,1,0:T(8,128)S(1)}, f32[4,160,128]{2,1,0:T(8,128)S(1)}, u32[]{:S(2)}, u32[]{:S(2)}) collective-permute-start(f32[4,160,128]{2,1,0:T(8,128)S(1)} %collective-permute-done.3.own_low), channel_id=1, source_target_pairs={{0,1},{1,0},{2,3},{3,2},{4,5},{5,4},{6,7},{7,6},{8,9},{9,8},{10,11... | collective-permute-start | bytes 983048 | tf_op jit(solution)/shard_map/ppermute | solution.py:862
  43.1 2.1 %collective-permute-start.7 = (f32[4,160,128]{2,1,0:T(8,128)S(1)}, f32[4,160,128]{2,1,0:T(8,128)S(1)}, u32[]{:S(2)}, u32[]{:S(2)}) collective-permute-start(f32[4,160,128]{2,1,0:T(8,128)S(1)} %collective-permute-done.4.own_high), channel_id=1, source_target_pairs={{0,1},{1,0},{2,3},{3,2},{4,5},{5,4},{6,7},{7,6},{8,9},{9,8},{10,11... | collective-permute-start | bytes 983048 | tf_op jit(solution)/shard_map/ppermute | solution.py:863
  43.6 1.6 %copy-start.4 = (f32[4,160,128]{2,1,0:T(8,128)}, f32[4,160,128]{2,1,0:T(8,128)S(1)}, u32[]{:S(2)}) copy-start(f32[4,160,128]{2,1,0:T(8,128)S(1)} %collective-permute-done.5.other) | copy-start | bytes 983044
  44.7 0.7 copy-start.5
  45.1 0.7 copy-start.6
  45.9 41.0 %copy-start.2 = (s32[4]{0:T(128)S(1)}, s32[4]{0:T(128)}, u32[]{:S(2)}) copy-start(s32[4]{0:T(128)} %codes.5) | copy-start | bytes 52
  70.4 2.1 %collective-permute-start.8 = (f32[4,4,40,256]{3,2,1,0:T(8,128)S(1)}, f32[4,4,40,256]{3,2,1,0:T(8,128)S(1)}, u32[]{:S(2)}, u32[]{:S(2)}) collective-permute-start(f32[4,4,40,256]{3,2,1,0:T(8,128)S(1)} %all_to_all.5.mine), channel_id=1, source_target_pairs={{0,1},{1,0},{2,3},{3,2},{4,5},{5,4},{6,7},{7,6},{8,9},{9,8},{10,11... | collective-permute-start | bytes 1966088 | tf_op jit(solution)/shard_map/ppermute | solution.py:903
  72.5 0.7 copy-start.1
  74.1 7.6 %collective-permute-start.10 = (f32[4,40,256]{2,1,0:T(8,128)S(1)}, f32[4,40,256]{2,1,0:T(8,128)S(1)}, u32[]{:S(2)}, u32[]{:S(2)}) collective-permute-start(f32[4,40,256]{2,1,0:T(8,128)S(1)} %get-tuple-element.54), channel_id=1, source_target_pairs={{2,0},{3,1},{4,2},{5,3},{6,4},{7,5},{8,6},{9,7},{10,8},{11,9},{12,... | collective-permute-start | bytes 491528 | tf_op jit(solution)/shard_map/ppermute | solution.py:750
  77.5 9.3 %collective-permute-start.9 = (f32[4,40,256]{2,1,0:T(8,128)S(1)}, f32[4,40,256]{2,1,0:T(8,128)S(1)}, u32[]{:S(2)}, u32[]{:S(2)}) collective-permute-start(f32[4,40,256]{2,1,0:T(8,128)S(1)} %get-tuple-element.52), channel_id=1, source_target_pairs={{0,2},{1,3},{2,4},{3,5},{4,6},{5,7},{6,8},{7,9},{8,10},{9,11},{10,... | collective-permute-start | bytes 491528 | tf_op jit(solution)/shard_map/ppermute | solution.py:750
  87.5 14.3 %copy-start = (f32[4,40,256]{2,1,0:T(8,128)}, f32[4,40,256]{2,1,0:T(8,128)S(1)}, u32[]{:S(2)}) copy-start(f32[4,40,256]{2,1,0:T(8,128)S(1)} %choose.1.part0) | copy-start | bytes 491524
  87.5 6.1 %collective-permute-start.11 = (f32[4,40,256]{2,1,0:T(8,128)S(1)}, f32[4,40,256]{2,1,0:T(8,128)S(1)}, u32[]{:S(2)}, u32[]{:S(2)}) collective-permute-start(f32[4,40,256]{2,1,0:T(8,128)S(1)} %choose.1.part0), channel_id=1, source_target_pairs={{32,0},{33,1},{34,2},{35,3},{36,4},{37,5},{38,6},{39,7},{40,8},{41... | collective-permute-start | bytes 491528 | tf_op jit(solution)/shard_map/ppermute | solution.py:923
  88.8 7.6 %collective-permute-start.12 = (f32[4,40,256]{2,1,0:T(8,128)S(1)}, f32[4,40,256]{2,1,0:T(8,128)S(1)}, u32[]{:S(2)}, u32[]{:S(2)}) collective-permute-start(f32[4,40,256]{2,1,0:T(8,128)S(1)} %choose.1.part0), channel_id=1, source_target_pairs={{64,0},{65,1},{66,2},{67,3},{68,4},{69,5},{70,6},{71,7},{72,8},{73... | collective-permute-start | bytes 491528 | tf_op jit(solution)/shard_map/ppermute | solution.py:923
  90.1 11.7 %collective-permute-start.13 = (f32[4,40,256]{2,1,0:T(8,128)S(1)}, f32[4,40,256]{2,1,0:T(8,128)S(1)}, u32[]{:S(2)}, u32[]{:S(2)}) collective-permute-start(f32[4,40,256]{2,1,0:T(8,128)S(1)} %choose.1.part0), channel_id=1, source_target_pairs={{96,0},{97,1},{98,2},{99,3},{100,4},{101,5},{102,6},{103,7},{104,8... | collective-permute-start | bytes 491528 | tf_op jit(solution)/shard_map/ppermute | solution.py:923
  93.6 8.3 %copy-start.10 = (f32[4,40,256]{2,1,0:T(8,128)}, f32[4,40,256]{2,1,0:T(8,128)S(1)}, u32[]{:S(2)}) copy-start(f32[4,40,256]{2,1,0:T(8,128)S(1)} %collective-permute-done.11.part1) | copy-start | bytes 491524
  96.4 5.4 %copy-start.11 = (f32[4,40,256]{2,1,0:T(8,128)}, f32[4,40,256]{2,1,0:T(8,128)S(1)}, u32[]{:S(2)}) copy-start(f32[4,40,256]{2,1,0:T(8,128)S(1)} %collective-permute-done.12.part2) | copy-start | bytes 491524
  101.8 0.7 copy-start.12
where the time goes:
time: 112 us; the launch traced here: 111 us
  Pallas kernels  42.4 us (38%)
  starting transfers between devices  22.4 us (20%)
  waiting for transfers between devices  21.5 us (19%)
  blocking collectives  21.5 us (19%)
  local copies, waits for them, and re-layouts  2.11 us (2%)
    all_to_all x1, blocking collectives, per_device(): mine = lax.all_to_all(payload, 'lev', 0, 0)  21.5 us
    pallas_call x2, Pallas kernels, early(): pl.pallas_call(functools.partial(early_kernel, base, len(carried) > 0), g...  19.6 us
    ppermute x4, starting transfers between devices, shifted(): lax.ppermute(block, axis, [(i - distance, i) for i in devices if i - dist...  12.7 us
    ppermute x3, waiting for transfers between devices, per_device(): lax.ppermute(quarter, 'lev', [(q, 0)])  10.4 us
    pallas_call x1, Pallas kernels, per_device(): pl.pallas_call(message_kernel, in_specs=[smem] * 4 + [in_vmem] + [hbm] *...  9.81 us
    pallas_call x1, Pallas kernels, per_device(): pl.pallas_call(finish_kernel, grid_spec=pltpu.PrefetchScalarGridSpec(num_...  8.49 us
    ppermute x4, waiting for transfers between devices, shifted(): lax.ppermute(block, axis, [(i - distance, i) for i in devices if i - dist...  7.42 us
    ppermute x3, starting transfers between devices, per_device(): spread_out = [lax.ppermute(message, 'lev', [(0, r)]) for r in (1, 3, 2)]  3.93 us
  transfers between devices with their start and end apart: 14, of which 8 were waited for; matrix products, arithmetic and copies ran while one was open for 0% of the time, Pallas kernels for 18%

commit v1 on v0

--- a/solution.py
+++ b/solution.py
@@ -61,10 +61,19 @@
     for g in range(4):
         up_layer[32 * g + line // 2, line] = 1
         up_layer[32 * g + 16 + line // 2, 64 + line] = 1
-    return sel_x, sel_yz, up_x, twice, window_z, center, layers, up_layer
-
-
-SEL_X, SEL_YZ, UP_X, TWICE, WINDOW_Z, CENTER, LAYERS, UP_LAYER = selection_tables()
+    fill = np.zeros((2, 256, 512), np.float32)
+    z_column = np.zeros((2, 128, 512), np.float32)
+    y_row = np.zeros((4, 128, 128), np.float32)
+    for g in range(4):
+        for z_half in range(2):
+            fill[z_half, place, a * 32 + 16 * z_half + b] = 1
+            z_column[z_half, 32 * g + 16 + i, i * 32 + 16 - z_half] = 1
+        for octant in range(4):
+            y_row[octant, 32 * g + i, 96 * (octant % 2) + 16 * (octant // 2) + i] = 1
+    return sel_x, sel_yz, up_x, twice, window_z, center, layers, up_layer, fill, z_column, y_row
+
+
+SEL_X, SEL_YZ, UP_X, TWICE, WINDOW_Z, CENTER, LAYERS, UP_LAYER, FILL, Z_COLUMN, Y_ROW = selection_tables()
 
 
 def table(values):
@@ -149,7 +158,7 @@
             coef[k, t] = kind[:, 128 * t : 128 * t + 128]
 
 
-def advance(cells, coef, reacted, rates, spread, store):
+def advance(cells, coef, reacted, rates, spread, store, layers=None, parts=None):
     lane = iota((8, 128), 1)
 
     def react(n, to):
@@ -158,6 +167,9 @@
         out = dot(rates[0], high) + dot(rates[1], high) + dot(rates[0], low)
         for h in range(2):
             to[:, h] = out[:, 128 * h : 128 * h + 128].reshape(8, 32, 128)
+        if layers is not None:
+            rows = layers[0, pl.ds(pl.multiple_of(256 * n, 256), 256), :]
+            parts[n] = dot(high, rows) + dot(low, rows)
 
     def add(t, term):
         for xt in range(4):
@@ -341,7 +353,7 @@
     base, again, octants, fine_octants, counts, spread_ref, reaction_smem, box, code, before, code_before, after,
     code_after, sel_x, sel_yz, layers, mean_x, couple, *refs,
 ):
-    states, register, edges, ends, average, cells, later, coef, now, then, rates = refs[5 * again :]
+    states, register, edges, ends, average, cells, later, coef, now, then, rates, parts = refs[5 * again :]
     i = pl.program_id(0)
     at = base + i
     coarse = lax.axis_index("lev") == 0
@@ -408,11 +420,10 @@
         @pl.when(jnp.logical_not(coarse))
         def _():
             spread = [spread_ref[s] * 2.0 for s in range(8)]
-            advance(cells, coef, (now, then), rates, spread, store_later)
-            advance(later, coef, (now, then), rates, spread, store)
-            edges[0, 0:256] = pick(box[0].reshape(256, 1024), layers[0])
-            middle = jnp.concatenate([later[:, t + 1, 8:40, :].reshape(256, 128) for t in range(8)], axis=1)
-            edges[0, 256:512] = pick(middle, layers[0])
+            advance(cells, coef, (now, then), rates, spread, store_later, layers, parts)
+            edges[0, 0:256] = parts[0] + parts[1] + parts[2] + parts[3]
+            advance(later, coef, (now, then), rates, spread, store, layers, parts)
+            edges[0, 256:512] = parts[0] + parts[1] + parts[2] + parts[3]
             edges[0, 512:544] = pick(f, layers[0])
             ends[0, 0:8] = box[0, :, 0, :]
             ends[0, 8:16] = box[0, :, 31, :]
@@ -427,7 +438,7 @@
     up_layer_all, twice_all, mean_x_all, mean_layer_all, couple_all, layers_all, layers_t_all, mean_layers_all,
     own, own_low, own_high, other, other_low, other_high, started, states, payload, codes, rates, messages, taken, coarse,
     first, code, edges, ends, average, up_x, up_layer, twice, mean_x, mean_layer, couple, layers, layers_t, mean_layers,
-    sems, fixed_sems,
+    rim, sems, fixed_sems,
 ):
     column = lax.axis_index("box")
     lists = [
@@ -464,7 +475,76 @@
     for copy in lists:
         copy.start()
 
+    def row_ends():
+        odd = (column & 1) == 1
+        wide = species_column(spread_ref, 1.0, 128)
+        ends_at = ((0, 0), (SLOTS - 1, 24))
+        loads = [pltpu.make_async_copy(own.at[pl.ds(0, 2)], rim.at[0], sems.at[0, 0])]
+        for p, (box, x) in enumerate(ends_at):
+            loads.append(pltpu.make_async_copy(words.at[box, pl.ds(x, 8)], code.at[p, pl.ds(0, 8)], sems.at[1, p]))
+            loads.append(pltpu.make_async_copy(states.at[box, :, pl.ds(x, 8)], first.at[p, :, pl.ds(0, 8)], sems.at[2, p]))
+        for p, (even_from, odd_from) in enumerate(((other_low, other), (other, other_high))):
+
+            @pl.when(odd)
+            def _():
+                pltpu.make_async_copy(odd_from.at[pl.ds(0, 2)], rim.at[1 + p], sems.at[3, p]).start()
+
+            @pl.when(jnp.logical_not(odd))
+            def _():
+                pltpu.make_async_copy(even_from.at[pl.ds(0, 2)], rim.at[1 + p], sems.at[3, p]).start()
+
+        for copy in loads:
+            copy.start()
+        for copy in loads:
+            copy.wait()
+        saves = []
+        for p, (box, x) in enumerate(ends_at):
+            pltpu.make_async_copy(other.at[pl.ds(0, 2)], rim.at[1 + p], sems.at[3, p]).wait()
+            at = 7 * p
+            f = code[p, at : at + 1, :].astype(F32) / LEVELS
+            scaling = COARSE_STEP / jnp.maximum(f, FLOOR)
+            for t in range(8):
+                part = slice(128 * t, 128 * t + 128)
+                here = 32 + (p * 8 + t) * 16
+                there = 32 + ((1 - p) * 8 + t) * 16
+                c = rim[0, here // 160, here % 160 : here % 160 + 8, :]
+                g = rim[1 + p, there // 160, there % 160 : there % 160 + 8, :]
+                g_f = rim[1 + p, there // 160, there % 160 + 8 : there % 160 + 9, :]
+                m = jnp.minimum(f[:, part], g_f)
+                if p == 0:
+                    gain = m * (ADVECT * g - wide * (c - g))
+                else:
+                    gain = -m * (ADVECT * c - wide * (g - c))
+                first[p, :, at, part] += scaling[:, part] * gain
+            saves.append(
+                pltpu.make_async_copy(first.at[p, :, pl.ds(0, 8)], states.at[box, :, pl.ds(x, 8)], sems.at[2, p])
+            )
+            saves[-1].start()
+        for copy in saves:
+            copy.wait()
+
+    pl.when(lax.axis_index("lev") == 0)(row_ends)
+
+    def fetch(n):
+        for copy in copies(n, None):
+            copy.start()
+        home = parents[n] // SLOTS
+        away = (home >> 1) - (column >> 1)
+        same = ((home - column) & 1) == 0
+        for source, is_same, step in (
+            (own_low, True, -1), (own, True, 0), (own_high, True, 1),
+            (other_low, False, -1), (other, False, 0), (other_high, False, 1),
+        ):
+
+            @pl.when((same == is_same) & (away == step))
+            def _():
+                message_copy(source, parents[n] % SLOTS, n).start()
+
     def one_slot(i, carry):
+        @pl.when(i + 1 < counts[0])
+        def _():
+            fetch(i + 1)
+
         for copy in copies(i, False):
             copy.wait()
         message_copy(own, 0, i).wait()
@@ -624,24 +704,7 @@
     def _():
         for copy in fixed:
             copy.start()
-        for n in range(SLOTS):
-
-            @pl.when(n < counts[0])
-            def _():
-                for copy in copies(n, None):
-                    copy.start()
-                home = parents[n] // SLOTS
-                away = (home >> 1) - (column >> 1)
-                same = ((home - column) & 1) == 0
-                for source, is_same, step in (
-                    (own_low, True, -1), (own, True, 0), (own_high, True, 1),
-                    (other_low, False, -1), (other, False, 0), (other_high, False, 1),
-                ):
-
-                    @pl.when((same == is_same) & (away == step))
-                    def _():
-                        message_copy(source, parents[n] % SLOTS, n).start()
-
+        fetch(0)
         set_rates(rates, reaction_smem, 0.5 * COARSE_STEP)
         for copy in fixed:
             copy.wait()
@@ -675,74 +738,64 @@
     for j in range(SLOTS):
         _, offset, _ = decode(codes[j])
         away = ((column + offset) >> 1) - (column >> 1)
-        chosen[j] = jnp.where(away < 0, from_low[j], jnp.where(away == 0, stay[j], from_high[j]))
+        chosen[0, j] = jnp.where(away < 0, from_low[j], jnp.where(away == 0, stay[j], from_high[j]))
 
 
 def finish_kernel(
-    octants, codes, spread_ref, updated, message, register, code_words, halo, other_low, other, other_high,
-    part0, part1, part2, part3, sel_x, sel_yz, states, chosen,
+    octants, codes, message, register, parts, fill, z_column, y_row, updated, states, window, beside, sems
 ):
-    i = pl.program_id(0)
-    column = lax.axis_index("box")
-    states[...] = updated[...]
+    def copies(i, out):
+        y_half = octants[i] % 2
+        pairs = (
+            (pl.ds(pl.multiple_of(512 * y_half, 512), 512), window.at[i]),
+            (pl.ds(pl.multiple_of(512 - 128 * y_half, 128), 128), beside.at[i]),
+        )
+        result = []
+        for n, (lanes, here) in enumerate(pairs):
+            there = states.at[i, :, :, lanes]
+            source, target = (here, there) if out else (there, here)
+            result.append(pltpu.make_async_copy(source, target, sems.at[i, n]))
+        return result
+
+    def one_box(i):
+        octant = octants[i]
+        z_half = octant // 2
+        inside = iota((1, 512), 1) % 32 // 16 == z_half
+        own_f = jnp.concatenate([message[i, 0:24, :], message[i, 24:48, :]], axis=1)
+        x_f = jnp.where(iota((16, 256), 0) < 8, own_f[16:17], own_f[17:18])
+        reg_x = jnp.concatenate([register[i, 0:16, :], register[i, 16:32, :]], axis=1)
+        fix_x = COARSE_STEP / jnp.maximum(x_f, FLOOR) * (parts[3, i, 8:24, :] - reg_x)
+        side_f = jnp.concatenate([message[i, 80:96, :]] * 2, axis=0)
+        sides = jnp.concatenate([parts[3, i, 24:40, 0:128], parts[3, i, 24:40, 128:256]], axis=0)
+        fix_sides = unpack_rows(COARSE_STEP / jnp.maximum(side_f, FLOOR) * (sides - register[i, 32:64, :]))
+        average = jnp.concatenate([parts[q, i] for q in range(3)] + [parts[3, i, 0:8, :]], axis=0)
+        planes = pick(fix_x, fill[z_half])
+        filled = pick(average, fill[z_half])
+        along = pick(fix_sides, z_column[z_half])
+        across = pick(fix_sides, y_row[octant])
+        for copy in copies(i, False):
+            copy.wait()
+        window[i, :, 7, :] += planes[0:8]
+        window[i, :, 24, :] += planes[8:16]
+        for s in range(8):
+            part = slice(16 * s, 16 * s + 16)
+            window[i, s, 8:24, :] = jnp.where(inside, filled[part], window[i, s, 8:24, :] + along[part])
+            beside[i, s, 8:24, :] += across[part]
+        for copy in copies(i, True):
+            copy.start()
+
+    def each(act):
+        for i in range(SLOTS):
+
+            @pl.when(codes[i] >= 0)
+            def _():
+                act(i)
 
     @pl.when(lax.axis_index("lev") == 0)
     def _():
-        wide = species_column(spread_ref, 1.0, 128)
-        odd = (column & 1) == 1
-
-        def end_plane(x, p, neighbour_p, neighbour):
-            f = code_words[0, x : x + 1, :].astype(F32) / LEVELS
-            scaling = COARSE_STEP / jnp.maximum(f, FLOOR)
-            for t in range(8):
-                part = slice(128 * t, 128 * t + 128)
-                base = 32 + (p * 8 + t) * 16
-                there = 32 + (neighbour_p * 8 + t) * 16
-                c = halo[base : base + 8, :]
-                g = neighbour(there, there + 8)
-                m = jnp.minimum(f[:, part], neighbour(there + 8, there + 9))
-                if p == 0:
-                    gain = m * (ADVECT * g - wide * (c - g))
-                else:
-                    gain = -m * (ADVECT * c - wide * (g - c))
-                states[0, :, x, part] += scaling[:, part] * gain
-
-        @pl.when(i == 0)
-        def _():
-            end_plane(0, 0, 1, lambda a, b: jnp.where(odd, other[a:b, :], other_low[a:b, :]))
-
-        @pl.when(i == SLOTS - 1)
-        def _():
-            end_plane(31, 1, 0, lambda a, b: jnp.where(odd, other_high[a:b, :], other[a:b, :]))
-
-        child = codes[i]
-
-        @pl.when(child >= 0)
-        def _():
-            for q, part in enumerate((part0, part1, part2, part3)):
-                chosen[40 * q : 40 * q + 40, :] = part[0]
-            octant = octants[i]
-            y_half = octant % 2
-            z_half = octant // 2
-            lane = iota((1, 1024), 1)
-            inside = (lane // 512 == y_half) & (lane % 32 // 16 == z_half)
-            own_f = jnp.concatenate([message[0, 0:24, :], message[0, 24:48, :]], axis=1)
-            half = iota((16, 256), 0) < 8
-            x_f = jnp.where(half, own_f[16:17], own_f[17:18])
-            reg_x = jnp.concatenate([register[0, 0:16, :], register[0, 16:32, :]], axis=1)
-            fix_x = COARSE_STEP / jnp.maximum(x_f, FLOOR) * (chosen[128:144, :] - reg_x)
-            side_f = jnp.concatenate([message[0, 80:96, :]] * 2, axis=0)
-            sides = jnp.concatenate([chosen[144:160, 0:128], chosen[144:160, 128:256]], axis=0)
-            fix_sides = COARSE_STEP / jnp.maximum(side_f, FLOOR) * (sides - register[0, 32:64, :])
-            planes = pick(fix_x, sel_x[0])
-            states[0, :, 7, :] += planes[0:8]
-            states[0, :, 24, :] += planes[8:16]
-            filled = pick(chosen[0:128, :], sel_x[0])
-            added = pick(unpack_rows(fix_sides), sel_yz[0])
-            for s in range(8):
-                part = slice(16 * s, 16 * s + 16)
-                here = states[0, s, 8:24, :]
-                states[0, s, 8:24, :] = jnp.where(inside, filled[part], here + added[part])
+        each(lambda i: [copy.start() for copy in copies(i, False)])
+        each(one_box)
+        each(lambda i: [copy.wait() for copy in copies(i, True)])
 
 
 def shifted(block, axis, distance):
@@ -838,6 +891,7 @@
                     pltpu.VMEM((8, 2, 32, 128), F32),
                     pltpu.VMEM((8, 2, 32, 128), F32),
                     pltpu.VMEM((2, 256, 256), BF16),
+                    pltpu.VMEM((4, 256, 128), F32),
                 ],
             ),
             out_shape=[shape((SLOTS,) + dims, F32) for dims in blocks],
@@ -885,6 +939,7 @@
             pltpu.VMEM((SLOTS, 128, 1024), BF16),
             pltpu.VMEM((SLOTS, 1024, 128), BF16),
             pltpu.VMEM((SLOTS, 128, 256), BF16),
+            pltpu.VMEM((3, 2, 160, 128), F32),
             pltpu.SemaphoreType.DMA((SLOTS, 10)),
             pltpu.SemaphoreType.DMA((9,)),
         ],
@@ -916,34 +971,26 @@
         choose_kernel,
         in_specs=[smem] + [in_vmem] * 3,
         out_specs=in_vmem,
-        out_shape=bundle,
+        out_shape=shape((4, SLOTS, 40, 256), F32),
         compiler_params=small,
         name="choose",
     )(coarse_child, from_low, stay, from_high)
-    quarters = [quarter] + [lax.ppermute(quarter, "lev", [(q, 0)]) for q in range(1, 4)]
-
-    back_x, back_yz = table(SEL_X.transpose(0, 2, 1)), table(SEL_YZ.transpose(0, 2, 1))
-    flat = [a.reshape(640, 128) for a in (other_low, other, other_high)]
+    parts = lax.all_to_all(quarter, "lev", 0, 0)
+
     return pl.pallas_call(
         finish_kernel,
-        grid_spec=pltpu.PrefetchScalarGridSpec(
-            num_scalar_prefetch=2,
-            grid=(SLOTS,),
-            in_specs=[smem, each((8, 32, 1024)), each((160, 128)), each((64, 128)), each((32, 1024))]
-            + [whole(halo)] * 4
-            + [each((40, 256))] * 4
-            + [pl.BlockSpec((1, 256, 1024), by_octant), pl.BlockSpec((1, 128, 1024), by_octant)],
-            out_specs=each((8, 32, 1024)),
-            scratch_shapes=[pltpu.VMEM((160, 256), F32)],
-        ),
+        in_specs=[smem] * 2 + [in_vmem] * 6 + [hbm],
+        out_specs=hbm,
+        scratch_shapes=[
+            pltpu.VMEM((SLOTS, 8, 32, 512), F32),
+            pltpu.VMEM((SLOTS, 8, 32, 128), F32),
+            pltpu.SemaphoreType.DMA((SLOTS, 2)),
+        ],
         out_shape=shape((SLOTS, 8, 32, 1024), F32),
-        input_output_aliases={3: 0},
-        compiler_params=vmem,
+        input_output_aliases={8: 0},
+        compiler_params=pltpu.CompilerParams(vmem_limit_bytes=24 * 1024 * 1024),
         name="finish",
-    )(
-        coarse_octant, coarse_child, diffusivity, states, message, register, cell_code, halo, *flat,
-        *quarters, back_x, back_yz,
-    )
+    )(coarse_octant, coarse_child, message, register, parts, table(FILL), table(Z_COLUMN), table(Y_ROW), states)
 
 
 def solution(mesh):

time: 112 us -> 105 us (0.938)
  the two profiles are of different devices: /device:TPU:3 before, /device:TPU:24 now
where the time goes in v1:
time: 105 us; the launch traced here: 104 us
  Pallas kernels  38 us (36%)
  blocking collectives  28.2 us (27%)
  starting transfers between devices  23.4 us (22%)
  waiting for transfers between devices  11.8 us (11%)
  local copies, waits for them, and re-layouts  1.48 us (1%)
  between operations  1.08 us (1%)
    pallas_call x2, Pallas kernels, early(): pl.pallas_call(functools.partial(early_kernel, base, len(carried) > 0), g...  19.3 us
    ppermute x4, starting transfers between devices, shifted(): lax.ppermute(block, axis, [(i - distance, i) for i in devices if i - dist...  18.6 us
    all_to_all x1, blocking collectives, per_device(): mine = lax.all_to_all(payload, 'lev', 0, 0)  15.5 us
    all_to_all x1, blocking collectives, per_device(): parts = lax.all_to_all(quarter, 'lev', 0, 0)  12.7 us
    pallas_call x1, Pallas kernels, per_device(): pl.pallas_call(message_kernel, in_specs=[smem] * 4 + [in_vmem] + [hbm] *...  9.71 us
    ppermute x4, waiting for transfers between devices, shifted(): lax.ppermute(block, axis, [(i - distance, i) for i in devices if i - dist...  8.04 us
    pallas_call x1, Pallas kernels, per_device(): pl.pallas_call(interface_kernel, in_specs=[smem] * 5 + [in_vmem] + [hbm]...  4.36 us
    ppermute x3, starting transfers between devices, per_device(): spread_out = [lax.ppermute(message, 'lev', [(0, r)]) for r in (1, 3, 2)]  3.93 us
  transfers between devices with their start and end apart: 11, of which 5 were waited for; matrix products, arithmetic and copies ran while one was open for 0% of the time, Pallas kernels for 19%

profile of v1, /device:TPU:24, one launch (start us, length us, event | category | flops | bytes accessed | tf_op | source)
XLA Modules:
  0.0 103.9 jit_solution(9390158588789298704)
XLA Ops:
  0.0 9.7 %shells.1 = (f32[4,160,128]{2,1,0:T(8,128)}, f32[640,128]{1,0:T(8,128)}) custom-call(s32[4]{0:T(128)} %octants.9, s32[4]{0:T(128)} %codes.5, f32[8]{0:T(128)} %spread_ref.7, f32[8,8]{1,0:T(8,128)} %reaction_ref.3, f32[8,8]{1,0:T(8,128)} %reaction_ref.3, f32[4,8,32,1024]{3,2,1,0:T(8,128)} %after.3, s32[4,32,1024]{2,1,0:T(8,128)} %words.3, ...), custom_call_target="tpu_custom_call" | custom-call | tf_op jit(solution)/shard_map/shells/pallas_call | solution.py:832
  9.7 1.3 %collective-permute-start.2 = (f32[4,160,128]{2,1,0:T(8,128)}, f32[4,160,128]{2,1,0:T(8,128)S(1)}, u32[]{:S(2)}, u32[]{:S(2)}) collective-permute-start(f32[4,160,128]{2,1,0:T(8,128)} %get-tuple-element.30.message), channel_id=1, source_target_pairs={{0,64},{1,65},{2,66},{3,67},{4,68},{5,69},{6,70},{7,71},{8,72},{9,... | collective-permute-start | bytes 983048 | tf_op jit(solution)/shard_map/ppermute | solution.py:908
  11.0 1.3 %collective-permute-start.1 = (f32[4,160,128]{2,1,0:T(8,128)}, f32[4,160,128]{2,1,0:T(8,128)S(1)}, u32[]{:S(2)}, u32[]{:S(2)}) collective-permute-start(f32[4,160,128]{2,1,0:T(8,128)} %get-tuple-element.30.message), channel_id=1, source_target_pairs={{0,96},{1,97},{2,98},{3,99},{4,100},{5,101},{6,102},{7,103},{8,104... | collective-permute-start | bytes 983048 | tf_op jit(solution)/shard_map/ppermute | solution.py:908
  12.4 1.3 %collective-permute-start = (f32[4,160,128]{2,1,0:T(8,128)}, f32[4,160,128]{2,1,0:T(8,128)S(1)}, u32[]{:S(2)}, u32[]{:S(2)}) collective-permute-start(f32[4,160,128]{2,1,0:T(8,128)} %get-tuple-element.30.message), channel_id=1, source_target_pairs={{0,32},{1,33},{2,34},{3,35},{4,36},{5,37},{6,38},{7,39},{8,40},{9,... | collective-permute-start | bytes 983048 | tf_op jit(solution)/shard_map/ppermute | solution.py:908
  14.3 0.0 copy-start.14
  14.3 12.7 %early_0.1 = (f32[4,8,32,1024]{3,2,1,0:T(8,128)}, f32[4,64,128]{2,1,0:T(8,128)}, f32[4,544,128]{2,1,0:T(8,128)}, f32[4,32,1024]{2,1,0:T(8,128)}, f32[4,128,256]{2,1,0:T(8,128)}) custom-call(s32[4]{0:T(128)} %octants.9, s32[4]{0:T(128)} %octants.8, s32[1]{0:T(128)S(6)} %copy.40.counts, f32[8]{0:T(128)} %spread_ref.7, f32[8,8]{1,0:T(8,128)} %reaction_ref.3, ...), custom_call_target="tpu_custom_call" | custom-call | flops 1000000000 | bytes 30000000 | tf_op jit(solution)/shard_map/early_0/pallas_call | solution.py:865
  27.0 0.0 collective-permute-done.2
  27.0 0.0 collective-permute-done.1
  27.1 0.0 collective-permute-done
  27.1 0.0 copy-done.14
  27.1 0.1 add_select_fusion.own
  27.2 0.0 copy-start.8
  27.2 2.3 %collective-permute-start.4 = (f32[4,160,128]{2,1,0:T(8,128)S(1)}, f32[4,160,128]{2,1,0:T(8,128)S(1)}, u32[]{:S(2)}, u32[]{:S(2)}) collective-permute-start(f32[4,160,128]{2,1,0:T(8,128)S(1)} %add_select_fusion.own), channel_id=1, source_target_pairs={{2,0},{3,1},{4,2},{5,3},{6,4},{7,5},{8,6},{9,7},{10,8},{11,9},{12,... | collective-permute-start | bytes 983048 | tf_op jit(solution)/shard_map/ppermute | solution.py:803
  29.4 5.7 %collective-permute-start.3 = (f32[4,160,128]{2,1,0:T(8,128)S(1)}, f32[4,160,128]{2,1,0:T(8,128)S(1)}, u32[]{:S(2)}, u32[]{:S(2)}) collective-permute-start(f32[4,160,128]{2,1,0:T(8,128)S(1)} %add_select_fusion.own), channel_id=1, source_target_pairs={{0,2},{1,3},{2,4},{3,5},{4,6},{5,7},{6,8},{7,9},{8,10},{9,11},{10,... | collective-permute-start | bytes 983048 | tf_op jit(solution)/shard_map/ppermute | solution.py:803
  35.1 0.1 collective-permute-start.5
  35.2 6.6 %early_3.1 = (f32[4,8,32,1024]{3,2,1,0:T(8,128)}, f32[4,64,128]{2,1,0:T(8,128)}, f32[4,544,128]{2,1,0:T(8,128)}, f32[4,32,1024]{2,1,0:T(8,128)}, f32[4,128,256]{2,1,0:T(8,128)}) custom-call(s32[4]{0:T(128)} %octants.9, s32[4]{0:T(128)} %octants.8, s32[1]{0:T(128)S(6)} %copy.40.counts, ...), custom_call_target="tpu_custom_call", output_to_operand_aliasing={{0}: (16, {}), {1}: (17, {}), {2}: (18, {}), {3}: (19, {}),... | custom-call | flops 1000000000 | bytes 30000000 | tf_op jit(solution)/shard_map/early_3/pallas_call | solution.py:865
  41.9 0.0 copy-done.8
  41.9 0.0 collective-permute-done.4.own_high
  41.9 0.0 copy-start.9
  41.9 0.0 collective-permute-done.3.own_low
  41.9 0.0 copy-start.10
  41.9 0.7 collective-permute-start.6
  42.6 0.1 collective-permute-start.7
  42.7 0.0 collective-permute-done.5.other
  42.7 1.2 %collective-permute-done.6.other_low = f32[4,160,128]{2,1,0:T(8,128)S(1)} collective-permute-done((f32[4,160,128]{2,1,0:T(8,128)S(1)}, f32[4,160,128]{2,1,0:T(8,128)S(1)}, u32[]{:S(2)}, u32[]{:S(2)}) %collective-permute-start.6) | collective-permute-done | bytes 327712 | tf_op jit(solution)/shard_map/ppermute | solution.py:916
  43.9 0.5 collective-permute-done.7.other_high
  44.4 0.0 copy-done.9
  44.4 0.0 copy-done.10
  44.4 0.0 copy-done.11
  44.4 0.3 copy-done.12
  44.6 0.5 copy-done.13
  45.1 4.4 %interfaces.1 = (f32[4,8,32,1024]{3,2,1,0:T(8,128)}, f32[4,4,40,256]{3,2,1,0:T(8,128)}, f32[3,8,128]{2,1,0:T(8,128)}) custom-call(s32[4]{0:T(128)} %parents.1, s32[4]{0:T(128)} %octants.8, s32[1]{0:T(128)S(6)} %copy.40.counts, f32[8]{0:T(128)} %spread_ref.7, f32[8,8]{1,0:T(8,128)} %reaction_ref.3, ...), custom_call_target="tpu_custom_call", output_to_operand_aliasing={{0}: (25, {})} | custom-call | tf_op jit(solution)/shard_map/interfaces/pallas_call | solution.py:922
  49.5 0.0 copy-start.1
  49.5 0.0 copy-start.2
  49.5 0.0 copy-start.3
  49.5 0.0 copy-start.4
  49.5 15.5 %all_to_all.10.mine = f32[4,4,40,256]{3,2,1,0:T(8,128)S(1)} all-to-all(f32[4,4,40,256]{3,2,1,0:T(8,128)} %get-tuple-element.50), channel_id=1, replica_groups=mesh['lev'=4,'box'=32] {'lev'}, dimensions={0} | all-to-all | bytes 1310720 | tf_op jit(solution)/shard_map/all_to_all | solution.py:957
  65.0 0.0 collective-permute-start.8
  65.0 2.1 %collective-permute-done.8.others = f32[4,4,40,256]{3,2,1,0:T(8,128)S(1)} collective-permute-done((f32[4,4,40,256]{3,2,1,0:T(8,128)S(1)}, f32[4,4,40,256]{3,2,1,0:T(8,128)S(1)}, u32[]{:S(2)}, u32[]{:S(2)}) %collective-permute-start.8) | collective-permute-done | bytes 655392 | tf_op jit(solution)/shard_map/ppermute | solution.py:958
  67.1 0.7 copy-done.5
  67.8 0.9 route.1
  68.7 8.7 %collective-permute-start.9 = (f32[4,40,256]{2,1,0:T(8,128)S(1)}, f32[4,40,256]{2,1,0:T(8,128)S(1)}, u32[]{:S(2)}, u32[]{:S(2)}) collective-permute-start(f32[4,40,256]{2,1,0:T(8,128)S(1)} %get-tuple-element.51), channel_id=1, source_target_pairs={{0,2},{1,3},{2,4},{3,5},{4,6},{5,7},{6,8},{7,9},{8,10},{9,11},{10,... | collective-permute-start | bytes 491528 | tf_op jit(solution)/shard_map/ppermute | solution.py:803
  77.4 1.9 %collective-permute-start.10 = (f32[4,40,256]{2,1,0:T(8,128)S(1)}, f32[4,40,256]{2,1,0:T(8,128)S(1)}, u32[]{:S(2)}, u32[]{:S(2)}) collective-permute-start(f32[4,40,256]{2,1,0:T(8,128)S(1)} %get-tuple-element.53), channel_id=1, source_target_pairs={{2,0},{3,1},{4,2},{5,3},{6,4},{7,5},{8,6},{9,7},{10,8},{11,9},{12,... | collective-permute-start | bytes 491528 | tf_op jit(solution)/shard_map/ppermute | solution.py:803
  79.3 1.8 %collective-permute-done.9.from_low = f32[4,40,256]{2,1,0:T(8,128)S(1)} collective-permute-done((f32[4,40,256]{2,1,0:T(8,128)S(1)}, f32[4,40,256]{2,1,0:T(8,128)S(1)}, u32[]{:S(2)}, u32[]{:S(2)}) %collective-permute-start.9) | collective-permute-done | bytes 163872 | tf_op jit(solution)/shard_map/ppermute | solution.py:803
  81.1 6.2 %collective-permute-done.10.from_high = f32[4,40,256]{2,1,0:T(8,128)S(1)} collective-permute-done((f32[4,40,256]{2,1,0:T(8,128)S(1)}, f32[4,40,256]{2,1,0:T(8,128)S(1)}, u32[]{:S(2)}, u32[]{:S(2)}) %collective-permute-start.10) | collective-permute-done | bytes 163872 | tf_op jit(solution)/shard_map/ppermute | solution.py:803
  87.4 0.6 choose.1
  87.9 12.7 %all_to_all.11.parts = f32[4,4,40,256]{3,2,1,0:T(8,128)S(1)} all-to-all(f32[4,4,40,256]{3,2,1,0:T(8,128)S(1)} %choose.1), channel_id=1, replica_groups=mesh['lev'=4,'box'=32] {'lev'}, dimensions={0} | all-to-all | bytes 1310720 | tf_op jit(solution)/shard_map/all_to_all | solution.py:978
  100.7 3.1 %finish.1 = f32[4,8,32,1024]{3,2,1,0:T(8,128)} custom-call(s32[4]{0:T(128)S(1)} %copy-done.6, s32[4]{0:T(128)S(1)} %copy-done.7, f32[4,160,128]{2,1,0:T(8,128)S(1)} %copy-done.2, f32[4,64,128]{2,1,0:T(8,128)S(1)} %copy-done, f32[4,4,40,256]{3,2,1,0:T(8,128)S(1)} %all_to_all.11.parts, ...), custom_call_target="tpu_custom_call", output_to_operand_aliasing={{}: (8, {})} | custom-call | tf_op jit(solution)/shard_map/finish/pallas_call | solution.py:980
  (14 shorter events, 0.0 us)
Async XLA Ops:
  9.7 17.3 %collective-permute-start.2 = (f32[4,160,128]{2,1,0:T(8,128)}, f32[4,160,128]{2,1,0:T(8,128)S(1)}, u32[]{:S(2)}, u32[]{:S(2)}) collective-permute-start(f32[4,160,128]{2,1,0:T(8,128)} %get-tuple-element.30.message), channel_id=1, source_target_pairs={{0,64},{1,65},{2,66},{3,67},{4,68},{5,69},{6,70},{7,71},{8,72},{9,... | collective-permute-start | bytes 983048 | tf_op jit(solution)/shard_map/ppermute | solution.py:908
  11.0 16.0 %collective-permute-start.1 = (f32[4,160,128]{2,1,0:T(8,128)}, f32[4,160,128]{2,1,0:T(8,128)S(1)}, u32[]{:S(2)}, u32[]{:S(2)}) collective-permute-start(f32[4,160,128]{2,1,0:T(8,128)} %get-tuple-element.30.message), channel_id=1, source_target_pairs={{0,96},{1,97},{2,98},{3,99},{4,100},{5,101},{6,102},{7,103},{8,104... | collective-permute-start | bytes 983048 | tf_op jit(solution)/shard_map/ppermute | solution.py:908
  12.4 14.7 %collective-permute-start = (f32[4,160,128]{2,1,0:T(8,128)}, f32[4,160,128]{2,1,0:T(8,128)S(1)}, u32[]{:S(2)}, u32[]{:S(2)}) collective-permute-start(f32[4,160,128]{2,1,0:T(8,128)} %get-tuple-element.30.message), channel_id=1, source_target_pairs={{0,32},{1,33},{2,34},{3,35},{4,36},{5,37},{6,38},{7,39},{8,40},{9,... | collective-permute-start | bytes 983048 | tf_op jit(solution)/shard_map/ppermute | solution.py:908
  14.3 12.7 %copy-start.14 = (f32[640,128]{1,0:T(8,128)S(1)}, f32[640,128]{1,0:T(8,128)}, u32[]{:S(2)}) copy-start(f32[640,128]{1,0:T(8,128)} %get-tuple-element.41) | copy-start | bytes 983044
  27.2 14.7 %copy-start.8 = (f32[4,160,128]{2,1,0:T(8,128)}, f32[4,160,128]{2,1,0:T(8,128)S(1)}, u32[]{:S(2)}) copy-start(f32[4,160,128]{2,1,0:T(8,128)S(1)} %add_select_fusion.own) | copy-start | bytes 983044
  27.2 14.7 %collective-permute-start.4 = (f32[4,160,128]{2,1,0:T(8,128)S(1)}, f32[4,160,128]{2,1,0:T(8,128)S(1)}, u32[]{:S(2)}, u32[]{:S(2)}) collective-permute-start(f32[4,160,128]{2,1,0:T(8,128)S(1)} %add_select_fusion.own), channel_id=1, source_target_pairs={{2,0},{3,1},{4,2},{5,3},{6,4},{7,5},{8,6},{9,7},{10,8},{11,9},{12,... | collective-permute-start | bytes 983048 | tf_op jit(solution)/shard_map/ppermute | solution.py:803
  29.4 12.5 %collective-permute-start.3 = (f32[4,160,128]{2,1,0:T(8,128)S(1)}, f32[4,160,128]{2,1,0:T(8,128)S(1)}, u32[]{:S(2)}, u32[]{:S(2)}) collective-permute-start(f32[4,160,128]{2,1,0:T(8,128)S(1)} %add_select_fusion.own), channel_id=1, source_target_pairs={{0,2},{1,3},{2,4},{3,5},{4,6},{5,7},{6,8},{7,9},{8,10},{9,11},{10,... | collective-permute-start | bytes 983048 | tf_op jit(solution)/shard_map/ppermute | solution.py:803
  35.1 7.6 %collective-permute-start.5 = (f32[4,160,128]{2,1,0:T(8,128)S(1)}, f32[4,160,128]{2,1,0:T(8,128)S(1)}, u32[]{:S(2)}, u32[]{:S(2)}) collective-permute-start(f32[4,160,128]{2,1,0:T(8,128)S(1)} %add_select_fusion.own), channel_id=1, source_target_pairs={{0,1},{1,0},{2,3},{3,2},{4,5},{5,4},{6,7},{7,6},{8,9},{9,8},{10,11... | collective-permute-start | bytes 983048 | tf_op jit(solution)/shard_map/ppermute | solution.py:915
  41.9 2.5 %copy-start.9 = (f32[4,160,128]{2,1,0:T(8,128)}, f32[4,160,128]{2,1,0:T(8,128)S(1)}, u32[]{:S(2)}) copy-start(f32[4,160,128]{2,1,0:T(8,128)S(1)} %collective-permute-done.4.own_high) | copy-start | bytes 983044
  41.9 2.5 %copy-start.10 = (f32[4,160,128]{2,1,0:T(8,128)}, f32[4,160,128]{2,1,0:T(8,128)S(1)}, u32[]{:S(2)}) copy-start(f32[4,160,128]{2,1,0:T(8,128)S(1)} %collective-permute-done.3.own_low) | copy-start | bytes 983044
  41.9 2.0 %collective-permute-start.6 = (f32[4,160,128]{2,1,0:T(8,128)S(1)}, f32[4,160,128]{2,1,0:T(8,128)S(1)}, u32[]{:S(2)}, u32[]{:S(2)}) collective-permute-start(f32[4,160,128]{2,1,0:T(8,128)S(1)} %collective-permute-done.3.own_low), channel_id=1, source_target_pairs={{0,1},{1,0},{2,3},{3,2},{4,5},{5,4},{6,7},{7,6},{8,9},{9,8},{10,11... | collective-permute-start | bytes 983048 | tf_op jit(solution)/shard_map/ppermute | solution.py:916
  42.6 1.7 %collective-permute-start.7 = (f32[4,160,128]{2,1,0:T(8,128)S(1)}, f32[4,160,128]{2,1,0:T(8,128)S(1)}, u32[]{:S(2)}, u32[]{:S(2)}) collective-permute-start(f32[4,160,128]{2,1,0:T(8,128)S(1)} %collective-permute-done.4.own_high), channel_id=1, source_target_pairs={{0,1},{1,0},{2,3},{3,2},{4,5},{5,4},{6,7},{7,6},{8,9},{9,8},{10,11... | collective-permute-start | bytes 983048 | tf_op jit(solution)/shard_map/ppermute | solution.py:917
  42.7 1.6 %copy-start.11 = (f32[4,160,128]{2,1,0:T(8,128)}, f32[4,160,128]{2,1,0:T(8,128)S(1)}, u32[]{:S(2)}) copy-start(f32[4,160,128]{2,1,0:T(8,128)S(1)} %collective-permute-done.5.other) | copy-start | bytes 983044
  43.9 0.7 copy-start.12
  44.4 0.7 copy-start.13
  45.1 42.3 %copy-start.7 = (s32[4]{0:T(128)S(1)}, s32[4]{0:T(128)}, u32[]{:S(2)}) copy-start(s32[4]{0:T(128)} %codes.5) | copy-start | bytes 52
  45.1 55.6 %copy-start.6 = (s32[4]{0:T(128)S(1)}, s32[4]{0:T(128)}, u32[]{:S(2)}) copy-start(s32[4]{0:T(128)} %octants.9) | copy-start | bytes 52
  49.5 51.2 %copy-start = (f32[4,64,128]{2,1,0:T(8,128)S(1)}, f32[4,64,128]{2,1,0:T(8,128)}, u32[]{:S(2)}) copy-start(f32[4,64,128]{2,1,0:T(8,128)} %get-tuple-element.37.register) | copy-start | bytes 393220
  49.5 51.2 %copy-start.1 = (bf16[2,256,512]{2,1,0:T(8,128)(2,1)S(1)}, bf16[2,256,512]{2,1,0:T(8,128)(2,1)}, u32[]{:S(2)}) copy-start(bf16[2,256,512]{2,1,0:T(8,128)(2,1)} %constant.53.clone.fill) | copy-start | bytes 1572868
  49.5 51.2 %copy-start.2 = (f32[4,160,128]{2,1,0:T(8,128)S(1)}, f32[4,160,128]{2,1,0:T(8,128)}, u32[]{:S(2)}) copy-start(f32[4,160,128]{2,1,0:T(8,128)} %get-tuple-element.30.message) | copy-start | bytes 983044
  49.5 51.2 %copy-start.3 = (bf16[2,128,512]{2,1,0:T(8,128)(2,1)S(1)}, bf16[2,128,512]{2,1,0:T(8,128)(2,1)}, u32[]{:S(2)}) copy-start(bf16[2,128,512]{2,1,0:T(8,128)(2,1)} %constant.54.clone.z_column) | copy-start | bytes 786436
  49.5 51.2 %copy-start.4 = (bf16[4,128,128]{2,1,0:T(8,128)(2,1)S(1)}, bf16[4,128,128]{2,1,0:T(8,128)(2,1)}, u32[]{:S(2)}) copy-start(bf16[4,128,128]{2,1,0:T(8,128)(2,1)} %constant.55.clone.y_row) | copy-start | bytes 393220
  65.0 2.1 %collective-permute-start.8 = (f32[4,4,40,256]{3,2,1,0:T(8,128)S(1)}, f32[4,4,40,256]{3,2,1,0:T(8,128)S(1)}, u32[]{:S(2)}, u32[]{:S(2)}) collective-permute-start(f32[4,4,40,256]{3,2,1,0:T(8,128)S(1)} %all_to_all.10.mine), channel_id=1, source_target_pairs={{0,1},{1,0},{2,3},{3,2},{4,5},{5,4},{6,7},{7,6},{8,9},{9,8},{10,11... | collective-permute-start | bytes 1966088 | tf_op jit(solution)/shard_map/ppermute | solution.py:958
  67.1 0.7 copy-start.5
  68.7 12.4 %collective-permute-start.9 = (f32[4,40,256]{2,1,0:T(8,128)S(1)}, f32[4,40,256]{2,1,0:T(8,128)S(1)}, u32[]{:S(2)}, u32[]{:S(2)}) collective-permute-start(f32[4,40,256]{2,1,0:T(8,128)S(1)} %get-tuple-element.51), channel_id=1, source_target_pairs={{0,2},{1,3},{2,4},{3,5},{4,6},{5,7},{6,8},{7,9},{8,10},{9,11},{10,... | collective-permute-start | bytes 491528 | tf_op jit(solution)/shard_map/ppermute | solution.py:803
  77.4 10.0 %collective-permute-start.10 = (f32[4,40,256]{2,1,0:T(8,128)S(1)}, f32[4,40,256]{2,1,0:T(8,128)S(1)}, u32[]{:S(2)}, u32[]{:S(2)}) collective-permute-start(f32[4,40,256]{2,1,0:T(8,128)S(1)} %get-tuple-element.53), channel_id=1, source_target_pairs={{2,0},{3,1},{4,2},{5,3},{6,4},{7,5},{8,6},{9,7},{10,8},{11,9},{12,... | collective-permute-start | bytes 491528 | tf_op jit(solution)/shard_map/ppermute | solution.py:803

commit v2 on v1

--- a/solution.py
+++ b/solution.py
@@ -211,8 +211,8 @@
 
 
 def message_kernel(
-    octants, codes, spread_ref, reaction_smem, reaction_ref, boxes, words, sel_x_all, window_z_all, center_all, message,
-    halo, rates, box_ref, code_ref, sel_x_ref, window_z_ref, center_ref, sems,
+    octants, codes, spread_ref, reaction_smem, reaction_ref, boxes, words, sel_x_all, window_z_all, center_all, messages,
+    halo_out, rates, box_ref, code_ref, sel_x_ref, window_z_ref, center_ref, message, halo, sems,
 ):
     def copies(i):
         octant = octants[i]
@@ -329,9 +329,8 @@
 
     @pl.when(lax.axis_index("lev") == 0)
     def _():
-        for i in range(SLOTS):
-            for copy in copies(i):
-                copy.start()
+        for copy in copies(0):
+            copy.start()
         set_rates(rates, reaction_smem, COARSE_STEP)
         where = iota((8, 128), 1)
         listed = jnp.zeros((8, 128), F32)
@@ -340,13 +339,27 @@
         halo[...] = jnp.zeros((640, 128), F32)
         halo[16:24, :] = listed
 
+        def result(i):
+            return pltpu.make_async_copy(message.at[i], messages.at[i], sems.at[i, 5])
+
         def each(i, carry):
+            @pl.when(i + 1 < SLOTS)
+            def _():
+                for copy in copies(i + 1):
+                    copy.start()
+
             for copy in copies(i):
                 copy.wait()
             one_message(i, listed)
+            result(i).start()
             return carry
 
         lax.fori_loop(0, SLOTS, each, 0)
+        last = pltpu.make_async_copy(halo, halo_out, sems.at[0, 0])
+        last.start()
+        for i in range(SLOTS):
+            result(i).wait()
+        last.wait()
 
 
 def early_kernel(
@@ -436,15 +449,16 @@
 def interface_kernel(
     parents, octants, counts, spread_ref, reaction_smem, reaction_ref, words, edges_all, ends_all, average_all, up_x_all,
     up_layer_all, twice_all, mean_x_all, mean_layer_all, couple_all, layers_all, layers_t_all, mean_layers_all,
-    own, own_low, own_high, other, other_low, other_high, started, states, payload, codes, rates, messages, taken, coarse,
+    own, near_a, near_b, other, other_a, other_b, started, states, payloads, codes, rates, messages, taken, coarse,
     first, code, edges, ends, average, up_x, up_layer, twice, mean_x, mean_layer, couple, layers, layers_t, mean_layers,
-    rim, sems, fixed_sems,
+    rim, payload, sems, fixed_sems,
 ):
     column = lax.axis_index("box")
     lists = [
         pltpu.make_async_copy(source.at[0, 16:24], codes.at[n], fixed_sems.at[n])
-        for n, source in enumerate((own_low, own, own_high))
+        for n, source in enumerate((near_a, own, near_b))
     ]
+    turn_step = 1 - 2 * ((column >> 1) & 1)
     fixed = [
         pltpu.make_async_copy(source, target, fixed_sems.at[3 + n])
         for n, (source, target) in enumerate((
@@ -469,8 +483,11 @@
     def message_copy(source, box, n):
         return pltpu.make_async_copy(source.at[box], messages.at[n], sems.at[n, 8])
 
-    def result_copy(n):
-        return pltpu.make_async_copy(first.at[n], states.at[n], sems.at[n, 9])
+    def result_copies(n):
+        return [
+            pltpu.make_async_copy(first.at[n], states.at[n], sems.at[n, 9]),
+            pltpu.make_async_copy(payload.at[:, n], payloads.at[:, n], sems.at[n, 10]),
+        ]
 
     for copy in lists:
         copy.start()
@@ -483,15 +500,16 @@
         for p, (box, x) in enumerate(ends_at):
             loads.append(pltpu.make_async_copy(words.at[box, pl.ds(x, 8)], code.at[p, pl.ds(0, 8)], sems.at[1, p]))
             loads.append(pltpu.make_async_copy(states.at[box, :, pl.ds(x, 8)], first.at[p, :, pl.ds(0, 8)], sems.at[2, p]))
-        for p, (even_from, odd_from) in enumerate(((other_low, other), (other, other_high))):
-
-            @pl.when(odd)
-            def _():
-                pltpu.make_async_copy(odd_from.at[pl.ds(0, 2)], rim.at[1 + p], sems.at[3, p]).start()
-
-            @pl.when(jnp.logical_not(odd))
-            def _():
-                pltpu.make_async_copy(even_from.at[pl.ds(0, 2)], rim.at[1 + p], sems.at[3, p]).start()
+        for p, step in enumerate((-1, 1)):
+            inside = odd if p == 0 else jnp.logical_not(odd)
+            for source, there in (
+                (other, inside), (other_a, jnp.logical_not(inside) & (turn_step == step)),
+                (other_b, jnp.logical_not(inside) & (turn_step != step)),
+            ):
+
+                @pl.when(there)
+                def _():
+                    pltpu.make_async_copy(source.at[pl.ds(0, 2)], rim.at[1 + p], sems.at[3, p]).start()
 
         for copy in loads:
             copy.start()
@@ -532,8 +550,8 @@
         away = (home >> 1) - (column >> 1)
         same = ((home - column) & 1) == 0
         for source, is_same, step in (
-            (own_low, True, -1), (own, True, 0), (own_high, True, 1),
-            (other_low, False, -1), (other, False, 0), (other_high, False, 1),
+            (near_a, True, turn_step), (own, True, 0), (near_b, True, -turn_step),
+            (other_a, False, turn_step), (other, False, 0), (other_b, False, -turn_step),
         ):
 
             @pl.when((same == is_same) & (away == step))
@@ -670,6 +688,11 @@
         row31 = end_high - scale_high * high_two + end_mixed[:, 1024:2048]
         row31 = row31 + wide * tangential(end_high, f[31:32], scale_high, scale_high * inner_high)
 
+        @pl.when(i == 0)
+        def _():
+            for copy in fixed[3:]:
+                copy.wait()
+
         x_parts = pick(
             jnp.concatenate([low_one + low_two, high_one + high_two, row0 + row1, row30 + row31], axis=0), mean_x[...]
         )
@@ -697,23 +720,25 @@
         first[i, :, 1, :] += row1
         first[i, :, 30, :] += row30
         first[i, :, 31, :] += row31
-        result_copy(i).start()
+        for copy in result_copies(i):
+            copy.start()
         return carry
 
     @pl.when(counts[0] > 0)
     def _():
+        fetch(0)
         for copy in fixed:
             copy.start()
-        fetch(0)
         set_rates(rates, reaction_smem, 0.5 * COARSE_STEP)
-        for copy in fixed:
+        for copy in fixed[:3]:
             copy.wait()
         lax.fori_loop(0, counts[0], one_slot, 0)
         for n in range(SLOTS):
 
             @pl.when(n < counts[0])
             def _():
-                result_copy(n).wait()
+                for copy in result_copies(n):
+                    copy.wait()
 
     for copy in lists:
         copy.wait()
@@ -724,21 +749,23 @@
     return safe // (OFFSETS * SLOTS) + 1, safe // SLOTS % OFFSETS - REACH, safe % SLOTS
 
 
-def route_kernel(codes, mine, others, to_low, stay, to_high):
+def route_kernel(codes, mine, others, to_a, stay, to_b):
     column = lax.axis_index("box")
-    for n, (step, target) in enumerate(((-1, to_low), (0, stay), (1, to_high))):
+    turn_step = 1 - 2 * ((column >> 1) & 1)
+    for n, (step, target) in enumerate(((turn_step, to_a), (0, stay), (-turn_step, to_b))):
         for j in range(SLOTS):
             row, offset, slot = decode(codes[n, 7, j].astype(jnp.int32))
             child = column + 2 * step + offset
             target[j] = jnp.where(((child - column) & 1) == 0, mine[row, slot], others[row, slot])
 
 
-def choose_kernel(codes, from_low, stay, from_high, chosen):
+def choose_kernel(codes, from_a, stay, from_b, chosen):
     column = lax.axis_index("box")
+    turn_step = 1 - 2 * ((column >> 1) & 1)
     for j in range(SLOTS):
         _, offset, _ = decode(codes[j])
         away = ((column + offset) >> 1) - (column >> 1)
-        chosen[0, j] = jnp.where(away < 0, from_low[j], jnp.where(away == 0, stay[j], from_high[j]))
+        chosen[0, j] = jnp.where(away == turn_step, from_a[j], jnp.where(away == 0, stay[j], from_b[j]))
 
 
 def finish_kernel(
@@ -798,17 +825,14 @@
         each(lambda i: [copy.wait() for copy in copies(i, True)])
 
 
-def shifted(block, axis, distance):
-    devices = range(lax.axis_size(axis))
-    return lax.ppermute(block, axis, [(i - distance, i) for i in devices if i - distance in devices])
-
-
 def per_device(
     box_states, cell_code, diffusivity, reaction, coarse_child, coarse_octant, fine_parent, fine_octant, fine_count
 ):
     row = lax.axis_index("lev")
     count = lax.axis_size("box")
     swap = [(i, i ^ 1) for i in range(count)]
+    round_a = [(i, i ^ 2) for i in range(count)]
+    round_b = [(i, ((i + 2) ^ 2) - 2) for i in range(2, count - 2)]
     vmem = pltpu.CompilerParams(vmem_limit_bytes=62 * 1024 * 1024)
     small = pltpu.CompilerParams(vmem_limit_bytes=8 * 1024 * 1024)
 
@@ -832,7 +856,7 @@
     message, halo = pl.pallas_call(
         message_kernel,
         in_specs=[smem] * 4 + [in_vmem] + [hbm] * 5,
-        out_specs=[in_vmem, in_vmem],
+        out_specs=[hbm, hbm],
         scratch_shapes=[
             pltpu.VMEM((2, 256, 256), BF16),
             pltpu.VMEM((SLOTS, 8, 32, 1024), F32),
@@ -840,7 +864,9 @@
             pltpu.VMEM((SLOTS, 1024, 256), BF16),
             pltpu.VMEM((SLOTS, 1024, 128), BF16),
             pltpu.VMEM((SLOTS, 256, 128), BF16),
-            pltpu.SemaphoreType.DMA((SLOTS, 5)),
+            pltpu.VMEM((SLOTS, 160, 128), F32),
+            pltpu.VMEM((640, 128), F32),
+            pltpu.SemaphoreType.DMA((SLOTS, 6)),
         ],
         out_shape=[shape((SLOTS, 160, 128), F32), shape((640, 128), F32)],
         compiler_params=vmem,
@@ -908,13 +934,13 @@
     spread_out = [lax.ppermute(message, "lev", [(0, r)]) for r in (1, 3, 2)]
     *spread_out, updated = lax.optimization_barrier((*spread_out, updated))
     own = jnp.where(row == 0, halo.reshape(SLOTS, 160, 128), spread_out[0] + spread_out[1] + spread_out[2])
-    own_low = shifted(own, "box", 2)
-    own_high = shifted(own, "box", -2)
+    near_a = lax.ppermute(own, "box", round_a)
+    near_b = lax.ppermute(own, "box", round_b)
     updated, register, *carried = early(3, 1, updated, *carried)
-    own_low, own_high, updated = lax.optimization_barrier((own_low, own_high, updated))
+    near_a, near_b, updated = lax.optimization_barrier((near_a, near_b, updated))
     other = lax.ppermute(own, "box", swap)
-    other_low = lax.ppermute(own_low, "box", swap)
-    other_high = lax.ppermute(own_high, "box", swap)
+    other_a = lax.ppermute(near_a, "box", swap)
+    other_b = lax.ppermute(near_b, "box", swap)
 
     up_x, up_layer, twice, mean_layer = table(UP_X), table(UP_LAYER), table(TWICE), table(0.25 * UP_LAYER.T)
     mean_layers = table(LAYERS @ (0.25 * UP_X.T))
@@ -922,7 +948,7 @@
     states, payload, codes = pl.pallas_call(
         interface_kernel,
         in_specs=[smem] * 5 + [in_vmem] + [hbm] * 20,
-        out_specs=[hbm, in_vmem, smem],
+        out_specs=[hbm, hbm, smem],
         scratch_shapes=[
             pltpu.VMEM((2, 256, 256), BF16),
             pltpu.VMEM((SLOTS, 160, 128), F32),
@@ -940,7 +966,8 @@
             pltpu.VMEM((SLOTS, 1024, 128), BF16),
             pltpu.VMEM((SLOTS, 128, 256), BF16),
             pltpu.VMEM((3, 2, 160, 128), F32),
-            pltpu.SemaphoreType.DMA((SLOTS, 10)),
+            pltpu.VMEM((4, SLOTS, 40, 256), F32),
+            pltpu.SemaphoreType.DMA((SLOTS, 11)),
             pltpu.SemaphoreType.DMA((9,)),
         ],
         out_shape=[
@@ -951,13 +978,13 @@
         name="interfaces",
     )(
         fine_parent, fine_octant, fine_count, diffusivity, reaction, reaction, cell_code, *carried, *constants, layers,
-        layers_t, mean_layers, own, own_low, own_high, other, other_low, other_high, updated,
+        layers_t, mean_layers, own, near_a, near_b, other, other_a, other_b, updated,
     )
 
     mine = lax.all_to_all(payload, "lev", 0, 0)
     others = lax.ppermute(mine, "box", swap)
     bundle = shape((SLOTS, 40, 256), F32)
-    to_low, stay, to_high = pl.pallas_call(
+    to_a, stay, to_b = pl.pallas_call(
         route_kernel,
         in_specs=[smem] + [in_vmem] * 2,
         out_specs=[in_vmem] * 3,
@@ -965,8 +992,8 @@
         compiler_params=small,
         name="route",
     )(codes, mine, others)
-    from_high = shifted(to_low, "box", -2)
-    from_low = shifted(to_high, "box", 2)
+    from_a = lax.ppermute(to_a, "box", round_a)
+    from_b = lax.ppermute(to_b, "box", round_b)
     quarter = pl.pallas_call(
         choose_kernel,
         in_specs=[smem] + [in_vmem] * 3,
@@ -974,7 +1001,7 @@
         out_shape=shape((4, SLOTS, 40, 256), F32),
         compiler_params=small,
         name="choose",
-    )(coarse_child, from_low, stay, from_high)
+    )(coarse_child, from_a, stay, from_b)
     parts = lax.all_to_all(quarter, "lev", 0, 0)
 
     return pl.pallas_call(

time: 105 us -> 99.9 us (0.951)
  the two profiles are of different devices: /device:TPU:24 before, /device:TPU:4 now
where the time goes in v2:
time: 99.9 us; the launch traced here: 98.1 us
  Pallas kernels  37.8 us (38%)
  blocking collectives  31.9 us (32%)
  waiting for transfers between devices  13.1 us (13%)
  starting transfers between devices  12.8 us (13%)
  local copies, waits for them, and re-layouts  1.48 us (1%)
  between operations  1.04 us (1%)
    pallas_call x2, Pallas kernels, early(): pl.pallas_call(functools.partial(early_kernel, base, len(carried) > 0), g...  19.3 us
    all_to_all x1, blocking collectives, per_device(): mine = lax.all_to_all(payload, 'lev', 0, 0)  18.6 us
    all_to_all x1, blocking collectives, per_device(): parts = lax.all_to_all(quarter, 'lev', 0, 0)  13.3 us
    pallas_call x1, Pallas kernels, per_device(): pl.pallas_call(message_kernel, in_specs=[smem] * 4 + [in_vmem] + [hbm] *...  9.19 us
    ppermute x1, starting transfers between devices, per_device(): near_b = lax.ppermute(own, 'box', round_b)  4.82 us
    pallas_call x1, Pallas kernels, per_device(): pl.pallas_call(interface_kernel, in_specs=[smem] * 5 + [in_vmem] + [hbm]...  4.25 us
    ppermute x1, waiting for transfers between devices, per_device(): from_b = lax.ppermute(to_b, 'box', round_b)  4.02 us
    ppermute x3, starting transfers between devices, per_device(): spread_out = [lax.ppermute(message, 'lev', [(0, r)]) for r in (1, 3, 2)]  3.93 us
  transfers between devices with their start and end apart: 11, of which 7 were waited for; matrix products, arithmetic and copies ran while one was open for 0% of the time, Pallas kernels for 20%

profile of v2, /device:TPU:4, one launch (start us, length us, event | category | flops | bytes accessed | tf_op | source)
XLA Modules:
  0.0 98.1 jit_solution(4365800881275383473)
XLA Ops:
  0.0 9.2 %shells.1 = (f32[4,160,128]{2,1,0:T(8,128)}, f32[640,128]{1,0:T(8,128)}) custom-call(s32[4]{0:T(128)} %octants.9, s32[4]{0:T(128)} %codes.5, f32[8]{0:T(128)} %spread_ref.7, f32[8,8]{1,0:T(8,128)} %reaction_ref.3, f32[8,8]{1,0:T(8,128)} %reaction_ref.3, f32[4,8,32,1024]{3,2,1,0:T(8,128)} %after.3, s32[4,32,1024]{2,1,0:T(8,128)} %words.3, ...), custom_call_target="tpu_custom_call" | custom-call | tf_op jit(solution)/shard_map/shells/pallas_call | solution.py:856
  9.2 1.3 %collective-permute-start.2 = (f32[4,160,128]{2,1,0:T(8,128)}, f32[4,160,128]{2,1,0:T(8,128)S(1)}, u32[]{:S(2)}, u32[]{:S(2)}) collective-permute-start(f32[4,160,128]{2,1,0:T(8,128)} %get-tuple-element.30.message), channel_id=1, source_target_pairs={{0,64},{1,65},{2,66},{3,67},{4,68},{5,69},{6,70},{7,71},{8,72},{9,... | collective-permute-start | bytes 983048 | tf_op jit(solution)/shard_map/ppermute | solution.py:934
  10.5 1.3 %collective-permute-start.1 = (f32[4,160,128]{2,1,0:T(8,128)}, f32[4,160,128]{2,1,0:T(8,128)S(1)}, u32[]{:S(2)}, u32[]{:S(2)}) collective-permute-start(f32[4,160,128]{2,1,0:T(8,128)} %get-tuple-element.30.message), channel_id=1, source_target_pairs={{0,96},{1,97},{2,98},{3,99},{4,100},{5,101},{6,102},{7,103},{8,104... | collective-permute-start | bytes 983048 | tf_op jit(solution)/shard_map/ppermute | solution.py:934
  11.8 1.3 %collective-permute-start = (f32[4,160,128]{2,1,0:T(8,128)}, f32[4,160,128]{2,1,0:T(8,128)S(1)}, u32[]{:S(2)}, u32[]{:S(2)}) collective-permute-start(f32[4,160,128]{2,1,0:T(8,128)} %get-tuple-element.30.message), channel_id=1, source_target_pairs={{0,32},{1,33},{2,34},{3,35},{4,36},{5,37},{6,38},{7,39},{8,40},{9,... | collective-permute-start | bytes 983048 | tf_op jit(solution)/shard_map/ppermute | solution.py:934
  13.8 0.0 copy-start.14
  13.8 12.7 %early_0.1 = (f32[4,8,32,1024]{3,2,1,0:T(8,128)}, f32[4,64,128]{2,1,0:T(8,128)}, f32[4,544,128]{2,1,0:T(8,128)}, f32[4,32,1024]{2,1,0:T(8,128)}, f32[4,128,256]{2,1,0:T(8,128)}) custom-call(s32[4]{0:T(128)} %octants.9, s32[4]{0:T(128)} %octants.8, s32[1]{0:T(128)S(6)} %copy.40.counts, f32[8]{0:T(128)} %spread_ref.7, f32[8,8]{1,0:T(8,128)} %reaction_ref.3, ...), custom_call_target="tpu_custom_call" | custom-call | flops 1000000000 | bytes 30000000 | tf_op jit(solution)/shard_map/early_0/pallas_call | solution.py:891
  26.5 0.0 collective-permute-done.2
  26.5 0.0 collective-permute-done.1
  26.5 0.0 collective-permute-done
  26.6 0.0 copy-done.14
  26.6 0.1 add_select_fusion.own
  26.6 0.0 copy-start.8
  26.6 4.8 %collective-permute-start.4 = (f32[4,160,128]{2,1,0:T(8,128)S(1)}, f32[4,160,128]{2,1,0:T(8,128)S(1)}, u32[]{:S(2)}, u32[]{:S(2)}) collective-permute-start(f32[4,160,128]{2,1,0:T(8,128)S(1)} %add_select_fusion.own), channel_id=1, source_target_pairs={{2,4},{3,5},{4,2},{5,3},{6,8},{7,9},{8,6},{9,7},{10,12},{11,13},{1... | collective-permute-start | bytes 983048 | tf_op jit(solution)/shard_map/ppermute | solution.py:938
  31.5 0.2 collective-permute-start.3
  31.7 0.0 collective-permute-start.5
  31.7 6.6 %early_3.1 = (f32[4,8,32,1024]{3,2,1,0:T(8,128)}, f32[4,64,128]{2,1,0:T(8,128)}, f32[4,544,128]{2,1,0:T(8,128)}, f32[4,32,1024]{2,1,0:T(8,128)}, f32[4,128,256]{2,1,0:T(8,128)}) custom-call(s32[4]{0:T(128)} %octants.9, s32[4]{0:T(128)} %octants.8, s32[1]{0:T(128)S(6)} %copy.40.counts, ...), custom_call_target="tpu_custom_call", output_to_operand_aliasing={{0}: (16, {}), {1}: (17, {}), {2}: (18, {}), {3}: (19, {}),... | custom-call | flops 1000000000 | bytes 30000000 | tf_op jit(solution)/shard_map/early_3/pallas_call | solution.py:891
  38.3 0.0 copy-done.8
  38.3 1.8 %collective-permute-done.4.near_b = f32[4,160,128]{2,1,0:T(8,128)S(1)} collective-permute-done((f32[4,160,128]{2,1,0:T(8,128)S(1)}, f32[4,160,128]{2,1,0:T(8,128)S(1)}, u32[]{:S(2)}, u32[]{:S(2)}) %collective-permute-start.4) | collective-permute-done | bytes 327712 | tf_op jit(solution)/shard_map/ppermute | solution.py:938
  40.1 0.6 collective-permute-done.3.near_a
  40.7 0.0 collective-permute-start.6
  40.7 0.5 collective-permute-start.7
  41.2 0.0 collective-permute-done.5.other
  41.2 1.1 %collective-permute-done.6.other_a = f32[4,160,128]{2,1,0:T(8,128)S(1)} collective-permute-done((f32[4,160,128]{2,1,0:T(8,128)S(1)}, f32[4,160,128]{2,1,0:T(8,128)S(1)}, u32[]{:S(2)}, u32[]{:S(2)}) %collective-permute-start.6) | collective-permute-done | bytes 327712 | tf_op jit(solution)/shard_map/ppermute | solution.py:942
  42.4 0.5 collective-permute-done.7.other_b
  42.8 0.0 copy-done.9
  42.8 0.0 copy-done.10
  42.8 0.0 copy-done.11
  42.8 0.3 copy-done.12
  43.1 0.5 copy-done.13
  43.6 4.3 %interfaces.1 = (f32[4,8,32,1024]{3,2,1,0:T(8,128)}, f32[4,4,40,256]{3,2,1,0:T(8,128)}, f32[3,8,128]{2,1,0:T(8,128)}) custom-call(s32[4]{0:T(128)} %parents.1, s32[4]{0:T(128)} %octants.8, s32[1]{0:T(128)S(6)} %copy.40.counts, f32[8]{0:T(128)} %spread_ref.7, f32[8,8]{1,0:T(8,128)} %reaction_ref.3, ...), custom_call_target="tpu_custom_call", output_to_operand_aliasing={{0}: (25, {})} | custom-call | tf_op jit(solution)/shard_map/interfaces/pallas_call | solution.py:948
  47.8 0.0 copy-start
  47.8 0.0 copy-start.1
  47.8 0.0 copy-start.2
  47.8 0.0 copy-start.3
  47.9 0.0 copy-start.4
  47.9 18.6 %all_to_all.10.mine = f32[4,4,40,256]{3,2,1,0:T(8,128)S(1)} all-to-all(f32[4,4,40,256]{3,2,1,0:T(8,128)} %get-tuple-element.50), channel_id=1, replica_groups=mesh['lev'=4,'box'=32] {'lev'}, dimensions={0} | all-to-all | bytes 1310720 | tf_op jit(solution)/shard_map/all_to_all | solution.py:984
  66.4 0.0 collective-permute-start.8
  66.4 2.1 %collective-permute-done.8.others = f32[4,4,40,256]{3,2,1,0:T(8,128)S(1)} collective-permute-done((f32[4,4,40,256]{3,2,1,0:T(8,128)S(1)}, f32[4,4,40,256]{3,2,1,0:T(8,128)S(1)}, u32[]{:S(2)}, u32[]{:S(2)}) %collective-permute-start.8) | collective-permute-done | bytes 655392 | tf_op jit(solution)/shard_map/ppermute | solution.py:985
  68.5 0.7 copy-done.5
  69.2 0.9 route.1
  70.1 0.1 collective-permute-start.9
  70.2 3.2 %collective-permute-start.10 = (f32[4,40,256]{2,1,0:T(8,128)S(1)}, f32[4,40,256]{2,1,0:T(8,128)S(1)}, u32[]{:S(2)}, u32[]{:S(2)}) collective-permute-start(f32[4,40,256]{2,1,0:T(8,128)S(1)} %get-tuple-element.53), channel_id=1, source_target_pairs={{2,4},{3,5},{4,2},{5,3},{6,8},{7,9},{8,6},{9,7},{10,12},{11,13},{1... | collective-permute-start | bytes 491528 | tf_op jit(solution)/shard_map/ppermute | solution.py:996
  73.5 3.0 %collective-permute-done.9.from_a = f32[4,40,256]{2,1,0:T(8,128)S(1)} collective-permute-done((f32[4,40,256]{2,1,0:T(8,128)S(1)}, f32[4,40,256]{2,1,0:T(8,128)S(1)}, u32[]{:S(2)}, u32[]{:S(2)}) %collective-permute-start.9) | collective-permute-done | bytes 163872 | tf_op jit(solution)/shard_map/ppermute | solution.py:995
  76.5 4.0 %collective-permute-done.10.from_b = f32[4,40,256]{2,1,0:T(8,128)S(1)} collective-permute-done((f32[4,40,256]{2,1,0:T(8,128)S(1)}, f32[4,40,256]{2,1,0:T(8,128)S(1)}, u32[]{:S(2)}, u32[]{:S(2)}) %collective-permute-start.10) | collective-permute-done | bytes 163872 | tf_op jit(solution)/shard_map/ppermute | solution.py:996
  80.5 0.6 choose.1
  81.1 13.3 %all_to_all.11.parts = f32[4,4,40,256]{3,2,1,0:T(8,128)S(1)} all-to-all(f32[4,4,40,256]{3,2,1,0:T(8,128)S(1)} %choose.1), channel_id=1, replica_groups=mesh['lev'=4,'box'=32] {'lev'}, dimensions={0} | all-to-all | bytes 1310720 | tf_op jit(solution)/shard_map/all_to_all | solution.py:1005
  94.4 0.0 copy-done.1
  94.4 3.5 %finish.1 = f32[4,8,32,1024]{3,2,1,0:T(8,128)} custom-call(s32[4]{0:T(128)S(1)} %copy-done.6, s32[4]{0:T(128)S(1)} %copy-done.7, f32[4,160,128]{2,1,0:T(8,128)S(1)} %copy-done.2, f32[4,64,128]{2,1,0:T(8,128)S(1)} %copy-done, f32[4,4,40,256]{3,2,1,0:T(8,128)S(1)} %all_to_all.11.parts, ...), custom_call_target="tpu_custom_call", output_to_operand_aliasing={{}: (8, {})} | custom-call | tf_op jit(solution)/shard_map/finish/pallas_call | solution.py:1007
  (14 shorter events, 0.0 us)
Async XLA Ops:
  9.2 17.3 %collective-permute-start.2 = (f32[4,160,128]{2,1,0:T(8,128)}, f32[4,160,128]{2,1,0:T(8,128)S(1)}, u32[]{:S(2)}, u32[]{:S(2)}) collective-permute-start(f32[4,160,128]{2,1,0:T(8,128)} %get-tuple-element.30.message), channel_id=1, source_target_pairs={{0,64},{1,65},{2,66},{3,67},{4,68},{5,69},{6,70},{7,71},{8,72},{9,... | collective-permute-start | bytes 983048 | tf_op jit(solution)/shard_map/ppermute | solution.py:934
  10.5 16.0 %collective-permute-start.1 = (f32[4,160,128]{2,1,0:T(8,128)}, f32[4,160,128]{2,1,0:T(8,128)S(1)}, u32[]{:S(2)}, u32[]{:S(2)}) collective-permute-start(f32[4,160,128]{2,1,0:T(8,128)} %get-tuple-element.30.message), channel_id=1, source_target_pairs={{0,96},{1,97},{2,98},{3,99},{4,100},{5,101},{6,102},{7,103},{8,104... | collective-permute-start | bytes 983048 | tf_op jit(solution)/shard_map/ppermute | solution.py:934
  11.8 14.7 %collective-permute-start = (f32[4,160,128]{2,1,0:T(8,128)}, f32[4,160,128]{2,1,0:T(8,128)S(1)}, u32[]{:S(2)}, u32[]{:S(2)}) collective-permute-start(f32[4,160,128]{2,1,0:T(8,128)} %get-tuple-element.30.message), channel_id=1, source_target_pairs={{0,32},{1,33},{2,34},{3,35},{4,36},{5,37},{6,38},{7,39},{8,40},{9,... | collective-permute-start | bytes 983048 | tf_op jit(solution)/shard_map/ppermute | solution.py:934
  13.8 12.7 %copy-start.14 = (f32[640,128]{1,0:T(8,128)S(1)}, f32[640,128]{1,0:T(8,128)}, u32[]{:S(2)}) copy-start(f32[640,128]{1,0:T(8,128)} %get-tuple-element.41) | copy-start | bytes 983044
  26.6 11.7 %copy-start.8 = (f32[4,160,128]{2,1,0:T(8,128)}, f32[4,160,128]{2,1,0:T(8,128)S(1)}, u32[]{:S(2)}) copy-start(f32[4,160,128]{2,1,0:T(8,128)S(1)} %add_select_fusion.own) | copy-start | bytes 983044
  26.6 13.5 %collective-permute-start.4 = (f32[4,160,128]{2,1,0:T(8,128)S(1)}, f32[4,160,128]{2,1,0:T(8,128)S(1)}, u32[]{:S(2)}, u32[]{:S(2)}) collective-permute-start(f32[4,160,128]{2,1,0:T(8,128)S(1)} %add_select_fusion.own), channel_id=1, source_target_pairs={{2,4},{3,5},{4,2},{5,3},{6,8},{7,9},{8,6},{9,7},{10,12},{11,13},{1... | collective-permute-start | bytes 983048 | tf_op jit(solution)/shard_map/ppermute | solution.py:938
  31.5 9.2 %collective-permute-start.3 = (f32[4,160,128]{2,1,0:T(8,128)S(1)}, f32[4,160,128]{2,1,0:T(8,128)S(1)}, u32[]{:S(2)}, u32[]{:S(2)}) collective-permute-start(f32[4,160,128]{2,1,0:T(8,128)S(1)} %add_select_fusion.own), channel_id=1, source_target_pairs={{0,2},{1,3},{2,0},{3,1},{4,6},{5,7},{6,4},{7,5},{8,10},{9,11},{10,... | collective-permute-start | bytes 983048 | tf_op jit(solution)/shard_map/ppermute | solution.py:937
  31.7 9.5 %collective-permute-start.5 = (f32[4,160,128]{2,1,0:T(8,128)S(1)}, f32[4,160,128]{2,1,0:T(8,128)S(1)}, u32[]{:S(2)}, u32[]{:S(2)}) collective-permute-start(f32[4,160,128]{2,1,0:T(8,128)S(1)} %add_select_fusion.own), channel_id=1, source_target_pairs={{0,1},{1,0},{2,3},{3,2},{4,5},{5,4},{6,7},{7,6},{8,9},{9,8},{10,11... | collective-permute-start | bytes 983048 | tf_op jit(solution)/shard_map/ppermute | solution.py:941
  40.1 2.7 %copy-start.9 = (f32[4,160,128]{2,1,0:T(8,128)}, f32[4,160,128]{2,1,0:T(8,128)S(1)}, u32[]{:S(2)}) copy-start(f32[4,160,128]{2,1,0:T(8,128)S(1)} %collective-permute-done.4.near_b) | copy-start | bytes 983044
  40.7 2.1 %copy-start.10 = (f32[4,160,128]{2,1,0:T(8,128)}, f32[4,160,128]{2,1,0:T(8,128)S(1)}, u32[]{:S(2)}) copy-start(f32[4,160,128]{2,1,0:T(8,128)S(1)} %collective-permute-done.3.near_a) | copy-start | bytes 983044
  40.7 1.6 %collective-permute-start.6 = (f32[4,160,128]{2,1,0:T(8,128)S(1)}, f32[4,160,128]{2,1,0:T(8,128)S(1)}, u32[]{:S(2)}, u32[]{:S(2)}) collective-permute-start(f32[4,160,128]{2,1,0:T(8,128)S(1)} %collective-permute-done.3.near_a), channel_id=1, source_target_pairs={{0,1},{1,0},{2,3},{3,2},{4,5},{5,4},{6,7},{7,6},{8,9},{9,8},{10,11... | collective-permute-start | bytes 983048 | tf_op jit(solution)/shard_map/ppermute | solution.py:942
  40.7 2.1 %collective-permute-start.7 = (f32[4,160,128]{2,1,0:T(8,128)S(1)}, f32[4,160,128]{2,1,0:T(8,128)S(1)}, u32[]{:S(2)}, u32[]{:S(2)}) collective-permute-start(f32[4,160,128]{2,1,0:T(8,128)S(1)} %collective-permute-done.4.near_b), channel_id=1, source_target_pairs={{0,1},{1,0},{2,3},{3,2},{4,5},{5,4},{6,7},{7,6},{8,9},{9,8},{10,11... | collective-permute-start | bytes 983048 | tf_op jit(solution)/shard_map/ppermute | solution.py:943
  41.2 1.6 %copy-start.11 = (f32[4,160,128]{2,1,0:T(8,128)}, f32[4,160,128]{2,1,0:T(8,128)S(1)}, u32[]{:S(2)}) copy-start(f32[4,160,128]{2,1,0:T(8,128)S(1)} %collective-permute-done.5.other) | copy-start | bytes 983044
  42.4 0.7 copy-start.12
  42.8 0.7 copy-start.13
  43.5 36.9 %copy-start.7 = (s32[4]{0:T(128)S(1)}, s32[4]{0:T(128)}, u32[]{:S(2)}) copy-start(s32[4]{0:T(128)} %codes.5) | copy-start | bytes 52
  43.6 50.9 %copy-start.6 = (s32[4]{0:T(128)S(1)}, s32[4]{0:T(128)}, u32[]{:S(2)}) copy-start(s32[4]{0:T(128)} %octants.9) | copy-start | bytes 52
  47.8 46.6 %copy-start = (f32[4,64,128]{2,1,0:T(8,128)S(1)}, f32[4,64,128]{2,1,0:T(8,128)}, u32[]{:S(2)}) copy-start(f32[4,64,128]{2,1,0:T(8,128)} %get-tuple-element.37.register) | copy-start | bytes 393220
  47.8 46.6 %copy-start.1 = (bf16[2,256,512]{2,1,0:T(8,128)(2,1)S(1)}, bf16[2,256,512]{2,1,0:T(8,128)(2,1)}, u32[]{:S(2)}) copy-start(bf16[2,256,512]{2,1,0:T(8,128)(2,1)} %constant.53.clone.fill) | copy-start | bytes 1572868
  47.8 46.6 %copy-start.2 = (f32[4,160,128]{2,1,0:T(8,128)S(1)}, f32[4,160,128]{2,1,0:T(8,128)}, u32[]{:S(2)}) copy-start(f32[4,160,128]{2,1,0:T(8,128)} %get-tuple-element.30.message) | copy-start | bytes 983044
  47.8 46.6 %copy-start.3 = (bf16[2,128,512]{2,1,0:T(8,128)(2,1)S(1)}, bf16[2,128,512]{2,1,0:T(8,128)(2,1)}, u32[]{:S(2)}) copy-start(bf16[2,128,512]{2,1,0:T(8,128)(2,1)} %constant.54.clone.z_column) | copy-start | bytes 786436
  47.9 46.6 %copy-start.4 = (bf16[4,128,128]{2,1,0:T(8,128)(2,1)S(1)}, bf16[4,128,128]{2,1,0:T(8,128)(2,1)}, u32[]{:S(2)}) copy-start(bf16[4,128,128]{2,1,0:T(8,128)(2,1)} %constant.55.clone.y_row) | copy-start | bytes 393220
  66.4 2.1 %collective-permute-start.8 = (f32[4,4,40,256]{3,2,1,0:T(8,128)S(1)}, f32[4,4,40,256]{3,2,1,0:T(8,128)S(1)}, u32[]{:S(2)}, u32[]{:S(2)}) collective-permute-start(f32[4,4,40,256]{3,2,1,0:T(8,128)S(1)} %all_to_all.10.mine), channel_id=1, source_target_pairs={{0,1},{1,0},{2,3},{3,2},{4,5},{5,4},{6,7},{7,6},{8,9},{9,8},{10,11... | collective-permute-start | bytes 1966088 | tf_op jit(solution)/shard_map/ppermute | solution.py:985
  68.5 0.7 copy-start.5
  70.1 6.3 %collective-permute-start.9 = (f32[4,40,256]{2,1,0:T(8,128)S(1)}, f32[4,40,256]{2,1,0:T(8,128)S(1)}, u32[]{:S(2)}, u32[]{:S(2)}) collective-permute-start(f32[4,40,256]{2,1,0:T(8,128)S(1)} %get-tuple-element.51), channel_id=1, source_target_pairs={{0,2},{1,3},{2,0},{3,1},{4,6},{5,7},{6,4},{7,5},{8,10},{9,11},{10,... | collective-permute-start | bytes 491528 | tf_op jit(solution)/shard_map/ppermute | solution.py:995
  70.2 10.2 %collective-permute-start.10 = (f32[4,40,256]{2,1,0:T(8,128)S(1)}, f32[4,40,256]{2,1,0:T(8,128)S(1)}, u32[]{:S(2)}, u32[]{:S(2)}) collective-permute-start(f32[4,40,256]{2,1,0:T(8,128)S(1)} %get-tuple-element.53), channel_id=1, source_target_pairs={{2,4},{3,5},{4,2},{5,3},{6,8},{7,9},{8,6},{9,7},{10,12},{11,13},{1... | collective-permute-start | bytes 491528 | tf_op jit(solution)/shard_map/ppermute | solution.py:996

commit v3 on v2

--- a/solution.py
+++ b/solution.py
@@ -303,19 +303,21 @@
         blank = jnp.zeros((8, 1024), F32)
         x_parts = pick(jnp.concatenate(planes + [faces] + new_planes + [blank], axis=0), sel_x_ref[i])
 
+        sublane = iota((8, 128), 0)
         message[i, 0:16, :] = x_parts[0:16, 0:128]
-        message[i, 16:24, :] = jnp.where(iota((8, 128), 0) == 7, listed, x_parts[16:24, 0:128])
-        message[i, 24:48, :] = x_parts[0:24, 128:256]
-        message[i, 48:80, :] = pack_rows(side_parts[0:128])
-        message[i, 80:96, :] = side_parts[256:272]
-        message[i, 96:112, :] = x_parts[24:40, 0:128]
-        message[i, 112:128, :] = x_parts[24:40, 128:256]
-        message[i, 128:160, :] = pack_rows(side_parts[128:256])
+        message[i, 16:32, :] = x_parts[0:16, 128:256]
+        message[i, 32:64, :] = pack_rows(side_parts[0:128])
+        face_f = jnp.where(sublane < 2, x_parts[16:24, 0:128], pltpu.roll(x_parts[16:24, 128:256], 2, 0))
+        message[i, 64:72, :] = jnp.where(sublane < 4, face_f, jnp.where(sublane == 7, listed, 0.0))
+        message[i, 72:80, :] = jnp.where(iota((8, 128), 1) < 64, side_parts[256:264], side_parts[264:272])
+        message[i, 80:96, :] = x_parts[24:40, 0:128]
+        message[i, 96:112, :] = x_parts[24:40, 128:256]
+        message[i, 112:144, :] = pack_rows(side_parts[128:256])
 
         def put_plane(p, x):
             plane = box[0, :, x, :]
             for t in range(8):
-                base = 32 + (p * 8 + t) * 16
+                base = 144 + (p * 8 + t) * 16
                 halo[base : base + 8, :] = plane[:, 128 * t : 128 * t + 128]
                 halo[base + 8 : base + 16, :] = jnp.broadcast_to(f[x : x + 1, 128 * t : 128 * t + 128], (8, 128))
 
@@ -336,8 +338,8 @@
         listed = jnp.zeros((8, 128), F32)
         for j in range(SLOTS):
             listed = jnp.where(where == j, codes[j].astype(F32), listed)
-        halo[...] = jnp.zeros((640, 128), F32)
-        halo[16:24, :] = listed
+        halo[...] = jnp.zeros((576, 128), F32)
+        halo[64:72, :] = listed
 
         def result(i):
             return pltpu.make_async_copy(message.at[i], messages.at[i], sems.at[i, 5])
@@ -363,14 +365,30 @@
 
 
 def early_kernel(
-    base, again, octants, fine_octants, counts, spread_ref, reaction_smem, box, code, before, code_before, after,
-    code_after, sel_x, sel_yz, layers, mean_x, couple, *refs,
+    base, again, octants, fine_octants, counts, spread_ref, reaction_smem, box, code, boxes, words,
+    sel_x_all, sel_yz_all, layers, mean_x, couple, *refs,
 ):
-    states, register, edges, ends, average, cells, later, coef, now, then, rates, parts = refs[5 * again :]
+    states, register, edges, ends, average, *refs = refs[5 * again :]
+    cells, later, coef, now, then, rates, parts, before, code_before, after, code_after, sel_x, sel_yz, sems = refs
     i = pl.program_id(0)
     at = base + i
     coarse = lax.axis_index("lev") == 0
     used = coarse | (at < counts[0])
+
+    def coarse_copies(first=0, last=6):
+        octant = octants[at]
+        previous, following = jnp.maximum(at - 1, 0), jnp.minimum(at + 1, SLOTS - 1)
+        pairs = (
+            (boxes.at[previous, :, pl.ds(24, 8)], before), (words.at[previous, pl.ds(24, 8)], code_before),
+            (boxes.at[following, :, pl.ds(0, 8)], after), (words.at[following, pl.ds(0, 8)], code_after),
+            (sel_x_all.at[octant], sel_x), (sel_yz_all.at[octant], sel_yz),
+        )
+        return [pltpu.make_async_copy(*pairs[n], sems.at[n]) for n in range(first, last)]
+
+    @pl.when(coarse)
+    def _():
+        for copy in coarse_copies():
+            copy.start()
 
     @pl.when(jnp.logical_not(used))
     def _():
@@ -385,13 +403,7 @@
             clear_rim(later)
 
         f = code[0].astype(F32) / LEVELS
-        f_before = jnp.where(coarse & (at > 0), code_before[0, 7:8, :].astype(F32) / LEVELS, 0.0)
-        f_after = jnp.where(coarse & (at < SLOTS - 1), code_after[0, 0:1, :].astype(F32) / LEVELS, 0.0)
         load_cells(cells, box[0])
-        for t in range(8):
-            cells[:, t + 1, 7, :] = before[0, :, 7, 128 * t : 128 * t + 128]
-            cells[:, t + 1, 40, :] = after[0, :, 0, 128 * t : 128 * t + 128]
-        prepare(f, f_before, f_after, coef, COARSE_STEP)
 
         def store(s, t, xt, value):
             states[0, s, 8 * xt : 8 * xt + 8, pl.ds(pl.multiple_of(128 * t, 128), 128)] = value
@@ -401,9 +413,17 @@
 
         @pl.when(coarse)
         def _():
+            octant = octants[at]
+            for copy in coarse_copies(0, 4):
+                copy.wait()
+            for t in range(8):
+                cells[:, t + 1, 7, :] = before[:, 7, 128 * t : 128 * t + 128]
+                cells[:, t + 1, 40, :] = after[:, 0, 128 * t : 128 * t + 128]
+            f_before = jnp.where(at > 0, code_before[7:8, :].astype(F32) / LEVELS, 0.0)
+            f_after = jnp.where(at < SLOTS - 1, code_after[0:1, :].astype(F32) / LEVELS, 0.0)
+            prepare(f, f_before, f_after, coef, COARSE_STEP)
             spread = [spread_ref[s] for s in range(8)]
             advance(cells, coef, (now, then), rates, spread, store)
-            octant = octants[at]
             y_half = octant % 2
             z_half = octant // 2
             wide = species_column(spread_ref, 1.0, 1024)
@@ -411,7 +431,9 @@
             c23, c24 = box[0, :, 23, :], box[0, :, 24, :]
             low_flux = -jnp.minimum(f[7:8], f[8:9]) * (ADVECT * c7 - wide * (c8 - c7))
             high_flux = jnp.minimum(f[23:24], f[24:25]) * (ADVECT * c23 - wide * (c24 - c23))
-            x_parts = pick(jnp.concatenate([low_flux, high_flux], axis=0), sel_x[0])
+            for copy in coarse_copies(4, 6):
+                copy.wait()
+            x_parts = pick(jnp.concatenate([low_flux, high_flux], axis=0), sel_x[...])
 
             lane = iota((1, 1024), 1)
             y_row = lane // 32 == 16 - y_half
@@ -425,13 +447,14 @@
                 c = box[0, s, 8:24, :]
                 inner = jnp.where(y_row, pltpu.roll(c, y_roll, 1), pltpu.roll(c, z_roll, 1))
                 fluxes.append(spread[s] * weight * (c - inner))
-            side_parts = pick(jnp.concatenate(fluxes, axis=0), sel_yz[0])
+            side_parts = pick(jnp.concatenate(fluxes, axis=0), sel_yz[...])
             register[0, 0:16, :] = x_parts[:, 0:128]
             register[0, 16:32, :] = x_parts[:, 128:256]
             register[0, 32:64, :] = pack_rows(side_parts)
 
         @pl.when(jnp.logical_not(coarse))
         def _():
+            prepare(f, 0.0, 0.0, coef, COARSE_STEP)
             spread = [spread_ref[s] * 2.0 for s in range(8)]
             advance(cells, coef, (now, then), rates, spread, store_later, layers, parts)
             edges[0, 0:256] = parts[0] + parts[1] + parts[2] + parts[3]
@@ -449,18 +472,14 @@
 def interface_kernel(
     parents, octants, counts, spread_ref, reaction_smem, reaction_ref, words, edges_all, ends_all, average_all, up_x_all,
     up_layer_all, twice_all, mean_x_all, mean_layer_all, couple_all, layers_all, layers_t_all, mean_layers_all,
-    own, near_a, near_b, other, other_a, other_b, started, states, payloads, codes, rates, messages, taken, coarse,
+    own, near_a, near_b, other, other_a, other_b, started, states, payloads, rates, messages, taken, coarse,
     first, code, edges, ends, average, up_x, up_layer, twice, mean_x, mean_layer, couple, layers, layers_t, mean_layers,
     rim, payload, sems, fixed_sems,
 ):
     column = lax.axis_index("box")
-    lists = [
-        pltpu.make_async_copy(source.at[0, 16:24], codes.at[n], fixed_sems.at[n])
-        for n, source in enumerate((near_a, own, near_b))
-    ]
     turn_step = 1 - 2 * ((column >> 1) & 1)
     fixed = [
-        pltpu.make_async_copy(source, target, fixed_sems.at[3 + n])
+        pltpu.make_async_copy(source, target, fixed_sems.at[n])
         for n, (source, target) in enumerate((
             (up_x_all, up_x), (up_layer_all, up_layer), (twice_all, twice), (mean_x_all, mean_x),
             (mean_layer_all, mean_layer), (couple_all, couple),
@@ -489,14 +508,11 @@
             pltpu.make_async_copy(payload.at[:, n], payloads.at[:, n], sems.at[n, 10]),
         ]
 
-    for copy in lists:
-        copy.start()
-
     def row_ends():
         odd = (column & 1) == 1
         wide = species_column(spread_ref, 1.0, 128)
         ends_at = ((0, 0), (SLOTS - 1, 24))
-        loads = [pltpu.make_async_copy(own.at[pl.ds(0, 2)], rim.at[0], sems.at[0, 0])]
+        loads = [pltpu.make_async_copy(own.at[pl.ds(1, 2)], rim.at[0], sems.at[0, 0])]
         for p, (box, x) in enumerate(ends_at):
             loads.append(pltpu.make_async_copy(words.at[box, pl.ds(x, 8)], code.at[p, pl.ds(0, 8)], sems.at[1, p]))
             loads.append(pltpu.make_async_copy(states.at[box, :, pl.ds(x, 8)], first.at[p, :, pl.ds(0, 8)], sems.at[2, p]))
@@ -509,7 +525,7 @@
 
                 @pl.when(there)
                 def _():
-                    pltpu.make_async_copy(source.at[pl.ds(0, 2)], rim.at[1 + p], sems.at[3, p]).start()
+                    pltpu.make_async_copy(source.at[pl.ds(1, 2)], rim.at[1 + p], sems.at[3, p]).start()
 
         for copy in loads:
             copy.start()
@@ -517,17 +533,17 @@
             copy.wait()
         saves = []
         for p, (box, x) in enumerate(ends_at):
-            pltpu.make_async_copy(other.at[pl.ds(0, 2)], rim.at[1 + p], sems.at[3, p]).wait()
+            pltpu.make_async_copy(other.at[pl.ds(1, 2)], rim.at[1 + p], sems.at[3, p]).wait()
             at = 7 * p
             f = code[p, at : at + 1, :].astype(F32) / LEVELS
             scaling = COARSE_STEP / jnp.maximum(f, FLOOR)
             for t in range(8):
                 part = slice(128 * t, 128 * t + 128)
-                here = 32 + (p * 8 + t) * 16
-                there = 32 + ((1 - p) * 8 + t) * 16
-                c = rim[0, here // 160, here % 160 : here % 160 + 8, :]
-                g = rim[1 + p, there // 160, there % 160 : there % 160 + 8, :]
-                g_f = rim[1 + p, there // 160, there % 160 + 8 : there % 160 + 9, :]
+                here = (p * 8 + t) * 16
+                there = ((1 - p) * 8 + t) * 16
+                c = rim[0, here // 144, here % 144 : here % 144 + 8, :]
+                g = rim[1 + p, there // 144, there % 144 : there % 144 + 8, :]
+                g_f = rim[1 + p, there // 144, there % 144 + 8 : there % 144 + 9, :]
                 m = jnp.minimum(f[:, part], g_f)
                 if p == 0:
                     gain = m * (ADVECT * g - wide * (c - g))
@@ -574,12 +590,12 @@
         wide = species_column(spread_ref, 2.0, 1024)
         f = code[i].astype(F32) / LEVELS
 
-        x_old = jnp.concatenate([chosen[0:24], chosen[24:48]], axis=1)
-        x_new = jnp.concatenate([chosen[96:112], chosen[112:128]], axis=1)
-        x_mid = 0.5 * (x_old[0:16] + x_new)
-        ghosts = pick(jnp.concatenate([x_old, x_mid, jnp.zeros((8, 256), F32)], axis=0), up_x[...])
-        side_old = chosen[48:80]
-        side_mid = 0.5 * (side_old + chosen[128:160])
+        x_old = jnp.concatenate([chosen[0:16], chosen[16:32]], axis=1)
+        x_new = jnp.concatenate([chosen[80:96], chosen[96:112]], axis=1)
+        face_f = jnp.concatenate([chosen[64:72], pltpu.roll(chosen[64:72], 6, 0)], axis=1)
+        ghosts = pick(jnp.concatenate([x_old, 0.5 * (x_old + x_new), face_f], axis=0), up_x[...])
+        side_old = chosen[32:64]
+        side_mid = 0.5 * (side_old + chosen[112:144])
 
         def side_ghosts(side):
             high, low = halves(unpack_rows(side))
@@ -589,7 +605,9 @@
 
         ghost_old = side_ghosts(side_old)
         ghost_mid = side_ghosts(side_mid)
-        high, low = halves(jnp.where(iota((16, 128), 1) < 32, chosen[80:96], 0.0))
+        group = iota((8, 128), 1) // 32
+        side_f = [jnp.where(group == g, chosen[72:80], 0.0) for g in (0, 2)]
+        high, low = halves(jnp.concatenate(side_f, axis=0))
         high = dot(twice[0:32, 0:16], high).astype(BF16)
         low = dot(twice[0:32, 0:16], low).astype(BF16)
         f_ghost = dot(high, up_layer[...]) + dot(low, up_layer[...])
@@ -619,7 +637,7 @@
             taken[s] = spread[s] * (scaling * q)
 
         long = iota((1, 1024), 1)
-        f_low, f_high = ghosts[16:17], ghosts[17:18]
+        f_low, f_high = ghosts[32:33], ghosts[33:34]
         m_low = jnp.minimum(f[0:1], f_low)
         m_high = jnp.minimum(f[31:32], f_high)
         scale_low = COARSE_STEP / jnp.maximum(f[0:1], FLOOR)
@@ -650,7 +668,7 @@
             c = c + jnp.where(row == 0, ends_there[s : s + 1], jnp.where(row == 31, ends_there[8 + s : 9 + s], 0.0))
             flux_two.append(through * (ghost_mid[part] - c))
         low_two, high_two = end_fluxes(
-            ghosts[24:32], ghosts[32:40], ends[i, 16:24] + end_low + crossed[0:8],
+            ghosts[16:24], ghosts[24:32], ends[i, 16:24] + end_low + crossed[0:8],
             ends[i, 24:32] + end_high + crossed[8:16],
         )
 
@@ -740,13 +758,20 @@
                 for copy in result_copies(n):
                     copy.wait()
 
-    for copy in lists:
-        copy.wait()
-
 
 def decode(code):
     safe = jnp.maximum(code, 0)
     return safe // (OFFSETS * SLOTS) + 1, safe // SLOTS % OFFSETS - REACH, safe % SLOTS
+
+
+def list_kernel(near_a, own, near_b, codes, sems):
+    copies = [
+        pltpu.make_async_copy(source.at[0, 64:72], codes.at[n], sems.at[n]) for n, source in enumerate((near_a, own, near_b))
+    ]
+    for copy in copies:
+        copy.start()
+    for copy in copies:
+        copy.wait()
 
 
 def route_kernel(codes, mine, others, to_a, stay, to_b):
@@ -788,11 +813,16 @@
         octant = octants[i]
         z_half = octant // 2
         inside = iota((1, 512), 1) % 32 // 16 == z_half
-        own_f = jnp.concatenate([message[i, 0:24, :], message[i, 24:48, :]], axis=1)
-        x_f = jnp.where(iota((16, 256), 0) < 8, own_f[16:17], own_f[17:18])
+        face_f = message[i, 64:72, :]
+        low_f = jnp.concatenate([face_f[0:1], face_f[2:3]], axis=1)
+        high_f = jnp.concatenate([face_f[1:2], face_f[3:4]], axis=1)
+        x_f = jnp.where(iota((16, 256), 0) < 8, low_f, high_f)
         reg_x = jnp.concatenate([register[i, 0:16, :], register[i, 16:32, :]], axis=1)
         fix_x = COARSE_STEP / jnp.maximum(x_f, FLOOR) * (parts[3, i, 8:24, :] - reg_x)
-        side_f = jnp.concatenate([message[i, 80:96, :]] * 2, axis=0)
+        near_f = message[i, 72:80, :]
+        far_f = pltpu.roll(near_f, 64, 1)
+        left = iota((8, 128), 1) < 64
+        side_f = jnp.concatenate([jnp.where(left, near_f, far_f), jnp.where(left, far_f, near_f)] * 2, axis=0)
         sides = jnp.concatenate([parts[3, i, 24:40, 0:128], parts[3, i, 24:40, 128:256]], axis=0)
         fix_sides = unpack_rows(COARSE_STEP / jnp.maximum(side_f, FLOOR) * (sides - register[i, 32:64, :]))
         average = jnp.concatenate([parts[q, i] for q in range(3)] + [parts[3, i, 0:8, :]], axis=0)
@@ -864,11 +894,11 @@
             pltpu.VMEM((SLOTS, 1024, 256), BF16),
             pltpu.VMEM((SLOTS, 1024, 128), BF16),
             pltpu.VMEM((SLOTS, 256, 128), BF16),
-            pltpu.VMEM((SLOTS, 160, 128), F32),
-            pltpu.VMEM((640, 128), F32),
+            pltpu.VMEM((SLOTS, 144, 128), F32),
+            pltpu.VMEM((576, 128), F32),
             pltpu.SemaphoreType.DMA((SLOTS, 6)),
         ],
-        out_shape=[shape((SLOTS, 160, 128), F32), shape((640, 128), F32)],
+        out_shape=[shape((SLOTS, 144, 128), F32), shape((576, 128), F32)],
         compiler_params=vmem,
         name="shells",
     )(
@@ -898,12 +928,10 @@
                     smem,
                     at((8, 32, 1024)),
                     at((32, 1024)),
-                    pl.BlockSpec((1, 8, 8, 1024), lambda i, *_: (previous(base + i), 0, 3, 0)),
-                    pl.BlockSpec((1, 8, 1024), lambda i, *_: (previous(base + i), 3, 0)),
-                    pl.BlockSpec((1, 8, 8, 1024), lambda i, *_: (following(base + i), 0, 0, 0)),
-                    pl.BlockSpec((1, 8, 1024), lambda i, *_: (following(base + i), 0, 0)),
-                    for_octant((1024, 256)),
-                    for_octant((1024, 128)),
+                    hbm,
+                    hbm,
+                    hbm,
+                    hbm,
                     pl.BlockSpec((1, 1024, 128), lambda i, octants, fine, *_: (fine[base + i], 0, 0)),
                     whole(mean_x),
                     whole(couple),
@@ -918,22 +946,29 @@
                     pltpu.VMEM((8, 2, 32, 128), F32),
                     pltpu.VMEM((2, 256, 256), BF16),
                     pltpu.VMEM((4, 256, 128), F32),
+                    pltpu.VMEM((8, 8, 1024), F32),
+                    pltpu.VMEM((8, 1024), jnp.int32),
+                    pltpu.VMEM((8, 8, 1024), F32),
+                    pltpu.VMEM((8, 1024), jnp.int32),
+                    pltpu.VMEM((1024, 256), BF16),
+                    pltpu.VMEM((1024, 128), BF16),
+                    pltpu.SemaphoreType.DMA((6,)),
                 ],
             ),
             out_shape=[shape((SLOTS,) + dims, F32) for dims in blocks],
-            input_output_aliases={16 + n: n for n in range(len(carried))},
+            input_output_aliases={14 + n: n for n in range(len(carried))},
             compiler_params=vmem,
             cost_estimate=pl.CostEstimate(flops=10**9, bytes_accessed=30 * 10**6, transcendentals=0),
             name=f"early_{base}",
         )(
             coarse_octant, fine_octant, fine_count, diffusivity, reaction, box_states, cell_code, box_states, cell_code,
-            box_states, cell_code, sel_x, sel_yz, layers_t, mean_x, couple, *carried,
+            sel_x, sel_yz, layers_t, mean_x, couple, *carried,
         )
 
     updated, *carried = early(0, 3)
     spread_out = [lax.ppermute(message, "lev", [(0, r)]) for r in (1, 3, 2)]
     *spread_out, updated = lax.optimization_barrier((*spread_out, updated))
-    own = jnp.where(row == 0, halo.reshape(SLOTS, 160, 128), spread_out[0] + spread_out[1] + spread_out[2])
+    own = jnp.where(row == 0, halo.reshape(SLOTS, 144, 128), spread_out[0] + spread_out[1] + spread_out[2])
     near_a = lax.ppermute(own, "box", round_a)
     near_b = lax.ppermute(own, "box", round_b)
     updated, register, *carried = early(3, 1, updated, *carried)
@@ -945,13 +980,13 @@
     up_x, up_layer, twice, mean_layer = table(UP_X), table(UP_LAYER), table(TWICE), table(0.25 * UP_LAYER.T)
     mean_layers = table(LAYERS @ (0.25 * UP_X.T))
     constants = [up_x, up_layer, twice, mean_x, mean_layer, couple]
-    states, payload, codes = pl.pallas_call(
+    states, payload = pl.pallas_call(
         interface_kernel,
         in_specs=[smem] * 5 + [in_vmem] + [hbm] * 20,
-        out_specs=[hbm, hbm, smem],
+        out_specs=[hbm, hbm],
         scratch_shapes=[
             pltpu.VMEM((2, 256, 256), BF16),
-            pltpu.VMEM((SLOTS, 160, 128), F32),
+            pltpu.VMEM((SLOTS, 144, 128), F32),
             pltpu.VMEM((8, 32, 128), F32),
             pltpu.VMEM((8, 16, 256), F32),
             pltpu.VMEM((SLOTS, 8, 32, 1024), F32),
@@ -965,14 +1000,12 @@
             pltpu.VMEM((SLOTS, 128, 1024), BF16),
             pltpu.VMEM((SLOTS, 1024, 128), BF16),
             pltpu.VMEM((SLOTS, 128, 256), BF16),
-            pltpu.VMEM((3, 2, 160, 128), F32),
+            pltpu.VMEM((3, 2, 144, 128), F32),
             pltpu.VMEM((4, SLOTS, 40, 256), F32),
             pltpu.SemaphoreType.DMA((SLOTS, 11)),
-            pltpu.SemaphoreType.DMA((9,)),
+            pltpu.SemaphoreType.DMA((6,)),
         ],
-        out_shape=[
-            shape((SLOTS, 8, 32, 1024), F32), shape((4, SLOTS, 40, 256), F32), shape((3, 8, 128), F32)
-        ],
+        out_shape=[shape((SLOTS, 8, 32, 1024), F32), shape((4, SLOTS, 40, 256), F32)],
         input_output_aliases={25: 0},
         compiler_params=vmem,
         name="interfaces",
@@ -983,6 +1016,16 @@
 
     mine = lax.all_to_all(payload, "lev", 0, 0)
     others = lax.ppermute(mine, "box", swap)
+    mine, near_a, own, near_b = lax.optimization_barrier((mine, near_a, own, near_b))
+    codes = pl.pallas_call(
+        list_kernel,
+        in_specs=[pl.BlockSpec(memory_space=pltpu.HBM)] * 3,
+        out_specs=pl.BlockSpec(memory_space=pltpu.HBM),
+        scratch_shapes=[pltpu.SemaphoreType.DMA((3,))],
+        out_shape=shape((3, 8, 128), F32),
+        compiler_params=small,
+        name="lists",
+    )(near_a, own, near_b)
     bundle = shape((SLOTS, 40, 256), F32)
     to_a, stay, to_b = pl.pallas_call(
         route_kernel,

time: 99.9 us -> 97.9 us (0.980)
  the two profiles are of different devices: /device:TPU:4 before, /device:TPU:6 now
where the time goes in v3:
time: 97.9 us; the launch traced here: 97.1 us
  Pallas kernels  41.1 us (42%)
  blocking collectives  28.1 us (29%)
  starting transfers between devices  14.2 us (15%)
  waiting for transfers between devices  9.95 us (10%)
  local copies, waits for them, and re-layouts  2.68 us (3%)
  between operations  1.08 us (1%)
    pallas_call x2, Pallas kernels, early(): pl.pallas_call(functools.partial(early_kernel, base, len(carried) > 0), g...  22.9 us
    all_to_all x1, blocking collectives, per_device(): mine = lax.all_to_all(payload, 'lev', 0, 0)  15.1 us
    all_to_all x1, blocking collectives, per_device(): parts = lax.all_to_all(quarter, 'lev', 0, 0)  13.1 us
    pallas_call x1, Pallas kernels, per_device(): pl.pallas_call(message_kernel, in_specs=[smem] * 4 + [in_vmem] + [hbm] *...  9.18 us
    ppermute x1, starting transfers between devices, per_device(): near_b = lax.ppermute(own, 'box', round_b)  5.18 us
    ppermute x1, waiting for transfers between devices, per_device(): from_b = lax.ppermute(to_b, 'box', round_b)  4.84 us
    pallas_call x1, Pallas kernels, per_device(): pl.pallas_call(finish_kernel, in_specs=[smem] * 2 + [in_vmem] * 6 + [hbm]...  3.99 us
    ppermute x3, starting transfers between devices, per_device(): spread_out = [lax.ppermute(message, 'lev', [(0, r)]) for r in (1, 3, 2)]  3.92 us
  transfers between devices with their start and end apart: 11, of which 7 were waited for; matrix products, arithmetic and copies ran while one was open for 0% of the time, Pallas kernels for 24%

profile of v3, /device:TPU:6, one launch (start us, length us, event | category | flops | bytes accessed | tf_op | source)
XLA Modules:
  0.0 97.1 jit_solution(16726109631430660883)
XLA Ops:
  0.0 9.2 %shells.1 = (f32[4,144,128]{2,1,0:T(8,128)}, f32[576,128]{1,0:T(8,128)}) custom-call(s32[4]{0:T(128)} %octants.9, s32[4]{0:T(128)} %codes.5, f32[8]{0:T(128)} %spread_ref.7, f32[8,8]{1,0:T(8,128)} %reaction_ref.3, f32[8,8]{1,0:T(8,128)} %reaction_ref.3, f32[4,8,32,1024]{3,2,1,0:T(8,128)} %boxes.5, s32[4,32,1024]{2,1,0:T(8,128)} %words.7, ...), custom_call_target="tpu_custom_call" | custom-call | tf_op jit(solution)/shard_map/shells/pallas_call | solution.py:886
  9.2 1.3 %collective-permute-start.2 = (f32[4,144,128]{2,1,0:T(8,128)}, f32[4,144,128]{2,1,0:T(8,128)S(1)}, u32[]{:S(2)}, u32[]{:S(2)}) collective-permute-start(f32[4,144,128]{2,1,0:T(8,128)} %get-tuple-element.33.message), channel_id=1, source_target_pairs={{0,64},{1,65},{2,66},{3,67},{4,68},{5,69},{6,70},{7,71},{8,72},{9,... | collective-permute-start | bytes 884744 | tf_op jit(solution)/shard_map/ppermute | solution.py:969
  10.5 1.3 %collective-permute-start.1 = (f32[4,144,128]{2,1,0:T(8,128)}, f32[4,144,128]{2,1,0:T(8,128)S(1)}, u32[]{:S(2)}, u32[]{:S(2)}) collective-permute-start(f32[4,144,128]{2,1,0:T(8,128)} %get-tuple-element.33.message), channel_id=1, source_target_pairs={{0,96},{1,97},{2,98},{3,99},{4,100},{5,101},{6,102},{7,103},{8,104... | collective-permute-start | bytes 884744 | tf_op jit(solution)/shard_map/ppermute | solution.py:969
  11.8 1.3 %collective-permute-start = (f32[4,144,128]{2,1,0:T(8,128)}, f32[4,144,128]{2,1,0:T(8,128)S(1)}, u32[]{:S(2)}, u32[]{:S(2)}) collective-permute-start(f32[4,144,128]{2,1,0:T(8,128)} %get-tuple-element.33.message), channel_id=1, source_target_pairs={{0,32},{1,33},{2,34},{3,35},{4,36},{5,37},{6,38},{7,39},{8,40},{9,... | collective-permute-start | bytes 884744 | tf_op jit(solution)/shard_map/ppermute | solution.py:969
  13.8 0.0 copy-start.16
  13.8 15.8 %early_0.1 = (f32[4,8,32,1024]{3,2,1,0:T(8,128)}, f32[4,64,128]{2,1,0:T(8,128)}, f32[4,544,128]{2,1,0:T(8,128)}, f32[4,32,1024]{2,1,0:T(8,128)}, f32[4,128,256]{2,1,0:T(8,128)}) custom-call(s32[4]{0:T(128)} %octants.9, s32[4]{0:T(128)} %octants.8, s32[1]{0:T(128)S(6)} %copy.40.counts, f32[8]{0:T(128)} %spread_ref.7, f32[8,8]{1,0:T(8,128)} %reaction_ref.3, ...), custom_call_target="tpu_custom_call" | custom-call | flops 1000000000 | bytes 30000000 | tf_op jit(solution)/shard_map/early_0/pallas_call | solution.py:921
  29.6 0.0 collective-permute-done.2
  29.6 0.0 collective-permute-done.1
  29.6 0.0 collective-permute-done
  29.6 0.0 copy-done.16
  29.7 0.1 add_select_fusion.own
  29.7 0.0 copy-start
  29.7 5.2 %collective-permute-start.4 = (f32[4,144,128]{2,1,0:T(8,128)S(1)}, f32[4,144,128]{2,1,0:T(8,128)S(1)}, u32[]{:S(2)}, u32[]{:S(2)}) collective-permute-start(f32[4,144,128]{2,1,0:T(8,128)S(1)} %add_select_fusion.own), channel_id=1, source_target_pairs={{2,4},{3,5},{4,2},{5,3},{6,8},{7,9},{8,6},{9,7},{10,12},{11,13},{1... | collective-permute-start | bytes 884744 | tf_op jit(solution)/shard_map/ppermute | solution.py:973
  34.9 0.1 collective-permute-start.3
  35.0 0.1 collective-permute-start.5
  35.1 7.1 %early_3.1 = (f32[4,8,32,1024]{3,2,1,0:T(8,128)}, f32[4,64,128]{2,1,0:T(8,128)}, f32[4,544,128]{2,1,0:T(8,128)}, f32[4,32,1024]{2,1,0:T(8,128)}, f32[4,128,256]{2,1,0:T(8,128)}) custom-call(s32[4]{0:T(128)} %octants.9, s32[4]{0:T(128)} %octants.8, s32[1]{0:T(128)S(6)} %copy.40.counts, ...), custom_call_target="tpu_custom_call", output_to_operand_aliasing={{0}: (14, {}), {1}: (15, {}), {2}: (16, {}), {3}: (17, {}),... | custom-call | flops 1000000000 | bytes 30000000 | tf_op jit(solution)/shard_map/early_3/pallas_call | solution.py:921
  42.2 0.0 copy-done
  42.2 0.3 collective-permute-done.4.near_b
  42.5 1.0 %collective-permute-done.3.near_a = f32[4,144,128]{2,1,0:T(8,128)S(1)} collective-permute-done((f32[4,144,128]{2,1,0:T(8,128)S(1)}, f32[4,144,128]{2,1,0:T(8,128)S(1)}, u32[]{:S(2)}, u32[]{:S(2)}) %collective-permute-start.3) | collective-permute-done | bytes 294944 | tf_op jit(solution)/shard_map/ppermute | solution.py:972
  43.5 0.0 collective-permute-start.6
  43.5 0.5 collective-permute-start.7
  44.0 0.0 collective-permute-done.5.other
  44.0 1.1 %collective-permute-done.6.other_a = f32[4,144,128]{2,1,0:T(8,128)S(1)} collective-permute-done((f32[4,144,128]{2,1,0:T(8,128)S(1)}, f32[4,144,128]{2,1,0:T(8,128)S(1)}, u32[]{:S(2)}, u32[]{:S(2)}) %collective-permute-start.6) | collective-permute-done | bytes 294944 | tf_op jit(solution)/shard_map/ppermute | solution.py:977
  45.1 0.4 collective-permute-done.7.other_b
  45.5 0.0 copy-done.2
  45.5 0.0 copy-done.4
  45.5 0.0 copy-done.13
  45.5 0.3 copy-done.14
  45.8 0.4 copy-done.15
  46.2 3.5 %interfaces.1 = (f32[4,8,32,1024]{3,2,1,0:T(8,128)}, f32[4,4,40,256]{3,2,1,0:T(8,128)}) custom-call(s32[4]{0:T(128)} %parents.1, s32[4]{0:T(128)} %octants.8, s32[1]{0:T(128)S(6)} %copy.40.counts, f32[8]{0:T(128)} %spread_ref.7, f32[8,8]{1,0:T(8,128)} %reaction_ref.3, f32[8,8]{1,0:T(8,128)} %reaction_ref.3, ...), custom_call_target="tpu_custom_call", output_to_operand_aliasing={{0}: (25, {})} | custom-call | tf_op jit(solution)/shard_map/interfaces/pallas_call | solution.py:983
  49.7 0.0 copy-start.7
  49.7 0.0 copy-start.9
  49.7 0.0 copy-start.11
  49.7 15.1 %all_to_all.10.mine = f32[4,4,40,256]{3,2,1,0:T(8,128)S(1)} all-to-all(f32[4,4,40,256]{3,2,1,0:T(8,128)} %get-tuple-element.52), channel_id=1, replica_groups=mesh['lev'=4,'box'=32] {'lev'}, dimensions={0} | all-to-all | bytes 1310720 | tf_op jit(solution)/shard_map/all_to_all | solution.py:1017
  64.8 0.0 collective-permute-start.8
  64.8 1.0 copy-done.3
  65.8 1.0 copy-done.5
  66.8 0.1 collective-permute-done.8.others
  66.9 0.9 route.1
  67.8 1.2 %collective-permute-start.9 = (f32[4,40,256]{2,1,0:T(8,128)S(1)}, f32[4,40,256]{2,1,0:T(8,128)S(1)}, u32[]{:S(2)}, u32[]{:S(2)}) collective-permute-start(f32[4,40,256]{2,1,0:T(8,128)S(1)} %get-tuple-element.57), channel_id=1, source_target_pairs={{0,2},{1,3},{2,0},{3,1},{4,6},{5,7},{6,4},{7,5},{8,10},{9,11},{10,... | collective-permute-start | bytes 491528 | tf_op jit(solution)/shard_map/ppermute | solution.py:1038
  69.0 3.2 %collective-permute-start.10 = (f32[4,40,256]{2,1,0:T(8,128)S(1)}, f32[4,40,256]{2,1,0:T(8,128)S(1)}, u32[]{:S(2)}, u32[]{:S(2)}) collective-permute-start(f32[4,40,256]{2,1,0:T(8,128)S(1)} %get-tuple-element.59), channel_id=1, source_target_pairs={{2,4},{3,5},{4,2},{5,3},{6,8},{7,9},{8,6},{9,7},{10,12},{11,13},{1... | collective-permute-start | bytes 491528 | tf_op jit(solution)/shard_map/ppermute | solution.py:1039
  72.2 2.2 %collective-permute-done.9.from_a = f32[4,40,256]{2,1,0:T(8,128)S(1)} collective-permute-done((f32[4,40,256]{2,1,0:T(8,128)S(1)}, f32[4,40,256]{2,1,0:T(8,128)S(1)}, u32[]{:S(2)}, u32[]{:S(2)}) %collective-permute-start.9) | collective-permute-done | bytes 163872 | tf_op jit(solution)/shard_map/ppermute | solution.py:1038
  74.4 4.8 %collective-permute-done.10.from_b = f32[4,40,256]{2,1,0:T(8,128)S(1)} collective-permute-done((f32[4,40,256]{2,1,0:T(8,128)S(1)}, f32[4,40,256]{2,1,0:T(8,128)S(1)}, u32[]{:S(2)}, u32[]{:S(2)}) %collective-permute-start.10) | collective-permute-done | bytes 163872 | tf_op jit(solution)/shard_map/ppermute | solution.py:1039
  79.2 0.0 copy-done.12
  79.3 0.6 choose.1
  79.8 13.1 %all_to_all.11.parts = f32[4,4,40,256]{3,2,1,0:T(8,128)S(1)} all-to-all(f32[4,4,40,256]{3,2,1,0:T(8,128)S(1)} %choose.1), channel_id=1, replica_groups=mesh['lev'=4,'box'=32] {'lev'}, dimensions={0} | all-to-all | bytes 1310720 | tf_op jit(solution)/shard_map/all_to_all | solution.py:1048
  92.9 0.0 copy-done.6
  92.9 4.0 %finish.1 = f32[4,8,32,1024]{3,2,1,0:T(8,128)} custom-call(s32[4]{0:T(128)S(1)} %copy-done.11, s32[4]{0:T(128)S(1)} %copy-done.12, f32[4,144,128]{2,1,0:T(8,128)S(1)} %copy-done.8, f32[4,64,128]{2,1,0:T(8,128)S(1)} %copy-done.6, f32[4,4,40,256]{3,2,1,0:T(8,128)S(1)} %all_to_all.11.parts, ...), custom_call_target="tpu_custom_call", output_to_operand_aliasing={{}: (8, {})} | custom-call | tf_op jit(solution)/shard_map/finish/pallas_call | solution.py:1050
  (19 shorter events, 0.1 us)
Async XLA Ops:
  9.2 20.4 %collective-permute-start.2 = (f32[4,144,128]{2,1,0:T(8,128)}, f32[4,144,128]{2,1,0:T(8,128)S(1)}, u32[]{:S(2)}, u32[]{:S(2)}) collective-permute-start(f32[4,144,128]{2,1,0:T(8,128)} %get-tuple-element.33.message), channel_id=1, source_target_pairs={{0,64},{1,65},{2,66},{3,67},{4,68},{5,69},{6,70},{7,71},{8,72},{9,... | collective-permute-start | bytes 884744 | tf_op jit(solution)/shard_map/ppermute | solution.py:969
  10.5 19.1 %collective-permute-start.1 = (f32[4,144,128]{2,1,0:T(8,128)}, f32[4,144,128]{2,1,0:T(8,128)S(1)}, u32[]{:S(2)}, u32[]{:S(2)}) collective-permute-start(f32[4,144,128]{2,1,0:T(8,128)} %get-tuple-element.33.message), channel_id=1, source_target_pairs={{0,96},{1,97},{2,98},{3,99},{4,100},{5,101},{6,102},{7,103},{8,104... | collective-permute-start | bytes 884744 | tf_op jit(solution)/shard_map/ppermute | solution.py:969
  11.8 17.8 %collective-permute-start = (f32[4,144,128]{2,1,0:T(8,128)}, f32[4,144,128]{2,1,0:T(8,128)S(1)}, u32[]{:S(2)}, u32[]{:S(2)}) collective-permute-start(f32[4,144,128]{2,1,0:T(8,128)} %get-tuple-element.33.message), channel_id=1, source_target_pairs={{0,32},{1,33},{2,34},{3,35},{4,36},{5,37},{6,38},{7,39},{8,40},{9,... | collective-permute-start | bytes 884744 | tf_op jit(solution)/shard_map/ppermute | solution.py:969
  13.8 15.9 %copy-start.16 = (f32[576,128]{1,0:T(8,128)S(1)}, f32[576,128]{1,0:T(8,128)}, u32[]{:S(2)}) copy-start(f32[576,128]{1,0:T(8,128)} %get-tuple-element.44) | copy-start | bytes 884740
  29.7 12.5 %copy-start = (f32[4,144,128]{2,1,0:T(8,128)}, f32[4,144,128]{2,1,0:T(8,128)S(1)}, u32[]{:S(2)}) copy-start(f32[4,144,128]{2,1,0:T(8,128)S(1)} %add_select_fusion.own) | copy-start | bytes 884740
  29.7 12.8 %collective-permute-start.4 = (f32[4,144,128]{2,1,0:T(8,128)S(1)}, f32[4,144,128]{2,1,0:T(8,128)S(1)}, u32[]{:S(2)}, u32[]{:S(2)}) collective-permute-start(f32[4,144,128]{2,1,0:T(8,128)S(1)} %add_select_fusion.own), channel_id=1, source_target_pairs={{2,4},{3,5},{4,2},{5,3},{6,8},{7,9},{8,6},{9,7},{10,12},{11,13},{1... | collective-permute-start | bytes 884744 | tf_op jit(solution)/shard_map/ppermute | solution.py:973
  34.9 8.5 %collective-permute-start.3 = (f32[4,144,128]{2,1,0:T(8,128)S(1)}, f32[4,144,128]{2,1,0:T(8,128)S(1)}, u32[]{:S(2)}, u32[]{:S(2)}) collective-permute-start(f32[4,144,128]{2,1,0:T(8,128)S(1)} %add_select_fusion.own), channel_id=1, source_target_pairs={{0,2},{1,3},{2,0},{3,1},{4,6},{5,7},{6,4},{7,5},{8,10},{9,11},{10,... | collective-permute-start | bytes 884744 | tf_op jit(solution)/shard_map/ppermute | solution.py:972
  35.0 9.0 %collective-permute-start.5 = (f32[4,144,128]{2,1,0:T(8,128)S(1)}, f32[4,144,128]{2,1,0:T(8,128)S(1)}, u32[]{:S(2)}, u32[]{:S(2)}) collective-permute-start(f32[4,144,128]{2,1,0:T(8,128)S(1)} %add_select_fusion.own), channel_id=1, source_target_pairs={{0,1},{1,0},{2,3},{3,2},{4,5},{5,4},{6,7},{7,6},{8,9},{9,8},{10,11... | collective-permute-start | bytes 884744 | tf_op jit(solution)/shard_map/ppermute | solution.py:976
  42.5 3.0 %copy-start.2 = (f32[4,144,128]{2,1,0:T(8,128)}, f32[4,144,128]{2,1,0:T(8,128)S(1)}, u32[]{:S(2)}) copy-start(f32[4,144,128]{2,1,0:T(8,128)S(1)} %collective-permute-done.4.near_b) | copy-start | bytes 884740
  43.5 2.0 %copy-start.4 = (f32[4,144,128]{2,1,0:T(8,128)}, f32[4,144,128]{2,1,0:T(8,128)S(1)}, u32[]{:S(2)}) copy-start(f32[4,144,128]{2,1,0:T(8,128)S(1)} %collective-permute-done.3.near_a) | copy-start | bytes 884740
  43.5 1.6 %collective-permute-start.6 = (f32[4,144,128]{2,1,0:T(8,128)S(1)}, f32[4,144,128]{2,1,0:T(8,128)S(1)}, u32[]{:S(2)}, u32[]{:S(2)}) collective-permute-start(f32[4,144,128]{2,1,0:T(8,128)S(1)} %collective-permute-done.3.near_a), channel_id=1, source_target_pairs={{0,1},{1,0},{2,3},{3,2},{4,5},{5,4},{6,7},{7,6},{8,9},{9,8},{10,11... | collective-permute-start | bytes 884744 | tf_op jit(solution)/shard_map/ppermute | solution.py:977
  43.5 2.0 %collective-permute-start.7 = (f32[4,144,128]{2,1,0:T(8,128)S(1)}, f32[4,144,128]{2,1,0:T(8,128)S(1)}, u32[]{:S(2)}, u32[]{:S(2)}) collective-permute-start(f32[4,144,128]{2,1,0:T(8,128)S(1)} %collective-permute-done.4.near_b), channel_id=1, source_target_pairs={{0,1},{1,0},{2,3},{3,2},{4,5},{5,4},{6,7},{7,6},{8,9},{9,8},{10,11... | collective-permute-start | bytes 884744 | tf_op jit(solution)/shard_map/ppermute | solution.py:978
  44.0 1.5 %copy-start.13 = (f32[4,144,128]{2,1,0:T(8,128)}, f32[4,144,128]{2,1,0:T(8,128)S(1)}, u32[]{:S(2)}) copy-start(f32[4,144,128]{2,1,0:T(8,128)S(1)} %collective-permute-done.5.other) | copy-start | bytes 884740
  45.1 0.7 copy-start.14
  45.5 0.7 copy-start.15
  46.2 18.6 %copy-start.1 = (f32[4,144,128]{2,1,0:T(8,128)S(1)}, f32[4,144,128]{2,1,0:T(8,128)}, u32[]{:S(2)}) copy-start(f32[4,144,128]{2,1,0:T(8,128)} %copy-done) | copy-start | bytes 884740
  46.2 33.1 %copy-start.12 = (s32[4]{0:T(128)S(1)}, s32[4]{0:T(128)}, u32[]{:S(2)}) copy-start(s32[4]{0:T(128)} %codes.5) | copy-start | bytes 52
  46.2 46.7 %copy-start.10 = (bf16[4,128,128]{2,1,0:T(8,128)(2,1)S(1)}, bf16[4,128,128]{2,1,0:T(8,128)(2,1)}, u32[]{:S(2)}) copy-start(bf16[4,128,128]{2,1,0:T(8,128)(2,1)} %constant.55.clone.y_row) | copy-start | bytes 393220
  49.7 43.2 %copy-start.6 = (f32[4,64,128]{2,1,0:T(8,128)S(1)}, f32[4,64,128]{2,1,0:T(8,128)}, u32[]{:S(2)}) copy-start(f32[4,64,128]{2,1,0:T(8,128)} %get-tuple-element.40.register) | copy-start | bytes 393220
  49.7 43.2 %copy-start.7 = (bf16[2,256,512]{2,1,0:T(8,128)(2,1)S(1)}, bf16[2,256,512]{2,1,0:T(8,128)(2,1)}, u32[]{:S(2)}) copy-start(bf16[2,256,512]{2,1,0:T(8,128)(2,1)} %constant.53.clone.fill) | copy-start | bytes 1572868
  49.7 43.2 %copy-start.8 = (f32[4,144,128]{2,1,0:T(8,128)S(1)}, f32[4,144,128]{2,1,0:T(8,128)}, u32[]{:S(2)}) copy-start(f32[4,144,128]{2,1,0:T(8,128)} %get-tuple-element.33.message) | copy-start | bytes 884740
  49.7 43.2 %copy-start.9 = (bf16[2,128,512]{2,1,0:T(8,128)(2,1)S(1)}, bf16[2,128,512]{2,1,0:T(8,128)(2,1)}, u32[]{:S(2)}) copy-start(bf16[2,128,512]{2,1,0:T(8,128)(2,1)} %constant.54.clone.z_column) | copy-start | bytes 786436
  49.7 43.2 %copy-start.11 = (s32[4]{0:T(128)S(1)}, s32[4]{0:T(128)}, u32[]{:S(2)}) copy-start(s32[4]{0:T(128)} %octants.9) | copy-start | bytes 52
  64.8 2.1 %collective-permute-start.8 = (f32[4,4,40,256]{3,2,1,0:T(8,128)S(1)}, f32[4,4,40,256]{3,2,1,0:T(8,128)S(1)}, u32[]{:S(2)}, u32[]{:S(2)}) collective-permute-start(f32[4,4,40,256]{3,2,1,0:T(8,128)S(1)} %all_to_all.10.mine), channel_id=1, source_target_pairs={{0,1},{1,0},{2,3},{3,2},{4,5},{5,4},{6,7},{7,6},{8,9},{9,8},{10,11... | collective-permute-start | bytes 1966088 | tf_op jit(solution)/shard_map/ppermute | solution.py:1018
  64.8 1.0 copy-start.3
  65.8 1.0 copy-start.5
  67.8 6.6 %collective-permute-start.9 = (f32[4,40,256]{2,1,0:T(8,128)S(1)}, f32[4,40,256]{2,1,0:T(8,128)S(1)}, u32[]{:S(2)}, u32[]{:S(2)}) collective-permute-start(f32[4,40,256]{2,1,0:T(8,128)S(1)} %get-tuple-element.57), channel_id=1, source_target_pairs={{0,2},{1,3},{2,0},{3,1},{4,6},{5,7},{6,4},{7,5},{8,10},{9,11},{10,... | collective-permute-start | bytes 491528 | tf_op jit(solution)/shard_map/ppermute | solution.py:1038
  69.0 10.2 %collective-permute-start.10 = (f32[4,40,256]{2,1,0:T(8,128)S(1)}, f32[4,40,256]{2,1,0:T(8,128)S(1)}, u32[]{:S(2)}, u32[]{:S(2)}) collective-permute-start(f32[4,40,256]{2,1,0:T(8,128)S(1)} %get-tuple-element.59), channel_id=1, source_target_pairs={{2,4},{3,5},{4,2},{5,3},{6,8},{7,9},{8,6},{9,7},{10,12},{11,13},{1... | collective-permute-start | bytes 491528 | tf_op jit(solution)/shard_map/ppermute | solution.py:1039

commit v4 on v3

--- a/solution.py
+++ b/solution.py
@@ -365,7 +365,7 @@
 
 
 def early_kernel(
-    base, again, octants, fine_octants, counts, spread_ref, reaction_smem, box, code, boxes, words,
+    base, count, again, octants, fine_octants, counts, spread_ref, reaction_smem, box, code, boxes, words,
     sel_x_all, sel_yz_all, layers, mean_x, couple, *refs,
 ):
     states, register, edges, ends, average, *refs = refs[5 * again :]
@@ -375,7 +375,9 @@
     coarse = lax.axis_index("lev") == 0
     used = coarse | (at < counts[0])
 
-    def coarse_copies(first=0, last=6):
+    slot = i % 2
+
+    def coarse_copies(at, to, first=0, last=6):
         octant = octants[at]
         previous, following = jnp.maximum(at - 1, 0), jnp.minimum(at + 1, SLOTS - 1)
         pairs = (
@@ -383,11 +385,18 @@
             (boxes.at[following, :, pl.ds(0, 8)], after), (words.at[following, pl.ds(0, 8)], code_after),
             (sel_x_all.at[octant], sel_x), (sel_yz_all.at[octant], sel_yz),
         )
-        return [pltpu.make_async_copy(*pairs[n], sems.at[n]) for n in range(first, last)]
-
-    @pl.when(coarse)
+        return [
+            pltpu.make_async_copy(pairs[n][0], pairs[n][1].at[to], sems.at[to, n]) for n in range(first, last)
+        ]
+
+    @pl.when(coarse & (i == 0))
     def _():
-        for copy in coarse_copies():
+        for copy in coarse_copies(at, slot):
+            copy.start()
+
+    @pl.when(coarse & (i + 1 < count))
+    def _():
+        for copy in coarse_copies(at + 1, 1 - slot):
             copy.start()
 
     @pl.when(jnp.logical_not(used))
@@ -414,13 +423,13 @@
         @pl.when(coarse)
         def _():
             octant = octants[at]
-            for copy in coarse_copies(0, 4):
+            for copy in coarse_copies(at, slot, 0, 4):
                 copy.wait()
             for t in range(8):
-                cells[:, t + 1, 7, :] = before[:, 7, 128 * t : 128 * t + 128]
-                cells[:, t + 1, 40, :] = after[:, 0, 128 * t : 128 * t + 128]
-            f_before = jnp.where(at > 0, code_before[7:8, :].astype(F32) / LEVELS, 0.0)
-            f_after = jnp.where(at < SLOTS - 1, code_after[0:1, :].astype(F32) / LEVELS, 0.0)
+                cells[:, t + 1, 7, :] = before[slot, :, 7, 128 * t : 128 * t + 128]
+                cells[:, t + 1, 40, :] = after[slot, :, 0, 128 * t : 128 * t + 128]
+            f_before = jnp.where(at > 0, code_before[slot, 7:8, :].astype(F32) / LEVELS, 0.0)
+            f_after = jnp.where(at < SLOTS - 1, code_after[slot, 0:1, :].astype(F32) / LEVELS, 0.0)
             prepare(f, f_before, f_after, coef, COARSE_STEP)
             spread = [spread_ref[s] for s in range(8)]
             advance(cells, coef, (now, then), rates, spread, store)
@@ -431,9 +440,9 @@
             c23, c24 = box[0, :, 23, :], box[0, :, 24, :]
             low_flux = -jnp.minimum(f[7:8], f[8:9]) * (ADVECT * c7 - wide * (c8 - c7))
             high_flux = jnp.minimum(f[23:24], f[24:25]) * (ADVECT * c23 - wide * (c24 - c23))
-            for copy in coarse_copies(4, 6):
+            for copy in coarse_copies(at, slot, 4, 6):
                 copy.wait()
-            x_parts = pick(jnp.concatenate([low_flux, high_flux], axis=0), sel_x[...])
+            x_parts = pick(jnp.concatenate([low_flux, high_flux], axis=0), sel_x[slot])
 
             lane = iota((1, 1024), 1)
             y_row = lane // 32 == 16 - y_half
@@ -447,7 +456,7 @@
                 c = box[0, s, 8:24, :]
                 inner = jnp.where(y_row, pltpu.roll(c, y_roll, 1), pltpu.roll(c, z_roll, 1))
                 fluxes.append(spread[s] * weight * (c - inner))
-            side_parts = pick(jnp.concatenate(fluxes, axis=0), sel_yz[...])
+            side_parts = pick(jnp.concatenate(fluxes, axis=0), sel_yz[slot])
             register[0, 0:16, :] = x_parts[:, 0:128]
             register[0, 16:32, :] = x_parts[:, 128:256]
             register[0, 32:64, :] = pack_rows(side_parts)
@@ -919,7 +928,7 @@
 
         blocks = [(8, 32, 1024), (64, 128), (544, 128), (32, 1024), (128, 256)]
         return pl.pallas_call(
-            functools.partial(early_kernel, base, len(carried) > 0),
+            functools.partial(early_kernel, base, boxes, len(carried) > 0),
             grid_spec=pltpu.PrefetchScalarGridSpec(
                 num_scalar_prefetch=3,
                 grid=(boxes,),
@@ -946,13 +955,13 @@
                     pltpu.VMEM((8, 2, 32, 128), F32),
                     pltpu.VMEM((2, 256, 256), BF16),
                     pltpu.VMEM((4, 256, 128), F32),
-                    pltpu.VMEM((8, 8, 1024), F32),
-                    pltpu.VMEM((8, 1024), jnp.int32),
-                    pltpu.VMEM((8, 8, 1024), F32),
-                    pltpu.VMEM((8, 1024), jnp.int32),
-                    pltpu.VMEM((1024, 256), BF16),
-                    pltpu.VMEM((1024, 128), BF16),
-                    pltpu.SemaphoreType.DMA((6,)),
+                    pltpu.VMEM((2, 8, 8, 1024), F32),
+                    pltpu.VMEM((2, 8, 1024), jnp.int32),
+                    pltpu.VMEM((2, 8, 8, 1024), F32),
+                    pltpu.VMEM((2, 8, 1024), jnp.int32),
+                    pltpu.VMEM((2, 1024, 256), BF16),
+                    pltpu.VMEM((2, 1024, 128), BF16),
+                    pltpu.SemaphoreType.DMA((2, 6)),
                 ],
             ),
             out_shape=[shape((SLOTS,) + dims, F32) for dims in blocks],

time: 97.9 us -> 96.8 us (0.989)
  Pallas kernels: 41.1 us -> 38 us
  starting transfers between devices: 14.2 us -> 16.8 us
  blocking collectives: 28.1 us -> 30.7 us
  waiting for transfers between devices: 9.95 us -> 7.56 us
    ppermute x1, starting transfers between devices: 3.16 us -> 6.88 us  [per_device(): from_b = lax.ppermute(to_b, 'box', round_b)]
    pallas_call x2, Pallas kernels: 22.9 us -> 19.8 us  [early(): pl.pallas_call(functools.partial(early_kernel, base, boxes, len(carried)...]
    ppermute x1, waiting for transfers between devices: 2.24 us -> 0.01 us  [per_device(): from_a = lax.ppermute(to_a, 'box', round_a)]
    all_to_all x1, blocking collectives: 15.1 us -> 17.1 us  [per_device(): mine = lax.all_to_all(payload, 'lev', 0, 0)]
    ppermute x1, starting transfers between devices: 1.21 us -> 0.09 us  [per_device(): from_a = lax.ppermute(to_a, 'box', round_a)]
  transfers between devices with their start and end apart: 11 -> 11, of which waited for: 7 -> 6; matrix products, arithmetic and copies ran while one was open for 0% -> 0% of each run, Pallas kernels for 24% -> 21%
where the time goes in v4:
time: 96.8 us
  Pallas kernels  38 us (39%)
  blocking collectives  30.7 us (32%)
  starting transfers between devices  16.8 us (17%)
  waiting for transfers between devices  7.56 us (8%)
  local copies, waits for them, and re-layouts  2.68 us (3%)
  between operations  1.09 us (1%)
    pallas_call x2, Pallas kernels, early(): pl.pallas_call(functools.partial(early_kernel, base, boxes, len(carried)...  19.8 us
    all_to_all x1, blocking collectives, per_device(): mine = lax.all_to_all(payload, 'lev', 0, 0)  17.1 us
    all_to_all x1, blocking collectives, per_device(): parts = lax.all_to_all(quarter, 'lev', 0, 0)  13.6 us
    pallas_call x1, Pallas kernels, per_device(): pl.pallas_call(message_kernel, in_specs=[smem] * 4 + [in_vmem] + [hbm] *...  9.18 us
    ppermute x1, starting transfers between devices, per_device(): from_b = lax.ppermute(to_b, 'box', round_b)  6.88 us
    ppermute x1, starting transfers between devices, per_device(): near_b = lax.ppermute(own, 'box', round_b)  5.18 us
    ppermute x1, waiting for transfers between devices, per_device(): from_b = lax.ppermute(to_b, 'box', round_b)  4.73 us
    pallas_call x1, Pallas kernels, per_device(): pl.pallas_call(finish_kernel, in_specs=[smem] * 2 + [in_vmem] * 6 + [hbm]...  3.99 us
  transfers between devices with their start and end apart: 11, of which 6 were waited for; matrix products, arithmetic and copies ran while one was open for 0% of the time, Pallas kernels for 21%

profile of v4, /device:TPU:6, one launch (start us, length us, event | category | flops | bytes accessed | tf_op | source)
XLA Modules:
  0.0 96.8 jit_solution(5418532900266681532)
XLA Ops:
  0.0 9.2 %shells.1 = (f32[4,144,128]{2,1,0:T(8,128)}, f32[576,128]{1,0:T(8,128)}) custom-call(s32[4]{0:T(128)} %octants.9, s32[4]{0:T(128)} %codes.5, f32[8]{0:T(128)} %spread_ref.7, f32[8,8]{1,0:T(8,128)} %reaction_ref.3, f32[8,8]{1,0:T(8,128)} %reaction_ref.3, f32[4,8,32,1024]{3,2,1,0:T(8,128)} %boxes.5, s32[4,32,1024]{2,1,0:T(8,128)} %words.7, ...), custom_call_target="tpu_custom_call" | custom-call | tf_op jit(solution)/shard_map/shells/pallas_call | solution.py:895
  9.2 1.3 %collective-permute-start.2 = (f32[4,144,128]{2,1,0:T(8,128)}, f32[4,144,128]{2,1,0:T(8,128)S(1)}, u32[]{:S(2)}, u32[]{:S(2)}) collective-permute-start(f32[4,144,128]{2,1,0:T(8,128)} %get-tuple-element.33.message), channel_id=1, source_target_pairs={{0,64},{1,65},{2,66},{3,67},{4,68},{5,69},{6,70},{7,71},{8,72},{9,... | collective-permute-start | bytes 884744 | tf_op jit(solution)/shard_map/ppermute | solution.py:978
  10.5 1.3 %collective-permute-start.1 = (f32[4,144,128]{2,1,0:T(8,128)}, f32[4,144,128]{2,1,0:T(8,128)S(1)}, u32[]{:S(2)}, u32[]{:S(2)}) collective-permute-start(f32[4,144,128]{2,1,0:T(8,128)} %get-tuple-element.33.message), channel_id=1, source_target_pairs={{0,96},{1,97},{2,98},{3,99},{4,100},{5,101},{6,102},{7,103},{8,104... | collective-permute-start | bytes 884744 | tf_op jit(solution)/shard_map/ppermute | solution.py:978
  11.8 1.3 %collective-permute-start = (f32[4,144,128]{2,1,0:T(8,128)}, f32[4,144,128]{2,1,0:T(8,128)S(1)}, u32[]{:S(2)}, u32[]{:S(2)}) collective-permute-start(f32[4,144,128]{2,1,0:T(8,128)} %get-tuple-element.33.message), channel_id=1, source_target_pairs={{0,32},{1,33},{2,34},{3,35},{4,36},{5,37},{6,38},{7,39},{8,40},{9,... | collective-permute-start | bytes 884744 | tf_op jit(solution)/shard_map/ppermute | solution.py:978
  13.8 0.0 copy-start.16
  13.8 12.7 %early_0.1 = (f32[4,8,32,1024]{3,2,1,0:T(8,128)}, f32[4,64,128]{2,1,0:T(8,128)}, f32[4,544,128]{2,1,0:T(8,128)}, f32[4,32,1024]{2,1,0:T(8,128)}, f32[4,128,256]{2,1,0:T(8,128)}) custom-call(s32[4]{0:T(128)} %octants.9, s32[4]{0:T(128)} %octants.8, s32[1]{0:T(128)S(6)} %copy.40.counts, f32[8]{0:T(128)} %spread_ref.7, f32[8,8]{1,0:T(8,128)} %reaction_ref.3, ...), custom_call_target="tpu_custom_call" | custom-call | flops 1000000000 | bytes 30000000 | tf_op jit(solution)/shard_map/early_0/pallas_call | solution.py:930
  26.5 0.0 collective-permute-done.2
  26.5 0.0 collective-permute-done.1
  26.5 0.0 collective-permute-done
  26.5 0.0 copy-done.16
  26.6 0.1 add_select_fusion.own
  26.6 0.0 copy-start
  26.6 5.2 %collective-permute-start.4 = (f32[4,144,128]{2,1,0:T(8,128)S(1)}, f32[4,144,128]{2,1,0:T(8,128)S(1)}, u32[]{:S(2)}, u32[]{:S(2)}) collective-permute-start(f32[4,144,128]{2,1,0:T(8,128)S(1)} %add_select_fusion.own), channel_id=1, source_target_pairs={{2,4},{3,5},{4,2},{5,3},{6,8},{7,9},{8,6},{9,7},{10,12},{11,13},{1... | collective-permute-start | bytes 884744 | tf_op jit(solution)/shard_map/ppermute | solution.py:982
  31.8 0.1 collective-permute-start.3
  31.9 0.1 collective-permute-start.5
  32.0 7.1 %early_3.1 = (f32[4,8,32,1024]{3,2,1,0:T(8,128)}, f32[4,64,128]{2,1,0:T(8,128)}, f32[4,544,128]{2,1,0:T(8,128)}, f32[4,32,1024]{2,1,0:T(8,128)}, f32[4,128,256]{2,1,0:T(8,128)}) custom-call(s32[4]{0:T(128)} %octants.9, s32[4]{0:T(128)} %octants.8, s32[1]{0:T(128)S(6)} %copy.40.counts, ...), custom_call_target="tpu_custom_call", output_to_operand_aliasing={{0}: (14, {}), {1}: (15, {}), {2}: (16, {}), {3}: (17, {}),... | custom-call | flops 1000000000 | bytes 30000000 | tf_op jit(solution)/shard_map/early_3/pallas_call | solution.py:930
  39.2 0.0 copy-done
  39.2 0.2 collective-permute-done.4.near_b
  39.4 1.0 %collective-permute-done.3.near_a = f32[4,144,128]{2,1,0:T(8,128)S(1)} collective-permute-done((f32[4,144,128]{2,1,0:T(8,128)S(1)}, f32[4,144,128]{2,1,0:T(8,128)S(1)}, u32[]{:S(2)}, u32[]{:S(2)}) %collective-permute-start.3) | collective-permute-done | bytes 294944 | tf_op jit(solution)/shard_map/ppermute | solution.py:981
  40.4 0.0 collective-permute-start.6
  40.4 0.5 collective-permute-start.7
  40.9 0.0 collective-permute-done.5.other
  40.9 1.1 %collective-permute-done.6.other_a = f32[4,144,128]{2,1,0:T(8,128)S(1)} collective-permute-done((f32[4,144,128]{2,1,0:T(8,128)S(1)}, f32[4,144,128]{2,1,0:T(8,128)S(1)}, u32[]{:S(2)}, u32[]{:S(2)}) %collective-permute-start.6) | collective-permute-done | bytes 294944 | tf_op jit(solution)/shard_map/ppermute | solution.py:986
  42.0 0.4 collective-permute-done.7.other_b
  42.4 0.0 copy-done.4
  42.4 0.3 copy-done.14
  42.7 0.4 copy-done.15
  43.1 3.5 %interfaces.1 = (f32[4,8,32,1024]{3,2,1,0:T(8,128)}, f32[4,4,40,256]{3,2,1,0:T(8,128)}) custom-call(s32[4]{0:T(128)} %parents.1, s32[4]{0:T(128)} %octants.8, s32[1]{0:T(128)S(6)} %copy.40.counts, f32[8]{0:T(128)} %spread_ref.7, f32[8,8]{1,0:T(8,128)} %reaction_ref.3, f32[8,8]{1,0:T(8,128)} %reaction_ref.3, ...), custom_call_target="tpu_custom_call", output_to_operand_aliasing={{0}: (25, {})} | custom-call | tf_op jit(solution)/shard_map/interfaces/pallas_call | solution.py:992
  46.6 0.0 copy-start.7
  46.6 0.0 copy-start.9
  46.6 0.0 copy-start.11
  46.6 17.1 %all_to_all.10.mine = f32[4,4,40,256]{3,2,1,0:T(8,128)S(1)} all-to-all(f32[4,4,40,256]{3,2,1,0:T(8,128)} %get-tuple-element.52), channel_id=1, replica_groups=mesh['lev'=4,'box'=32] {'lev'}, dimensions={0} | all-to-all | bytes 1310720 | tf_op jit(solution)/shard_map/all_to_all | solution.py:1026
  63.7 0.0 collective-permute-start.8
  63.7 1.0 copy-done.3
  64.7 1.0 copy-done.5
  65.7 0.1 collective-permute-done.8.others
  65.8 0.9 route.1
  66.7 0.1 collective-permute-start.9
  66.8 6.9 %collective-permute-start.10 = (f32[4,40,256]{2,1,0:T(8,128)S(1)}, f32[4,40,256]{2,1,0:T(8,128)S(1)}, u32[]{:S(2)}, u32[]{:S(2)}) collective-permute-start(f32[4,40,256]{2,1,0:T(8,128)S(1)} %get-tuple-element.59), channel_id=1, source_target_pairs={{2,4},{3,5},{4,2},{5,3},{6,8},{7,9},{8,6},{9,7},{10,12},{11,13},{1... | collective-permute-start | bytes 491528 | tf_op jit(solution)/shard_map/ppermute | solution.py:1048
  73.7 0.0 collective-permute-done.9.from_a
  73.7 4.7 %collective-permute-done.10.from_b = f32[4,40,256]{2,1,0:T(8,128)S(1)} collective-permute-done((f32[4,40,256]{2,1,0:T(8,128)S(1)}, f32[4,40,256]{2,1,0:T(8,128)S(1)}, u32[]{:S(2)}, u32[]{:S(2)}) %collective-permute-start.10) | collective-permute-done | bytes 163872 | tf_op jit(solution)/shard_map/ppermute | solution.py:1048
  78.5 0.6 choose.1
  79.1 13.6 %all_to_all.11.parts = f32[4,4,40,256]{3,2,1,0:T(8,128)S(1)} all-to-all(f32[4,4,40,256]{3,2,1,0:T(8,128)S(1)} %choose.1), channel_id=1, replica_groups=mesh['lev'=4,'box'=32] {'lev'}, dimensions={0} | all-to-all | bytes 1310720 | tf_op jit(solution)/shard_map/all_to_all | solution.py:1057
  92.6 0.0 copy-done.7
  92.6 0.0 copy-done.8
  92.6 0.0 copy-done.9
  92.6 0.0 copy-done.11
  92.7 4.0 %finish.1 = f32[4,8,32,1024]{3,2,1,0:T(8,128)} custom-call(s32[4]{0:T(128)S(1)} %copy-done.11, s32[4]{0:T(128)S(1)} %copy-done.12, f32[4,144,128]{2,1,0:T(8,128)S(1)} %copy-done.8, f32[4,64,128]{2,1,0:T(8,128)S(1)} %copy-done.6, f32[4,4,40,256]{3,2,1,0:T(8,128)S(1)} %all_to_all.11.parts, ...), custom_call_target="tpu_custom_call", output_to_operand_aliasing={{}: (8, {})} | custom-call | tf_op jit(solution)/shard_map/finish/pallas_call | solution.py:1059
  (19 shorter events, 0.1 us)
Async XLA Ops:
  9.2 17.3 %collective-permute-start.2 = (f32[4,144,128]{2,1,0:T(8,128)}, f32[4,144,128]{2,1,0:T(8,128)S(1)}, u32[]{:S(2)}, u32[]{:S(2)}) collective-permute-start(f32[4,144,128]{2,1,0:T(8,128)} %get-tuple-element.33.message), channel_id=1, source_target_pairs={{0,64},{1,65},{2,66},{3,67},{4,68},{5,69},{6,70},{7,71},{8,72},{9,... | collective-permute-start | bytes 884744 | tf_op jit(solution)/shard_map/ppermute | solution.py:978
  10.5 16.0 %collective-permute-start.1 = (f32[4,144,128]{2,1,0:T(8,128)}, f32[4,144,128]{2,1,0:T(8,128)S(1)}, u32[]{:S(2)}, u32[]{:S(2)}) collective-permute-start(f32[4,144,128]{2,1,0:T(8,128)} %get-tuple-element.33.message), channel_id=1, source_target_pairs={{0,96},{1,97},{2,98},{3,99},{4,100},{5,101},{6,102},{7,103},{8,104... | collective-permute-start | bytes 884744 | tf_op jit(solution)/shard_map/ppermute | solution.py:978
  11.8 14.7 %collective-permute-start = (f32[4,144,128]{2,1,0:T(8,128)}, f32[4,144,128]{2,1,0:T(8,128)S(1)}, u32[]{:S(2)}, u32[]{:S(2)}) collective-permute-start(f32[4,144,128]{2,1,0:T(8,128)} %get-tuple-element.33.message), channel_id=1, source_target_pairs={{0,32},{1,33},{2,34},{3,35},{4,36},{5,37},{6,38},{7,39},{8,40},{9,... | collective-permute-start | bytes 884744 | tf_op jit(solution)/shard_map/ppermute | solution.py:978
  13.8 12.8 %copy-start.16 = (f32[576,128]{1,0:T(8,128)S(1)}, f32[576,128]{1,0:T(8,128)}, u32[]{:S(2)}) copy-start(f32[576,128]{1,0:T(8,128)} %get-tuple-element.44) | copy-start | bytes 884740
  26.6 12.5 %copy-start = (f32[4,144,128]{2,1,0:T(8,128)}, f32[4,144,128]{2,1,0:T(8,128)S(1)}, u32[]{:S(2)}) copy-start(f32[4,144,128]{2,1,0:T(8,128)S(1)} %add_select_fusion.own) | copy-start | bytes 884740
  26.6 12.8 %collective-permute-start.4 = (f32[4,144,128]{2,1,0:T(8,128)S(1)}, f32[4,144,128]{2,1,0:T(8,128)S(1)}, u32[]{:S(2)}, u32[]{:S(2)}) collective-permute-start(f32[4,144,128]{2,1,0:T(8,128)S(1)} %add_select_fusion.own), channel_id=1, source_target_pairs={{2,4},{3,5},{4,2},{5,3},{6,8},{7,9},{8,6},{9,7},{10,12},{11,13},{1... | collective-permute-start | bytes 884744 | tf_op jit(solution)/shard_map/ppermute | solution.py:982
  31.8 8.5 %collective-permute-start.3 = (f32[4,144,128]{2,1,0:T(8,128)S(1)}, f32[4,144,128]{2,1,0:T(8,128)S(1)}, u32[]{:S(2)}, u32[]{:S(2)}) collective-permute-start(f32[4,144,128]{2,1,0:T(8,128)S(1)} %add_select_fusion.own), channel_id=1, source_target_pairs={{0,2},{1,3},{2,0},{3,1},{4,6},{5,7},{6,4},{7,5},{8,10},{9,11},{10,... | collective-permute-start | bytes 884744 | tf_op jit(solution)/shard_map/ppermute | solution.py:981
  31.9 9.0 %collective-permute-start.5 = (f32[4,144,128]{2,1,0:T(8,128)S(1)}, f32[4,144,128]{2,1,0:T(8,128)S(1)}, u32[]{:S(2)}, u32[]{:S(2)}) collective-permute-start(f32[4,144,128]{2,1,0:T(8,128)S(1)} %add_select_fusion.own), channel_id=1, source_target_pairs={{0,1},{1,0},{2,3},{3,2},{4,5},{5,4},{6,7},{7,6},{8,9},{9,8},{10,11... | collective-permute-start | bytes 884744 | tf_op jit(solution)/shard_map/ppermute | solution.py:985
  39.4 3.0 %copy-start.2 = (f32[4,144,128]{2,1,0:T(8,128)}, f32[4,144,128]{2,1,0:T(8,128)S(1)}, u32[]{:S(2)}) copy-start(f32[4,144,128]{2,1,0:T(8,128)S(1)} %collective-permute-done.4.near_b) | copy-start | bytes 884740
  40.4 2.0 %copy-start.4 = (f32[4,144,128]{2,1,0:T(8,128)}, f32[4,144,128]{2,1,0:T(8,128)S(1)}, u32[]{:S(2)}) copy-start(f32[4,144,128]{2,1,0:T(8,128)S(1)} %collective-permute-done.3.near_a) | copy-start | bytes 884740
  40.4 1.6 %collective-permute-start.6 = (f32[4,144,128]{2,1,0:T(8,128)S(1)}, f32[4,144,128]{2,1,0:T(8,128)S(1)}, u32[]{:S(2)}, u32[]{:S(2)}) collective-permute-start(f32[4,144,128]{2,1,0:T(8,128)S(1)} %collective-permute-done.3.near_a), channel_id=1, source_target_pairs={{0,1},{1,0},{2,3},{3,2},{4,5},{5,4},{6,7},{7,6},{8,9},{9,8},{10,11... | collective-permute-start | bytes 884744 | tf_op jit(solution)/shard_map/ppermute | solution.py:986
  40.4 2.0 %collective-permute-start.7 = (f32[4,144,128]{2,1,0:T(8,128)S(1)}, f32[4,144,128]{2,1,0:T(8,128)S(1)}, u32[]{:S(2)}, u32[]{:S(2)}) collective-permute-start(f32[4,144,128]{2,1,0:T(8,128)S(1)} %collective-permute-done.4.near_b), channel_id=1, source_target_pairs={{0,1},{1,0},{2,3},{3,2},{4,5},{5,4},{6,7},{7,6},{8,9},{9,8},{10,11... | collective-permute-start | bytes 884744 | tf_op jit(solution)/shard_map/ppermute | solution.py:987
  40.9 1.5 %copy-start.13 = (f32[4,144,128]{2,1,0:T(8,128)}, f32[4,144,128]{2,1,0:T(8,128)S(1)}, u32[]{:S(2)}) copy-start(f32[4,144,128]{2,1,0:T(8,128)S(1)} %collective-permute-done.5.other) | copy-start | bytes 884740
  42.0 0.7 copy-start.14
  42.4 0.7 copy-start.15
  43.1 20.6 %copy-start.1 = (f32[4,144,128]{2,1,0:T(8,128)S(1)}, f32[4,144,128]{2,1,0:T(8,128)}, u32[]{:S(2)}) copy-start(f32[4,144,128]{2,1,0:T(8,128)} %copy-done) | copy-start | bytes 884740
  43.1 35.4 %copy-start.12 = (s32[4]{0:T(128)S(1)}, s32[4]{0:T(128)}, u32[]{:S(2)}) copy-start(s32[4]{0:T(128)} %codes.5) | copy-start | bytes 52
  43.1 49.5 %copy-start.10 = (bf16[4,128,128]{2,1,0:T(8,128)(2,1)S(1)}, bf16[4,128,128]{2,1,0:T(8,128)(2,1)}, u32[]{:S(2)}) copy-start(bf16[4,128,128]{2,1,0:T(8,128)(2,1)} %constant.55.clone.y_row) | copy-start | bytes 393220
  46.6 46.0 %copy-start.6 = (f32[4,64,128]{2,1,0:T(8,128)S(1)}, f32[4,64,128]{2,1,0:T(8,128)}, u32[]{:S(2)}) copy-start(f32[4,64,128]{2,1,0:T(8,128)} %get-tuple-element.40.register) | copy-start | bytes 393220
  46.6 46.0 %copy-start.7 = (bf16[2,256,512]{2,1,0:T(8,128)(2,1)S(1)}, bf16[2,256,512]{2,1,0:T(8,128)(2,1)}, u32[]{:S(2)}) copy-start(bf16[2,256,512]{2,1,0:T(8,128)(2,1)} %constant.53.clone.fill) | copy-start | bytes 1572868
  46.6 46.0 %copy-start.8 = (f32[4,144,128]{2,1,0:T(8,128)S(1)}, f32[4,144,128]{2,1,0:T(8,128)}, u32[]{:S(2)}) copy-start(f32[4,144,128]{2,1,0:T(8,128)} %get-tuple-element.33.message) | copy-start | bytes 884740
  46.6 46.0 %copy-start.9 = (bf16[2,128,512]{2,1,0:T(8,128)(2,1)S(1)}, bf16[2,128,512]{2,1,0:T(8,128)(2,1)}, u32[]{:S(2)}) copy-start(bf16[2,128,512]{2,1,0:T(8,128)(2,1)} %constant.54.clone.z_column) | copy-start | bytes 786436
  46.6 46.0 %copy-start.11 = (s32[4]{0:T(128)S(1)}, s32[4]{0:T(128)}, u32[]{:S(2)}) copy-start(s32[4]{0:T(128)} %octants.9) | copy-start | bytes 52
  63.7 2.1 %collective-permute-start.8 = (f32[4,4,40,256]{3,2,1,0:T(8,128)S(1)}, f32[4,4,40,256]{3,2,1,0:T(8,128)S(1)}, u32[]{:S(2)}, u32[]{:S(2)}) collective-permute-start(f32[4,4,40,256]{3,2,1,0:T(8,128)S(1)} %all_to_all.10.mine), channel_id=1, source_target_pairs={{0,1},{1,0},{2,3},{3,2},{4,5},{5,4},{6,7},{7,6},{8,9},{9,8},{10,11... | collective-permute-start | bytes 1966088 | tf_op jit(solution)/shard_map/ppermute | solution.py:1027
  63.7 1.0 copy-start.3
  64.7 1.0 copy-start.5
  66.7 7.0 %collective-permute-start.9 = (f32[4,40,256]{2,1,0:T(8,128)S(1)}, f32[4,40,256]{2,1,0:T(8,128)S(1)}, u32[]{:S(2)}, u32[]{:S(2)}) collective-permute-start(f32[4,40,256]{2,1,0:T(8,128)S(1)} %get-tuple-element.57), channel_id=1, source_target_pairs={{0,2},{1,3},{2,0},{3,1},{4,6},{5,7},{6,4},{7,5},{8,10},{9,11},{10,... | collective-permute-start | bytes 491528 | tf_op jit(solution)/shard_map/ppermute | solution.py:1047
  66.8 11.6 %collective-permute-start.10 = (f32[4,40,256]{2,1,0:T(8,128)S(1)}, f32[4,40,256]{2,1,0:T(8,128)S(1)}, u32[]{:S(2)}, u32[]{:S(2)}) collective-permute-start(f32[4,40,256]{2,1,0:T(8,128)S(1)} %get-tuple-element.59), channel_id=1, source_target_pairs={{2,4},{3,5},{4,2},{5,3},{6,8},{7,9},{8,6},{9,7},{10,12},{11,13},{1... | collective-permute-start | bytes 491528 | tf_op jit(solution)/shard_map/ppermute | solution.py:1048
